TPU v7x, 256 devices: a whole 4x4x8 slice. The times are simulated.
256 devices in a mesh: xy: 32 (over z, x_lo, core), gz: 8 (over x_hi, y).
Axes of the slice: x: 4 (x_hi: 2, x_lo: 2; x = x_hi * 2 + x_lo), y: 4, z: 8, core: 2. Of those that a mesh axis runs over, the one named last changes fastest.
Arguments:
- features: float32 [524288, 128], P(('xy', 'gz')), may hold values from -6 to 6
- positions: float32 [2, 524288], P(None, ('xy', 'gz')), may hold values from 0 to 1
- plane_index: int32 [524288], P(('xy', 'gz')), may hold values from 0 to 2
- plane_frac: float32 [524288], P(('xy', 'gz')), may hold values from 0 to 1
- neighbours: int32 [16, 524288], P(None, ('xy', 'gz')), may hold values from 0 to 3071
- pair_weight: float32 [16, 524288], P(None, ('xy', 'gz')), may hold values from 0.05 to 0.5
- ghost_index: int32 [65536], P(('xy', 'gz')), may hold values from 0 to 2047
- wave_index: int32 [2, 512], replicated, may hold values from -12 to 12, as said below
- channel_filter: float32 [512, 128], replicated, may hold values from -6 to 6
- screening: float32 [32], P('gz'), may hold values from 4 to 96
- w_short: float32 [128, 128], replicated, may hold values from -0.5 to 0.5
Outputs:
- messages: float32 [524288, 128], P(('xy', 'gz'))
Inputs may be any that keep to these rules, and one draw needn't show every extreme that they name: `wave_index`: the wavevector pairs are distinct.
All inputs are finite; a program needn't handle non-finite values.
Results may differ from a plain program's by a relative error of at most 0.0015.
Values may be sent and summed in bfloat16 or wider, within the bound.
No kernel may reach another device: no remote copies, remote signals or barrier semaphores. Data moves between devices by JAX's collectives and lax.ppermute only.
A program may use at most 64 MiB of HBM per device.

v0:
```python
import math

import jax
import jax.numpy as jnp
from jax import lax
from jax.sharding import PartitionSpec as P

two_pi = 2.0 * math.pi
plane_gap = 0.01
long_gain = 0.125


def shifted(value, axis, steps):
    count = lax.axis_size(axis)
    pairs = [(source, (source + steps) % count) for source in range(count)]
    return lax.ppermute(value, axis, pairs)


def from_behind(block, axis, distance):
    devices = range(lax.axis_size(axis))
    route = [(i - distance, i) for i in devices if i - distance in devices]
    return lax.ppermute(block, axis, route)


def carried_in(part, axis, combine, identity, reverse):
    count = lax.axis_size(axis)
    place = lax.axis_index(axis)
    ahead = count - 1 - place if reverse else place
    gathered = jax.tree.map(lambda a: lax.all_gather(a, axis), part)
    state = jax.tree.map(lambda a, e: jnp.zeros_like(a) + jnp.asarray(e, a.dtype), part, identity)

    def one(hop, state):
        source = count - 1 - hop if reverse else hop
        return combine(
            state, jax.tree.map(lambda a: lax.dynamic_index_in_dim(a, source, 0, False), gathered)
        )

    return lax.fori_loop(0, ahead, one, state)


def kernels(wave_index, screening):
    wave_x = wave_index[0].astype(jnp.float32)
    wave_y = wave_index[1].astype(jnp.float32)
    radial = two_pi * two_pi * (wave_x * wave_x + wave_y * wave_y)
    spatial = jnp.sqrt(radial[None, :] + (screening * screening)[:, None])
    return (jnp.exp(-plane_gap * spatial), two_pi / spatial)


def phase_rows(pos_x, pos_y, wave_index):
    wave_x = wave_index[0].astype(jnp.float32)
    wave_y = wave_index[1].astype(jnp.float32)
    phase_angle = two_pi * (pos_x[:, None] * wave_x[None, :] + pos_y[:, None] * wave_y[None, :])
    stacked = jnp.stack([jnp.cos(phase_angle), -jnp.sin(phase_angle)], axis=-1)
    return stacked.reshape(pos_x.shape[0], -1).astype(jnp.bfloat16)


def hat_rows(plane_index, plane_frac, plane_count):
    slot_ids = jnp.arange(plane_count, dtype=jnp.int32)[None, :]
    low_plane = plane_index[:, None]
    frac_col = plane_frac[:, None]
    return jnp.where(slot_ids == low_plane, 1.0 - frac_col, 0.0) + jnp.where(
        slot_ids == low_plane + 1, frac_col, 0.0
    )


def lateral(sent_rows, offset):
    return shifted(sent_rows, "xy", offset)


def vertical(sent_rows, offset):
    return from_behind(sent_rows, "gz", offset)


def combine(earlier_pair, later_pair):
    return (earlier_pair[0] * later_pair[0], later_pair[0] * earlier_pair[1] + later_pair[1])


def carries(layer_scale, up_sum, down_sum):
    identity_pair = (jnp.ones_like(layer_scale), jnp.zeros_like(up_sum))
    up_in = carried_in((layer_scale, up_sum), "gz", combine, identity_pair, False)[1]
    down_in = carried_in((layer_scale, down_sum), "gz", combine, identity_pair, True)[1]
    return (up_in, down_in)


def potential(share_rows, wave_rows, filter_rows, screening):
    kept_waves = share_rows.shape[0] // 2
    planes = screening.shape[0]
    chan_count = filter_rows.shape[1]
    source = share_rows.reshape(kept_waves, 2, planes, chan_count)
    decay_rate, kernel = kernels(wave_rows, screening)
    forward = jnp.zeros((kept_waves, 2, chan_count), jnp.float32)
    up_states = []
    for plane_at in range(planes):
        forward = decay_rate[plane_at][:, None, None] * forward + source[:, :, plane_at]
        up_states.append(forward)
    backward = jnp.zeros((kept_waves, 2, chan_count), jnp.float32)
    down_states = [None] * planes
    for plane_at in reversed(range(planes)):
        backward = decay_rate[plane_at][:, None, None] * backward + source[:, :, plane_at]
        down_states[plane_at] = backward
    layer_scale = jnp.prod(decay_rate, axis=0)[:, None, None]
    up_in, down_in = carries(layer_scale, up_states[-1], down_states[0])
    growth = jnp.ones((kept_waves, 1, 1), jnp.float32)
    up_total = []
    for plane_at in range(planes):
        growth = growth * decay_rate[plane_at][:, None, None]
        up_total.append(up_states[plane_at] + growth * up_in)
    growth = jnp.ones((kept_waves, 1, 1), jnp.float32)
    down_total = [None] * planes
    for plane_at in reversed(range(planes)):
        growth = growth * decay_rate[plane_at][:, None, None]
        down_total[plane_at] = down_states[plane_at] + growth * down_in
    results = []
    for plane_at in range(planes):
        summed = up_total[plane_at] + down_total[plane_at] - source[:, :, plane_at]
        results.append(
            long_gain * kernel[plane_at][:, None, None] * filter_rows[:, None, :] * summed
        )
    return (
        jnp.stack(results, axis=2).reshape(2 * kept_waves, planes * chan_count).astype(jnp.bfloat16)
    )


def on_device(
    features,
    positions,
    plane_index,
    plane_frac,
    neighbours,
    pair_weight,
    ghost_index,
    wave_index,
    channel_filter,
    screening,
    w_short,
):
    atom_count = features.shape[0]
    chan_count = features.shape[1]
    planes = screening.shape[0]
    xy_count = lax.axis_size("xy")
    sent_rows = features[ghost_index]
    side_rows = [
        lateral(sent_rows, 1),
        lateral(sent_rows, -1),
        vertical(sent_rows, 1),
        vertical(sent_rows, -1),
    ]
    lookup_table = jnp.concatenate([features] + side_rows, axis=0)

    def add_pair(running, pair_item):
        index_row, weight_row = pair_item
        return (running + weight_row[:, None] * lookup_table[index_row], None)

    pair_sum = lax.scan(
        add_pair, jnp.zeros((atom_count, chan_count), jnp.float32), (neighbours, pair_weight)
    )[0]
    short_range = jnp.dot(pair_sum, w_short, precision=lax.Precision.HIGHEST)
    phase_table = phase_rows(positions[0], positions[1], wave_index)
    hat_table = hat_rows(plane_index, plane_frac, planes)
    weighted = (
        (hat_table[:, :, None] * features[:, None, :])
        .reshape(atom_count, planes * chan_count)
        .astype(jnp.bfloat16)
    )
    norm_scale = float(atom_count * xy_count) ** (-0.5)
    local_sums = (
        lax.dot_general(
            phase_table, weighted, (((0,), (0,)), ((), ())), preferred_element_type=jnp.float32
        )
        * norm_scale
    )
    whole_sums = lax.psum(local_sums, "xy")
    field_rows = potential(whole_sums, wave_index, channel_filter, screening)
    projected = jnp.dot(phase_table, field_rows, preferred_element_type=jnp.float32)
    long_range = jnp.sum(
        hat_table[:, :, None] * projected.reshape(atom_count, planes, chan_count), axis=1
    )
    return short_range + long_range


def solution(mesh):
    return jax.shard_map(
        on_device,
        mesh=mesh,
        in_specs=(
            P(("xy", "gz"), None),
            P(None, ("xy", "gz")),
            P(("xy", "gz")),
            P(("xy", "gz")),
            P(None, ("xy", "gz")),
            P(None, ("xy", "gz")),
            P(("xy", "gz")),
            P(),
            P(),
            P("gz"),
            P(),
        ),
        out_specs=P(("xy", "gz"), None),
        check_vma=False,
    )
```

profile of v0, /device:TPU:4, one launch (start us, length us, event | category | flops | bytes accessed | tf_op | source)
XLA Modules:
  0.0 550.1 jit_solution(8284004997899195918)
XLA Ops:
  8.1 17.1 %cosine_convert_fusion = (bf16[2048,512,1]{1,0,2:T(8,128)(2,1)S(1)}, bf16[2048,512,1]{1,0,2:T(8,128)(2,1)S(1)}) fusion(f32[512]{0:T(512)S(1)} %bitcast.214, f32[2048]{0:T(1024)S(1)} %bitcast.212, f32[512]{0:T(512)S(1)} %bitcast.213, f32[2048]{0:T(1024)S(1)} %bitcast.211), kind=kLoop, calls=%fused_computation.20 | loop fusion | flops 7340032 | bytes 4214784 | tf_op jit(solution)/shard_map/convert.8
  25.2 2.3 pad_maximum_fusion
  27.5 11.4 %copy.52 = bf16[2048,512,2]{0,2,1:T(2,128)(2,1)} copy(bf16[2048,512,2]{1,0,2:T(8,128)(2,1)} %pad_maximum_fusion) | data formatting | bytes 8388608 | tf_op jit(solution)/shard_map/stack | solution.py:53
  38.9 7.3 %convert_element_type.44 = bf16[2048,1024]{0,1:T(8,128)(2,1)} reshape(bf16[2048,512,2]{0,2,1:T(2,128)(2,1)} %copy.52) | data formatting | bytes 8388608 | tf_op jit(solution)/shard_map/convert_element_type | solution.py:54
  46.2 1.3 multiply_convert_fusion
  47.6 2.7 copy.53
  50.3 6.6 %convolution_multiply_fusion = f32[1024,512]{1,0:T(8,128)} fusion(bf16[2048,1024]{0,1:T(8,128)(2,1)} %convert_element_type.44, bf16[2048,512]{0,1:T(8,128)(2,1)} %bitcast.190), kind=kOutput, calls=%fused_computation.23 | convolution fusion | flops 2148007936 | bytes 8388608 | tf_op jit(solution)/shard_map/dot_general | solution.py:167
  56.9 1.9 reshape.610
  58.9 1.8 copy.54
  62.7 230.6 %all-reduce.2.cloned.1.call-done = f32[512,2,4,128]{3,0,1,2:T(8,128)} async-done(((f32[512,2,4,128]{3,0,1,2:T(8,128)}), f32[512,2,4,128]{3,0,1,2:T(8,128)}) %all-reduce.2.cloned.1.call-update) | async-done | bytes 2097168 | tf_op jit(solution)/shard_map/psum | solution.py:172
  293.3 3.0 bitcast_add_fusion.7
  296.4 1.3 gather_fusion.1
  297.9 4.0 collective-permute-start.1
  301.8 3.4 collective-permute-start.2
  305.2 6.1 %collective-permute-start.3 = (f32[256,128]{1,0:T(8,128)}, f32[256,128]{1,0:T(8,128)S(1)}, u32[]{:S(2)}, u32[]{:S(2)}) collective-permute-start(f32[256,128]{1,0:T(8,128)} %gather_fusion.1), channel_id=1, source_target_pairs={{1,0},{2,1},{3,2},{4,3},{5,4},{6,5},{7,6},{9,8},{10,9},{11,10},{12... | collective-permute-start | bytes 393224 | tf_op jit(solution)/shard_map/ppermute | solution.py:22
  311.3 1.2 broadcast_multiply_fusion.1
  312.6 29.8 %all-gather.1 = f32[8,1,512]{2,1,0:T(1,128)S(1)} all-gather(f32[1,1,512]{2,1,0:T(1,128)} %bitcast.219), channel_id=2, replica_groups=mesh['xy'=32,'gz'=8] {'gz'}, dimensions={0}, use_global_device_ids=true | all-gather | bytes 18432 | tf_op jit(solution)/shard_map/all_gather | solution.py:29
  342.6 154.6 %while.39 = (s32[]{:T(128)}, f32[2048,128]{1,0:T(8,128)}, f32[16,2048]{1,0:T(8,128)}, s32[16,2048]{1,0:T(8,128)}, f32[3072,128]{1,0:T(8,128)S(1)}, /*index=5*/s32[]{:T(128)}, s32[]{:T(128)}) while((s32[]{:T(128)}, f32[2048,128]{1,0:T(8,128)}, f32[16,2048]{1,0:T(8,128)}, s32[16,2048]{1,0:T(8,128)}, f32[3072,128]{1,0:T(8,128)S(1)}, ...), condition=%wide.region_1.2_spmd.clone, body=%wide.region_0.1_spmd.clone.sunk | while | flops 794627 | bytes 5308511 | solution.py:154
  343.4 5.5 gather_fusion
  349.8 1.3 select_add_fusion.3
  352.0 5.5 gather_fusion
  358.3 2.5 select_add_fusion.3
  361.7 5.5 gather_fusion
  368.0 2.5 select_add_fusion.3
  371.4 5.5 gather_fusion
  377.8 2.5 select_add_fusion.3
  381.2 5.5 gather_fusion
  387.5 2.6 select_add_fusion.3
  390.9 5.5 gather_fusion
  397.3 2.5 select_add_fusion.3
  400.7 5.5 gather_fusion
  407.0 2.5 select_add_fusion.3
  410.4 5.5 gather_fusion
  416.8 2.5 select_add_fusion.3
  420.2 5.5 gather_fusion
  426.5 2.5 select_add_fusion.3
  429.9 5.5 gather_fusion
  436.2 2.5 select_add_fusion.3
  439.6 5.5 gather_fusion
  446.0 2.5 select_add_fusion.3
  449.4 5.5 gather_fusion
  455.7 2.5 select_add_fusion.3
  459.1 5.5 gather_fusion
  465.4 2.5 select_add_fusion.3
  468.8 5.5 gather_fusion
  475.2 2.5 select_add_fusion.3
  478.6 5.5 gather_fusion
  484.9 2.5 select_add_fusion.3
  488.3 5.5 gather_fusion
  494.7 2.5 select_add_fusion.3
  497.3 19.1 %while.37 = (s32[]{:T(128)}, f32[512,2,128]{2,1,0:T(2,128)S(1)}, s32[]{:T(128)}, f32[8,512,1,1]{1,3,2,0:T(1,128)S(1)}, f32[8,512,2,128]{3,1,2,0:T(8,128)}, /*index=5*/s32[]{:T(128)}, s32[]{:T(128)}, s32[]{:T(128)}) while((s32[]{:T(128)}, f32[512,2,128]{2,1,0:T(2,128)S(1)}, s32[]{:T(128)}, f32[8,512,1,1]{1,3,2,0:T(1,128)S(1)}, ...), condition=%wide.region_5.6_spmd, body=%wide.region_4.5_spmd.sunk | while | flops 262149 | bytes 2627711 | solution.py:38
  498.6 3.6 fusion.44
  503.4 3.6 fusion.44
  508.1 3.6 fusion.44
  512.9 3.6 fusion.44
  516.7 14.4 %while.38 = (s32[]{:T(128)}, f32[512,2,128]{2,1,0:T(2,128)S(1)}, s32[]{:T(128)}, f32[8,512,1,1]{1,3,2,0:T(1,128)S(1)}, f32[8,512,2,128]{3,1,2,0:T(8,128)}, /*index=5*/s32[]{:T(128)}, s32[]{:T(128)}, s32[]{:T(128)}, s32[]{:T(128)}) while((s32[]{:T(128)}, f32[512,2,128]{2,1,0:T(2,128)S(1)}, s32[]{:T(128)}, f32[8,512,1,1]{1,3,2,0:T(1,128)S(1)}, ...), condition=%wide.region_7.8_spmd, body=%wide.region_6.7_spmd.sunk | while | flops 262150 | bytes 2627731 | solution.py:38
  516.7 1.2 constant_dynamic-slice_fusion.12
  517.9 3.6 fusion.45
  521.6 1.1 constant_dynamic-slice_fusion.12
  522.7 3.6 fusion.45
  527.4 3.6 fusion.45
  531.1 1.4 fusion.29
  535.8 5.9 %multiply_reduce_fusion = f32[2048,128]{1,0:T(8,128)S(1)} fusion(bf16[4,128,1024]{2,1,0:T(8,128)(2,1)S(1)} %bitcast.191, bf16[2048,1024]{0,1:T(8,128)(2,1)} %convert_element_type.44, f32[2048,4]{0,1:T(4,128)S(1)} %select_add_fusion.1), kind=kOutput, calls=%fused_computation.17 | convolution fusion | flops 2149318656 | bytes 6324224 | tf_op jit(solution)/shard_map/dot_general | solution.py:174
  541.6 2.0 convolution_add_fusion
  (129 shorter events, 40.3 us)
Async XLA Ops:
  6.5 535.1 %copy-start = (f32[128,128]{1,0:T(8,128)S(1)}, f32[128,128]{1,0:T(8,128)}, u32[]{:S(2)}) copy-start(f32[128,128]{1,0:T(8,128)} %param.27) | copy-start | bytes 196612
  6.5 286.7 %all-reduce.2.cloned.1.call-start = ((), (), s32[]{:S(2)}) async-start(), calls=%async_computation | async-start | bytes 4194304 | tf_op jit(solution)/shard_map/psum | solution.py:172
  38.9 7.3 %copy-start.8 = (s32[2048]{0:T(1024)S(1)}, s32[2048]{0:T(1024)}, u32[]{:S(2)}) copy-start(s32[2048]{0:T(1024)} %param.19) | copy-start | bytes 24580
  38.9 7.3 %copy-start.7 = (f32[2048]{0:T(1024)S(1)}, f32[2048]{0:T(1024)}, u32[]{:S(2)}) copy-start(f32[2048]{0:T(1024)} %param.20) | copy-start | bytes 24580
  38.9 7.3 %copy-start.3 = (f32[2048,128]{1,0:T(8,128)S(1)}, f32[2048,128]{1,0:T(8,128)}, u32[]{:S(2)}) copy-start(f32[2048,128]{1,0:T(8,128)} %param.17) | copy-start | bytes 3145732
  60.6 0.7 copy-start.14
  60.6 0.7 copy-start.9
  60.7 235.7 %copy-start.13 = (s32[256]{0:T(256)S(1)}, s32[256]{0:T(256)}, u32[]{:S(2)}) copy-start(s32[256]{0:T(256)} %param.23) | copy-start | bytes 3076
  60.7 436.5 %all-gather.5.cloned.1.call-start = ((), (), s32[]{:S(2)}) async-start(), calls=%async_computation.1 | async-start | bytes 4718592 | tf_op jit(solution)/shard_map/all_gather | solution.py:29
  293.3 18.0 %copy-start.6 = (f32[512,128]{1,0:T(8,128)S(1)}, f32[512,128]{1,0:T(8,128)}, u32[]{:S(2)}) copy-start(f32[512,128]{1,0:T(8,128)} %param.25) | copy-start | bytes 786436
  296.3 220.2 %all-gather.7.cloned.1.call-start = ((), (), s32[]{:S(2)}) async-start(), calls=%async_computation.2 | async-start | bytes 4718592 | tf_op jit(solution)/shard_map/all_gather | solution.py:29
  297.8 44.7 %collective-permute-start = (f32[256,128]{1,0:T(8,128)}, f32[256,128]{1,0:T(8,128)S(1)}, u32[]{:S(2)}, u32[]{:S(2)}) collective-permute-start(f32[256,128]{1,0:T(8,128)} %gather_fusion.1), channel_id=1, source_target_pairs={{0,8},{8,16},{16,24},{24,32},{32,40},{40,48},{48,56},{56,64},{64,7... | collective-permute-start | bytes 393224 | tf_op jit(solution)/shard_map/ppermute | solution.py:16
  297.9 44.6 %collective-permute-start.1 = (f32[256,128]{1,0:T(8,128)}, f32[256,128]{1,0:T(8,128)S(1)}, u32[]{:S(2)}, u32[]{:S(2)}) collective-permute-start(f32[256,128]{1,0:T(8,128)} %gather_fusion.1), channel_id=1, source_target_pairs={{0,248},{8,0},{16,8},{24,16},{32,24},{40,32},{48,40},{56,48},{64,5... | collective-permute-start | bytes 393224 | tf_op jit(solution)/shard_map/ppermute | solution.py:16
  301.8 40.6 %collective-permute-start.2 = (f32[256,128]{1,0:T(8,128)}, f32[256,128]{1,0:T(8,128)S(1)}, u32[]{:S(2)}, u32[]{:S(2)}) collective-permute-start(f32[256,128]{1,0:T(8,128)} %gather_fusion.1), channel_id=1, source_target_pairs={{0,1},{1,2},{2,3},{3,4},{4,5},{5,6},{6,7},{8,9},{9,10},{10,11},{11... | collective-permute-start | bytes 393224 | tf_op jit(solution)/shard_map/ppermute | solution.py:22
  305.2 37.3 %collective-permute-start.3 = (f32[256,128]{1,0:T(8,128)}, f32[256,128]{1,0:T(8,128)S(1)}, u32[]{:S(2)}, u32[]{:S(2)}) collective-permute-start(f32[256,128]{1,0:T(8,128)} %gather_fusion.1), channel_id=1, source_target_pairs={{1,0},{2,1},{3,2},{4,3},{5,4},{6,5},{7,6},{9,8},{10,9},{11,10},{12... | collective-permute-start | bytes 393224 | tf_op jit(solution)/shard_map/ppermute | solution.py:22
  516.6 14.4 %copy-start.2 = (f32[512,2,4,128]{3,0,1,2:T(8,128)S(1)}, f32[512,2,4,128]{3,0,1,2:T(8,128)}, u32[]{:S(2)}) copy-start(f32[512,2,4,128]{3,0,1,2:T(8,128)} %all-reduce.2.cloned.1.call-done) | copy-start | bytes 6291460
  531.0 1.5 copy-start.11
  531.0 1.5 copy-start.12
  532.5 1.0 copy-start.4
  532.5 1.0 copy-start.5
  532.5 1.0 copy-start.10
  535.7 5.9 %copy-start.1 = (f32[2048,128]{1,0:T(8,128)S(1)}, f32[2048,128]{1,0:T(8,128)}, u32[]{:S(2)}) copy-start(f32[2048,128]{1,0:T(8,128)} %get-tuple-element.160) | copy-start | bytes 3145732
Sparse Core Ops, SparseCore 0:
  60.8 232.4 all-reduce.1
  296.4 74.9 all-gather.4
  374.4 74.3 all-gather.6
where the time goes:
time: 553 us; the launch traced here: 550 us
  waiting for transfers between devices  231 us (42%)
  local copies, waits for them, and re-layouts  139 us (25%)
  other arithmetic  108 us (20%)
  blocking collectives  29.8 us (5%)
  matrix products  14.4 us (3%)
  starting transfers between devices  13.6 us (2%)
  between operations  13.5 us (2%)
    psum x1, waiting for transfers between devices, on_device(): whole_sums = lax.psum(local_sums, 'xy')  231 us
    gather x16, local copies, waits for them, and re-layouts, add_pair(): return (running + weight_row[:, None] * lookup_table[index_row], None)  87.5 us
    add x16, other arithmetic, add_pair(): return (running + weight_row[:, None] * lookup_table[index_row], None)  39.4 us
    all_gather x1, blocking collectives, carried_in(): gathered = jax.tree.map(lambda a: lax.all_gather(a, axis), part)  29.8 us
    add x7, other arithmetic, combine(): later_pair[0] * earlier_pair[1] + later_pair[1]  25.2 us
    another operation x1, other arithmetic  17.1 us
    dynamic_slice x16, local copies, waits for them, and re-layouts, on_device(): lax.scan(add_pair, jnp.zeros((atom_count, chan_count), jnp.float32), (nei...  13.7 us
    select_n x16, other arithmetic, add_pair(): return (running + weight_row[:, None] * lookup_table[index_row], None)  13.7 us
  transfers between devices with their start and end apart: 7, of which 1 were waited for; matrix products, arithmetic and copies ran while one was open for 32% of the time, Pallas kernels for 0%

commit v1 on v0

v1 whole, which is shorter than its diff:
```python
import math

import jax
import jax.numpy as jnp
from jax import lax
from jax.experimental import pallas as pl
from jax.experimental.pallas import tpu as pltpu
from jax.sharding import Mesh
from jax.sharding import PartitionSpec as P

two_pi = 2.0 * math.pi
plane_gap = 0.01
long_gain = 0.125

ATOMS = 2048
CHAN = 128
PLANES = 4
COLS = PLANES * CHAN
NBR = 16
GHOST = 256
TABLE = ATOMS + 4 * GHOST
LAYERS = 8
XY_DEVICES = 32
CHUNK = 24
CHUNKS = 16
HALF = CHUNKS * CHUNK
USED = 14 * CHUNK
PAYLOAD = 32

SPLIT = ("z", "xl", "core", "xh", "y")
LATERAL = ("z", "xl", "core")
SWAP = ("z", "xl")
VERTICAL = ("xh", "y")

smem = pl.BlockSpec(memory_space=pltpu.SMEM)
vmem = pl.BlockSpec(memory_space=pltpu.VMEM)


def cost(flops, nbytes):
    return pl.CostEstimate(flops=flops, bytes_accessed=nbytes, transcendentals=0)


def params(mebibytes=40):
    return pltpu.CompilerParams(vmem_limit_bytes=mebibytes << 20)


BLOCK = 512


def structure_kernel(meta, pos, low, frac, feat, phase, hat, own, other, weighted):
    tile_row = lax.broadcasted_iota(jnp.int32, (8, BLOCK), 0)
    upper = tile_row >= 4
    role = tile_row & 3
    wave_is_sin_x = (role == 1) | (role == 2)
    wave_is_sin_y = (role & 1) == 1
    orders = lax.broadcasted_iota(jnp.int32, (16, BLOCK), 0).astype(jnp.float32)

    def row(table, at):
        return jnp.broadcast_to(table[at : at + 1, :], (8, BLOCK))

    def block(at, _):
        lanes = pl.ds(pl.multiple_of(at * BLOCK, BLOCK), BLOCK)

        def tables(coordinate):
            turns = orders * coordinate
            turns = turns - jnp.floor(turns + 0.5)
            angle = two_pi * turns
            return jnp.cos(angle), jnp.sin(angle)

        cos_x, sin_x = tables(pos[0:1, lanes])
        cos_y, sin_y = tables(pos[1:2, lanes])
        for half in range(2):
            b_tiles, axis_tiles = [], []
            for tile in range(3):
                n = 6 * half + 1 + 2 * tile
                cos_n = jnp.where(upper, row(cos_y, n + 1), row(cos_y, n))
                sin_n = jnp.where(upper, row(sin_y, n + 1), row(sin_y, n))
                b_tiles.append(jnp.where(wave_is_sin_y, sin_n, cos_n))
                cos_m = jnp.where(upper, row(cos_x, n + 1), row(cos_x, n))
                sin_m = jnp.where(upper, row(sin_x, n + 1), row(sin_x, n))
                axis_tiles.append(
                    jnp.where(
                        role == 0,
                        cos_n,
                        jnp.where(role == 1, cos_m, jnp.where(role == 2, sin_m, sin_n)),
                    )
                )
            for pair in range(6):
                parts = []
                for a in (2 * pair + 1, 2 * pair + 2):
                    a_tile = jnp.where(wave_is_sin_x, row(sin_x, a), row(cos_x, a))
                    parts += [a_tile * b_tile for b_tile in b_tiles]
                rows = half * USED + pair * 2 * CHUNK
                phase[rows : rows + 2 * CHUNK, lanes] = jnp.concatenate(parts, axis=0).astype(
                    jnp.bfloat16
                )
            zero = jnp.zeros((8, BLOCK), jnp.float32)
            first = jnp.where(tile_row == 0, 1.0, 0.0) if half == 0 else zero
            rows = half * USED + 12 * CHUNK
            phase[rows : rows + 2 * CHUNK, lanes] = jnp.concatenate(
                axis_tiles + [first, zero, zero], axis=0
            ).astype(jnp.bfloat16)

        low_plane = low[:, lanes]
        height = frac[:, lanes]
        hat_block = jnp.where(tile_row == low_plane, 1.0 - height, 0.0) + jnp.where(
            tile_row == low_plane + 1, height, 0.0
        )
        hat[:, lanes] = hat_block
        hat_cols = jnp.transpose(hat_block)
        feat_block = feat[lanes, :]
        for plane in range(PLANES):
            weighted[lanes, plane * CHAN : (plane + 1) * CHAN] = (
                hat_cols[:, plane : plane + 1] * feat_block
            ).astype(jnp.bfloat16)
        return 0

    lax.fori_loop(0, ATOMS // BLOCK, block, 0)
    core = meta[0]
    for mine in (False, True):
        start = pl.multiple_of((core if mine else 1 - core) * USED, 16)
        sums = jnp.dot(
            phase[pl.ds(start, USED), :], weighted[...], preferred_element_type=jnp.float32
        )
        rest = jnp.zeros((HALF - USED, COLS), jnp.float32)
        if mine:
            own[0:USED, :] = sums
            own[USED:HALF, :] = rest
        else:
            other[0:USED, :] = sums.astype(jnp.bfloat16)
            other[USED:HALF, :] = rest.astype(jnp.bfloat16)


def local_structure(meta, positions, low, frac, features):
    return pl.pallas_call(
        structure_kernel,
        out_shape=(
            jax.ShapeDtypeStruct((2 * USED, ATOMS), jnp.bfloat16),
            jax.ShapeDtypeStruct((8, ATOMS), jnp.float32),
            jax.ShapeDtypeStruct((HALF, COLS), jnp.float32),
            jax.ShapeDtypeStruct((HALF, COLS), jnp.bfloat16),
        ),
        in_specs=[smem, vmem, vmem, vmem, vmem],
        out_specs=(vmem, vmem, vmem, vmem),
        scratch_shapes=[pltpu.VMEM((ATOMS, COLS), jnp.bfloat16)],
        cost_estimate=cost(1_500_000_000, 8_000_000),
        compiler_params=params(),
        name="local_structure",
    )(meta, positions, low, frac, features)


def wave_square(half, chunk):
    place = lax.broadcasted_iota(jnp.int32, (CHUNK, CHAN), 0)
    n = 6 * half + 1 + (place >> 2)
    n_square = jnp.where(chunk <= 12, n * n, 0)
    a_square = jnp.where(chunk < 12, (chunk + 1) * (chunk + 1), 0)
    return (n_square + a_square).astype(jnp.float32)


def coefficient_kernel(meta, waves, filters, alpha, beta):
    half, chunk = meta[0], meta[1]
    place = lax.broadcasted_iota(jnp.int32, (CHUNK, 512), 0)
    role = place & 3
    n = 6 * half + 1 + (place >> 2)
    along_x = (role == 1) | (role == 2)
    only_zero = jnp.where((place == 0) & (chunk == 13) & (half == 0), 0, -1)
    a = jnp.where(chunk < 12, chunk + 1, jnp.where(chunk == 12, jnp.where(along_x, n, 0), only_zero))
    b = jnp.where(chunk < 12, n, jnp.where(chunk == 12, jnp.where(along_x, 0, n), only_zero))
    kx, ky = waves[0:1, :], waves[1:2, :]
    hit = jnp.where((jnp.abs(kx) == a) & (jnp.abs(ky) == b), 1.0, 0.0)
    product = kx * ky
    sign = jnp.where(product > 0, 1.0, jnp.where(product < 0, -1.0, 0.0))
    signed = hit * sign * jnp.where(role < 2, -1.0, 1.0)
    both = jnp.dot(
        jnp.concatenate([hit, signed], axis=0),
        filters[...],
        preferred_element_type=jnp.float32,
        precision=lax.Precision.HIGHEST,
    )
    alpha[...] = both[0:CHUNK]
    beta[...] = both[CHUNK : 2 * CHUNK]


def coefficients(meta, waves, filters):
    return pl.pallas_call(
        coefficient_kernel,
        out_shape=(jax.ShapeDtypeStruct((CHUNK, CHAN), jnp.float32),) * 2,
        in_specs=[smem, vmem, vmem],
        out_specs=(vmem, vmem),
        cost_estimate=cost(40_000_000, 300_000),
        compiler_params=params(),
        name="coefficients",
    )(meta, waves, filters)


def spatial_wave(square, screen):
    return jnp.sqrt((two_pi * two_pi) * square + screen * screen)


def source_kernel(meta, screening, parts, source, payload):
    total = parts[0].astype(jnp.float32)
    for at in range(1, CHUNKS):
        total = total + parts[at].astype(jnp.float32)
    total = total * float(ATOMS * XY_DEVICES) ** -0.5
    source[...] = total
    square = wave_square(meta[0], meta[1])
    decay = [
        jnp.exp(-plane_gap * spatial_wave(square, screening[plane])) for plane in range(PLANES)
    ]
    planes = [total[:, plane * CHAN : (plane + 1) * CHAN] for plane in range(PLANES)]
    upward = planes[0]
    for plane in range(1, PLANES):
        upward = decay[plane] * upward + planes[plane]
    downward = planes[PLANES - 1]
    for plane in reversed(range(PLANES - 1)):
        downward = decay[plane] * downward + planes[plane]
    layer = meta[2]
    which = lax.broadcasted_iota(jnp.int32, (8, CHAN), 0)
    screens = jnp.zeros((8, CHAN), jnp.float32)
    for plane in range(PLANES):
        screens = jnp.where(which == plane, screening[plane], screens)
    for target in range(LAYERS):
        payload[target, 0:CHUNK, :] = jnp.where(layer < target, upward, downward)
        payload[target, CHUNK:PAYLOAD, :] = screens


def local_source(meta, screening, parts):
    return pl.pallas_call(
        source_kernel,
        out_shape=(
            jax.ShapeDtypeStruct((CHUNK, COLS), jnp.float32),
            jax.ShapeDtypeStruct((LAYERS, PAYLOAD, CHAN), jnp.float32),
        ),
        in_specs=[smem, smem, vmem],
        out_specs=(vmem, vmem),
        cost_estimate=cost(1_000_000, 600_000),
        compiler_params=params(),
        name="local_source",
    )(meta, screening, parts)


def potential_kernel(meta, screening, source, carried, alpha, beta, out):
    square = wave_square(meta[0], meta[1])
    layer = meta[2]
    upward = jnp.zeros((CHUNK, CHAN), jnp.float32)
    downward = jnp.zeros((CHUNK, CHAN), jnp.float32)
    scales = []
    for at in range(LAYERS):
        depth = jnp.zeros((CHUNK, CHAN), jnp.float32)
        for plane in range(PLANES):
            depth = depth + spatial_wave(square, carried[at, CHUNK + plane : CHUNK + plane + 1, :])
        scales.append(jnp.exp(-plane_gap * depth))
    for at in range(LAYERS):
        upward = jnp.where(at < layer, scales[at] * upward + carried[at, 0:CHUNK, :], upward)
    for at in reversed(range(LAYERS)):
        downward = jnp.where(at > layer, scales[at] * downward + carried[at, 0:CHUNK, :], downward)
    spatial = [spatial_wave(square, screening[plane]) for plane in range(PLANES)]
    decay = [jnp.exp(-plane_gap * s) for s in spatial]
    planes = [source[:, plane * CHAN : (plane + 1) * CHAN] for plane in range(PLANES)]
    sums = []
    for plane in range(PLANES):
        upward = decay[plane] * upward + planes[plane]
        sums.append(upward - planes[plane])
    for plane in reversed(range(PLANES)):
        downward = decay[plane] * downward + planes[plane]
        sums[plane] = sums[plane] + downward
    odd = (lax.broadcasted_iota(jnp.int32, (CHUNK, CHAN), 0) & 1) == 1
    results = []
    for plane in range(PLANES):
        field = sums[plane]
        partner = jnp.where(odd, pltpu.roll(field, 1, 0), pltpu.roll(field, CHUNK - 1, 0))
        mixed = alpha[...] * field + beta[...] * partner
        results.append((long_gain * two_pi) / spatial[plane] * mixed)
    full = jnp.concatenate(results, axis=1).astype(jnp.bfloat16)
    for at in range(CHUNKS):
        out[at] = full


def local_potential(meta, screening, source, carried, alpha, beta):
    return pl.pallas_call(
        potential_kernel,
        out_shape=jax.ShapeDtypeStruct((CHUNKS, CHUNK, COLS), jnp.bfloat16),
        in_specs=[smem, smem, vmem, vmem, vmem, vmem],
        out_specs=vmem,
        cost_estimate=cost(1_000_000, 1_000_000),
        compiler_params=params(),
        name="local_potential",
    )(meta, screening, source, carried, alpha, beta)


def ghost_kernel(rows, feat, out):
    def eight(at, _):
        for k in range(8):
            out[at * 8 + k] = feat[rows[at * 8 + k]]
        return 0

    lax.fori_loop(0, GHOST // 8, eight, 0)


def ghost_rows(rows, feat):
    return pl.pallas_call(
        ghost_kernel,
        out_shape=jax.ShapeDtypeStruct((GHOST, 1, CHAN), jnp.float32),
        in_specs=[smem, vmem],
        out_specs=vmem,
        cost_estimate=cost(1_000, 1_000_000),
        compiler_params=params(),
        name="ghost_rows",
    )(rows, feat)


def pair_messages(index, weight, table, w_short, name):
    count = weight.shape[0]

    def kernel(slots, weights, rows, projection, out, sums):
        place = lax.broadcasted_iota(jnp.int32, (8, CHAN), 0)

        def eight(at, _):
            base = pl.multiple_of(at * 8, 8)
            factor = weights[pl.ds(base, 8), :]
            total = jnp.zeros((8, CHAN), jnp.float32)
            for k in range(NBR):
                picked = jnp.broadcast_to(rows[slots[k * count + base]], (8, CHAN))
                for s in range(1, 8):
                    found = jnp.broadcast_to(rows[slots[k * count + base + s]], (8, CHAN))
                    picked = jnp.where(place == s, found, picked)
                total = total + picked * factor[:, k : k + 1]
            sums[pl.ds(base, 8), :] = total
            return 0

        lax.fori_loop(0, count // 8, eight, 0)
        out[...] = jnp.dot(
            sums[...],
            projection[...],
            preferred_element_type=jnp.float32,
            precision=lax.Precision.HIGHEST,
        )

    return pl.pallas_call(
        kernel,
        out_shape=jax.ShapeDtypeStruct((count, CHAN), jnp.float32),
        in_specs=[smem, vmem, vmem, vmem],
        out_specs=vmem,
        scratch_shapes=[pltpu.VMEM((count, CHAN), jnp.float32)],
        cost_estimate=cost(count * 200_000, count * 57_000),
        compiler_params=params(),
        name=name,
    )(index.reshape(-1), weight, table, w_short)


def project_kernel(meta, mine, theirs, phase, hat, short, out):
    core = meta[0]
    dims = (((0,), (0,)), ((), ()))
    near = pl.multiple_of(core * USED, 16)
    far = pl.multiple_of((1 - core) * USED, 16)
    projected = lax.dot_general(
        mine[0:USED, :], phase[pl.ds(near, USED), :], dims, preferred_element_type=jnp.float32
    ) + lax.dot_general(
        theirs[0:USED, :], phase[pl.ds(far, USED), :], dims, preferred_element_type=jnp.float32
    )
    total = hat[0:1, :] * projected[0:CHAN]
    for plane in range(1, PLANES):
        total = total + hat[plane : plane + 1, :] * projected[plane * CHAN : (plane + 1) * CHAN]
    out[...] = jnp.transpose(total) + short[...]


def project(meta, mine, theirs, phase, hat, short):
    return pl.pallas_call(
        project_kernel,
        grid=(ATOMS // BLOCK,),
        out_shape=jax.ShapeDtypeStruct((ATOMS, CHAN), jnp.float32),
        in_specs=[
            smem,
            pl.BlockSpec((HALF, COLS), lambda i: (0, 0)),
            pl.BlockSpec((HALF, COLS), lambda i: (0, 0)),
            pl.BlockSpec((2 * USED, BLOCK), lambda i: (0, i)),
            pl.BlockSpec((8, BLOCK), lambda i: (0, i)),
            pl.BlockSpec((BLOCK, CHAN), lambda i: (i, 0)),
        ],
        out_specs=pl.BlockSpec((BLOCK, CHAN), lambda i: (i, 0)),
        cost_estimate=cost(1_500_000_000, 6_000_000),
        compiler_params=params(),
        name="project",
    )(meta, mine, theirs, phase, hat, short)


PIECES = (512, 640, 896)


def shifted(value, axis, steps):
    count = lax.axis_size(axis)
    return lax.ppermute(value, axis, [(s, (s + steps) % count) for s in range(count)])


def stepped(value, axis, steps):
    devices = range(lax.axis_size(axis))
    return lax.ppermute(value, axis, [(i - steps, i) for i in devices if i - steps in devices])


def other_core(value):
    return lax.ppermute(value, "core", [(0, 1), (1, 0)])


def on_device(
    features,
    positions,
    plane_index,
    plane_frac,
    neighbours,
    pair_weight,
    ghost_index,
    wave_index,
    channel_filter,
    screening,
    w_short,
):
    tie = lax.optimization_barrier
    meta = jnp.stack(
        [lax.axis_index("core"), lax.axis_index(SWAP), lax.axis_index(VERTICAL)]
    ).astype(jnp.int32)
    phase, hat, own, other = local_structure(
        meta, positions, plane_index.reshape(1, -1), plane_frac.reshape(1, -1), features
    )
    joined = (own + other_core(other).astype(jnp.float32)).astype(jnp.bfloat16)
    joined = joined.reshape(CHUNKS, CHUNK, COLS)
    joined, ghost_index, weights = tie((joined, ghost_index, pair_weight))
    parts = lax.all_to_all(joined, SWAP, 0, 0)

    sent = ghost_rows(ghost_index, features.reshape(ATOMS, 1, CHAN)).reshape(GHOST, CHAN)
    sides = [
        shifted(sent, LATERAL, 1),
        shifted(sent, LATERAL, -1),
        stepped(sent, VERTICAL, 1),
        stepped(sent, VERTICAL, -1),
    ]
    table = jnp.concatenate([features] + sides, axis=0).reshape(TABLE, 1, CHAN)
    alpha, beta = coefficients(meta, wave_index, channel_filter)
    weights = weights.T
    first, second = PIECES[0], PIECES[0] + PIECES[1]
    short_a = pair_messages(neighbours[:, :first], weights[:first], table, w_short, "pair_a")

    parts, short_a, alpha, beta = tie((parts, short_a, alpha, beta))
    source, payload = local_source(meta, screening, parts)
    payload, slots_b = tie((payload, neighbours[:, first:second]))
    carried = lax.all_to_all(payload, VERTICAL, 0, 0)
    short_b = pair_messages(slots_b, weights[first:second], table, w_short, "pair_b")

    carried, short_b = tie((carried, short_b))
    field = local_potential(meta, screening, source, carried, alpha, beta)
    field, slots_c = tie((field, neighbours[:, second:]))
    mine = lax.all_to_all(field, SWAP, 0, 0)
    short_c = pair_messages(slots_c, weights[second:], table, w_short, "pair_c")

    mine, short_c = tie((mine, short_c))
    mine = mine.reshape(HALF, COLS)
    theirs = other_core(mine)
    short = jnp.concatenate([short_a, short_b, short_c], axis=0)
    return project(meta, mine, theirs, phase, hat, short)


def solution(mesh):
    split = Mesh(mesh.devices.reshape(8, 2, 2, 2, 4), SPLIT)
    return jax.shard_map(
        on_device,
        mesh=split,
        in_specs=(
            P(SPLIT, None),
            P(None, SPLIT),
            P(SPLIT),
            P(SPLIT),
            P(None, SPLIT),
            P(None, SPLIT),
            P(SPLIT),
            P(),
            P(),
            P(VERTICAL),
            P(),
        ),
        out_specs=P(SPLIT, None),
        check_vma=False,
    )
```

time: 553 us -> 107 us (0.19)
  waiting for transfers between devices: 231 us -> 3.88 us
  local copies, waits for them, and re-layouts: 139 us -> 12.6 us
  other arithmetic: 108 us -> 1.03 us
  Pallas kernels: 0 us -> 49.6 us
  blocking collectives: 29.8 us -> 0 us
  starting transfers between devices: 13.6 us -> 37.5 us
  matrix products: 14.4 us -> 0 us
  between operations: 13.5 us -> 0.37 us
    psum x1 -> x0, waiting for transfers between devices: 231 us -> none  [on_device(): whole_sums = lax.psum(local_sums, 'xy')]
    gather x17 -> x0, local copies, waits for them, and re-layouts: 88.8 us -> none  [the longest x16 87.5 us: add_pair(): return (running + weight_row[:, None] * lookup_table[index_row], None)]
    add x26 -> x0, other arithmetic: 67.7 us -> none  [the longest x16 39.4 us: add_pair(): return (running + weight_row[:, None] * lookup_table[index_row], None)]
    pallas_call x0 -> x9, Pallas kernels: none -> 49.6 us  [the longest x3 34.5 us: pair_messages(): pl.pallas_call(kernel, out_shape=jax.ShapeDtypeStruct((count, CHAN), jnp....]
    all_gather x1 -> x0, blocking collectives: 29.8 us -> none  [carried_in(): gathered = jax.tree.map(lambda a: lax.all_gather(a, axis), part)]
    all_to_all x0 -> x3, starting transfers between devices: none -> 24 us  [the longest x1 9.33 us: on_device(): parts = lax.all_to_all(joined, SWAP, 0, 0)]
    another operation x6 -> x1, other arithmetic: 21.8 us -> 0.08 us  [on_device(): jnp.stack([lax.axis_index('core'), lax.axis_index(SWAP), lax.axis_index(V...]
    dynamic_slice x30 -> x0, local copies, waits for them, and re-layouts: 21.5 us -> none  [the longest x16 13.7 us: on_device(): lax.scan(add_pair, jnp.zeros((atom_count, chan_count), jnp.float32), (nei...]
  transfers between devices with their start and end apart: 7 -> 9, of which waited for: 1 -> 3; matrix products, arithmetic and copies ran while one was open for 32% -> 5% of each run, Pallas kernels for 0% -> 34%
where the time goes in v1:
time: 107 us; the launch traced here: 105 us
  Pallas kernels  49.6 us (46%)
  starting transfers between devices  37.5 us (35%)
  local copies, waits for them, and re-layouts  12.6 us (12%)
  waiting for transfers between devices  3.88 us (4%)
    pallas_call x3, Pallas kernels, pair_messages(): pl.pallas_call(kernel, out_shape=jax.ShapeDtypeStruct((count, CHAN), jnp....  34.5 us
    ppermute x2, starting transfers between devices, stepped(): lax.ppermute(value, axis, [(i - steps, i) for i in devices if i - steps i...  9.46 us
    all_to_all x1, starting transfers between devices, on_device(): parts = lax.all_to_all(joined, SWAP, 0, 0)  9.33 us
    unnamed x40, local copies, waits for them, and re-layouts  7.6 us
    all_to_all x1, starting transfers between devices, on_device(): carried = lax.all_to_all(payload, VERTICAL, 0, 0)  7.5 us
    all_to_all x1, starting transfers between devices, on_device(): mine = lax.all_to_all(field, SWAP, 0, 0)  7.21 us
    pallas_call x1, Pallas kernels, local_structure(): pl.pallas_call(structure_kernel, out_shape=(jax.ShapeDtypeStruct((2 * USE...  5.72 us
    pallas_call x1, Pallas kernels, project(): pl.pallas_call(project_kernel, grid=(ATOMS // BLOCK,), out_shape=jax.Shap...  4.86 us
  transfers between devices with their start and end apart: 9, of which 3 were waited for; matrix products, arithmetic and copies ran while one was open for 5% of the time, Pallas kernels for 34%

profile of v1, /device:TPU:4, one launch (start us, length us, event | category | flops | bytes accessed | tf_op | source)
XLA Modules:
  0.0 105.0 jit_solution(16749001277894442585)
XLA Ops:
  0.0 0.1 pad_add_fusion.meta
  0.1 1.2 %copy-done = f32[2048,128]{1,0:T(8,128)S(1)} copy-done((f32[2048,128]{1,0:T(8,128)S(1)}, f32[2048,128]{1,0:T(8,128)}, u32[]{:S(2)}) %copy-start) | copy-done | bytes 1048600
  1.3 0.7 copy-done.12
  2.0 0.7 copy-done.13
  2.7 0.7 copy-done.14
  3.4 5.7 %local_structure.1 = (bf16[672,2048]{1,0:T(8,128)(2,1)S(1)}, f32[8,2048]{1,0:T(8,128)S(1)}, f32[384,512]{1,0:T(8,128)S(1)}, bf16[384,512]{1,0:T(8,128)(2,1)S(1)}) custom-call(s32[3]{0:T(128)S(1)} %pad_add_fusion.meta, f32[2,2048]{1,0:T(2,128)S(1)} %copy-done.12, s32[1,2048]{1,0:T(1,128)S(1)} %bitcast.25, f32[1,2048]{1,0:T(1,128)S(1)} %bitcast.26, ...), custom_call_target="tpu_custom_call" | custom-call | flops 1500000000 | bytes 8000000 | tf_op jit(solution)/shard_map/local_structure/pallas_call | solution.py:135
  9.1 0.0 copy-start.2
  9.2 1.5 %copy-done.2 = bf16[672,2048]{1,0:T(8,128)(2,1)} copy-done((bf16[672,2048]{1,0:T(8,128)(2,1)}, bf16[672,2048]{1,0:T(8,128)(2,1)S(1)}, u32[]{:S(2)}) %copy-start.2) | copy-done | bytes 2752536
  10.7 0.0 collective-permute-start
  10.7 1.7 %collective-permute-done = bf16[384,512]{1,0:T(8,128)(2,1)S(1)} collective-permute-done((bf16[384,512]{1,0:T(8,128)(2,1)S(1)}, bf16[384,512]{1,0:T(8,128)(2,1)S(1)}, u32[]{:S(2)}, u32[]{:S(2)}) %collective-permute-start) | collective-permute-done | bytes 393248 | tf_op jit(solution)/shard_map/ppermute | solution.py:401
  12.4 0.9 add_convert_fusion
  13.3 0.0 copy-done.7
  13.3 9.3 %all-to-all-start = ((bf16[16,24,512]{2,1,0:T(8,128)(2,1)}), bf16[16,24,512]{2,1,0:T(8,128)(2,1)S(1)}, u32[]{:S(2)}, u32[]{:S(2)}) async-start(bf16[16,24,512]{2,1,0:T(8,128)(2,1)} %bitcast.5), calls=%async_computation | async-start | bytes 786432 | tf_op jit(solution)/shard_map/all_to_all | solution.py:427
  22.6 0.0 copy-done.1
  22.6 0.0 copy-start.15
  22.6 0.0 copy-start.5
  22.7 0.0 copy-start.9
  22.7 0.0 copy-start.16
  22.7 0.1 constant_dynamic-update-slice_fusion.4
  22.8 0.0 copy-done.11
  22.8 0.9 ghost_rows.1
  23.6 0.1 collective-permute-start.1
  23.7 3.8 %collective-permute-start.2 = (f32[256,128]{1,0:T(8,128)S(1)}, f32[256,128]{1,0:T(8,128)S(1)}, u32[]{:S(2)}, u32[]{:S(2)}) collective-permute-start(f32[256,128]{1,0:T(8,128)S(1)} %bitcast.22), channel_id=1, source_target_pairs={{0,248},{8,0},{16,8},{24,16},{32,24},{40,32},{48,40},{56,48},{64,5... | collective-permute-start | bytes 393224 | tf_op jit(solution)/shard_map/ppermute | solution.py:392
  27.6 0.0 copy-done.15
  27.6 0.0 copy-done.5
  27.6 0.0 copy-done.9
  27.6 0.8 coefficients.1
  28.4 3.5 %collective-permute-start.3 = (f32[256,128]{1,0:T(8,128)S(1)}, f32[256,128]{1,0:T(8,128)S(1)}, u32[]{:S(2)}, u32[]{:S(2)}) collective-permute-start(f32[256,128]{1,0:T(8,128)S(1)} %bitcast.23), channel_id=1, source_target_pairs={{0,1},{1,2},{2,3},{3,4},{4,5},{5,6},{6,7},{8,9},{9,10},{10,11},{11... | collective-permute-start | bytes 393224 | tf_op jit(solution)/shard_map/ppermute | solution.py:397
  31.9 6.0 %collective-permute-start.4 = (f32[256,128]{1,0:T(8,128)S(1)}, f32[256,128]{1,0:T(8,128)S(1)}, u32[]{:S(2)}, u32[]{:S(2)}) collective-permute-start(f32[256,128]{1,0:T(8,128)S(1)} %bitcast.24), channel_id=1, source_target_pairs={{1,0},{2,1},{3,2},{4,3},{5,4},{6,5},{7,6},{9,8},{10,9},{11,10},{12... | collective-permute-start | bytes 393224 | tf_op jit(solution)/shard_map/ppermute | solution.py:397
  37.9 0.0 copy-done.16
  37.9 1.3 %copy.12 = f32[16,2048]{0,1:T(8,128)} copy(f32[16,2048]{1,0:T(8,128)S(1)} %copy-done.16) | data formatting | bytes 262144 | tf_op jit(solution)/shard_map/optimization_barrier | solution.py:426
  39.2 1.0 slice.24.weights
  40.2 0.0 copy-start.10
  40.2 0.0 collective-permute-done.1
  40.2 0.0 collective-permute-done.2
  40.3 0.5 collective-permute-done.3
  40.8 0.0 collective-permute-done.4
  40.8 0.0 copy-done.4
  40.8 0.0 slice-start
  40.9 8.8 %pair_a.1 = f32[512,128]{1,0:T(8,128)S(1)} custom-call(s32[8192]{0:T(1024)S(1)} %bitcast.20, f32[512,16]{1,0:T(8,128)S(1)} %slice.24.weights, f32[3072,1,128]{2,1,0:T(1,128)S(1)} %bitcast.14, f32[128,128]{1,0:T(8,128)S(1)} %copy-done.4), custom_call_target="tpu_custom_call" | custom-call | flops 102400000 | bytes 29184000 | tf_op jit(solution)/shard_map/pair_a/pallas_call | solution.py:339
  49.7 0.0 all-to-all-done.parts
  49.7 0.0 copy-done.10
  49.7 1.3 %local_source.1 = (f32[24,512]{1,0:T(8,128)S(1)}, f32[8,32,128]{2,1,0:T(8,128)}) custom-call(s32[3]{0:T(128)S(1)} %pad_add_fusion.meta, f32[4]{0:T(128)S(1)} %copy-done.10, bf16[16,24,512]{2,1,0:T(8,128)(2,1)S(1)} %all-to-all-done.parts), custom_call_target="tpu_custom_call" | custom-call | flops 1000000 | bytes 600000 | tf_op jit(solution)/shard_map/local_source/pallas_call | solution.py:228
  51.0 7.5 %all-to-all-start.1 = ((f32[8,32,128]{2,1,0:T(8,128)}), f32[8,32,128]{2,1,0:T(8,128)S(1)}, u32[]{:S(2)}, u32[]{:S(2)}) async-start(f32[8,32,128]{2,1,0:T(8,128)} %get-tuple-element.38), calls=%async_computation.1 | async-start | bytes 262144 | tf_op jit(solution)/shard_map/all_to_all | solution.py:445
  58.5 1.0 slice.25.weights
  59.5 0.0 slice-done
  59.5 10.8 %pair_b.1 = f32[640,128]{1,0:T(8,128)S(1)} custom-call(s32[10240]{0:T(1024)S(1)} %reshape.37.slots, f32[640,16]{1,0:T(8,128)S(1)} %slice.25.weights, f32[3072,1,128]{2,1,0:T(1,128)S(1)} %bitcast.15, f32[128,128]{1,0:T(8,128)S(1)} %copy-done.4), custom_call_target="tpu_custom_call" | custom-call | flops 128000000 | bytes 36480000 | tf_op jit(solution)/shard_map/pair_b/pallas_call | solution.py:339
  70.3 0.0 slice-start.1
  70.4 0.0 all-to-all-done.1.carried
  70.4 1.5 %local_potential.1 = bf16[16,24,512]{2,1,0:T(8,128)(2,1)} custom-call(s32[3]{0:T(128)S(1)} %pad_add_fusion.meta, f32[4]{0:T(128)S(1)} %copy-done.10, f32[24,512]{1,0:T(8,128)S(1)} %get-tuple-element.36.source, f32[8,32,128]{2,1,0:T(8,128)S(1)} %all-to-all-done.1.carried, f32[24,128]{1,0:T(8,128)S(1)} %get-tuple-element.41.alpha, ...), custom_call_target="tpu_custom_call" | custom-call | flops 1000000 | bytes 1000000 | tf_op jit(solution)/shard_map/local_potential/pallas_call | solution.py:280
  71.9 7.2 %all-to-all-start.2 = ((bf16[16,24,512]{2,1,0:T(8,128)(2,1)}), bf16[16,24,512]{2,1,0:T(8,128)(2,1)S(1)}, u32[]{:S(2)}, u32[]{:S(2)}) async-start(bf16[16,24,512]{2,1,0:T(8,128)(2,1)} %local_potential.1), calls=%async_computation.2 | async-start | bytes 786432 | tf_op jit(solution)/shard_map/all_to_all | solution.py:451
  79.1 1.1 %slice.26.weights = f32[896,16]{1,0:T(8,128)S(1)} slice(f32[2048,16]{1,0:T(8,128)} %bitcast.29), slice={[1152:2048], [0:16]} | slice | bytes 114688 | tf_op jit(solution)/shard_map/slice | solution.py:452
  80.2 0.0 slice-done.1
  80.2 0.6 reshape.38.slots
  80.8 0.8 copy-done.6
  81.6 14.9 %pair_c.1 = f32[896,128]{1,0:T(8,128)S(1)} custom-call(s32[14336]{0:T(1024)S(1)} %copy-done.6, f32[896,16]{1,0:T(8,128)S(1)} %slice.26.weights, f32[3072,1,128]{2,1,0:T(1,128)S(1)} %bitcast.16, f32[128,128]{1,0:T(8,128)S(1)} %copy-done.4), custom_call_target="tpu_custom_call" | custom-call | flops 179200000 | bytes 51072000 | tf_op jit(solution)/shard_map/pair_c/pallas_call | solution.py:339
  96.5 0.0 copy-start.8
  96.5 0.0 all-to-all-done.2
  96.5 0.1 collective-permute-start.5
  96.6 0.1 pad_maximum_fusion.short
  96.7 1.6 %collective-permute-done.5.theirs = bf16[384,512]{1,0:T(8,128)(2,1)S(1)} collective-permute-done((bf16[384,512]{1,0:T(8,128)(2,1)S(1)}, bf16[384,512]{1,0:T(8,128)(2,1)S(1)}, u32[]{:S(2)}, u32[]{:S(2)}) %collective-permute-start.5) | collective-permute-done | bytes 393248 | tf_op jit(solution)/shard_map/ppermute | solution.py:401
  98.3 0.0 copy-done.8
  98.4 1.8 %copy-done.3 = bf16[672,2048]{1,0:T(8,128)(2,1)S(1)} copy-done((bf16[672,2048]{1,0:T(8,128)(2,1)S(1)}, bf16[672,2048]{1,0:T(8,128)(2,1)}, u32[]{:S(2)}) %copy-start.3) | copy-done | bytes 2752536
  100.1 4.9 %project.1 = f32[2048,128]{1,0:T(8,128)} custom-call(s32[3]{0:T(128)S(1)} %pad_add_fusion.meta, bf16[384,512]{1,0:T(8,128)(2,1)S(1)} %bitcast.19, bf16[384,512]{1,0:T(8,128)(2,1)S(1)} %collective-permute-done.5.theirs, bf16[672,2048]{1,0:T(8,128)(2,1)S(1)} %copy-done.3, f32[8,2048]{1,0:T(8,128)S(1)} %copy-done.8, f32[2048,128]{1,0:T(8,128)S(1)} %pad_maximum_fusion.short), custom_call_target="tpu_custom_call" | custom-call | flops 1500000000 | bytes 6000000 | tf_op jit(solution)/shard_map/project/pallas_call | solution.py:368
  (17 shorter events, 0.1 us)
Async XLA Ops:
  0.1 1.2 %copy-start = (f32[2048,128]{1,0:T(8,128)S(1)}, f32[2048,128]{1,0:T(8,128)}, u32[]{:S(2)}) copy-start(f32[2048,128]{1,0:T(8,128)} %feat.1) | copy-start | bytes 3145732
  1.3 0.7 copy-start.12
  2.0 0.7 copy-start.13
  2.7 0.7 copy-start.14
  9.1 1.5 %copy-start.2 = (bf16[672,2048]{1,0:T(8,128)(2,1)}, bf16[672,2048]{1,0:T(8,128)(2,1)S(1)}, u32[]{:S(2)}) copy-start(bf16[672,2048]{1,0:T(8,128)(2,1)S(1)} %get-tuple-element.46.phase) | copy-start | bytes 8257540
  10.7 2.6 %copy-start.7 = (f32[8,2048]{1,0:T(8,128)}, f32[8,2048]{1,0:T(8,128)S(1)}, u32[]{:S(2)}) copy-start(f32[8,2048]{1,0:T(8,128)S(1)} %get-tuple-element.47.hat) | copy-start | bytes 196612
  10.7 12.0 %copy-start.1 = (f32[2048,128]{1,0:T(8,128)S(1)}, f32[2048,128]{1,0:T(8,128)}, u32[]{:S(2)}) copy-start(f32[2048,128]{1,0:T(8,128)} %feat.1) | copy-start | bytes 3145732
  10.7 1.7 %collective-permute-start = (bf16[384,512]{1,0:T(8,128)(2,1)S(1)}, bf16[384,512]{1,0:T(8,128)(2,1)S(1)}, u32[]{:S(2)}, u32[]{:S(2)}) collective-permute-start(bf16[384,512]{1,0:T(8,128)(2,1)S(1)} %get-tuple-element.29), channel_id=1, source_target_pairs={{0,8},{8,0},{1,9},{9,1},{2,10},{10,2},{3,11},{11,3},{4,12},{12,4},... | collective-permute-start | bytes 1179656 | tf_op jit(solution)/shard_map/ppermute | solution.py:401
  13.3 9.5 %copy-start.11 = (s32[256]{0:T(256)S(1)}, s32[256]{0:T(256)}, u32[]{:S(2)}) copy-start(s32[256]{0:T(256)} %rows) | copy-start | bytes 3076
  13.3 36.4 %all-to-all-start = ((bf16[16,24,512]{2,1,0:T(8,128)(2,1)}), bf16[16,24,512]{2,1,0:T(8,128)(2,1)S(1)}, u32[]{:S(2)}, u32[]{:S(2)}) async-start(bf16[16,24,512]{2,1,0:T(8,128)(2,1)} %bitcast.5), calls=%async_computation | async-start | bytes 786432 | tf_op jit(solution)/shard_map/all_to_all | solution.py:427
  22.6 5.0 %copy-start.15 = (s32[16,2048]{1,0:T(8,128)S(1)}, s32[16,2048]{1,0:T(8,128)}, u32[]{:S(2)}) copy-start(s32[16,2048]{1,0:T(8,128)} %param.15) | copy-start | bytes 393220
  22.6 5.0 %copy-start.5 = (f32[512,128]{1,0:T(8,128)S(1)}, f32[512,128]{1,0:T(8,128)}, u32[]{:S(2)}) copy-start(f32[512,128]{1,0:T(8,128)} %filters.1) | copy-start | bytes 786436
  22.7 5.0 %copy-start.9 = (s32[2,512]{1,0:T(2,128)S(1)}, s32[2,512]{1,0:T(2,128)}, u32[]{:S(2)}) copy-start(s32[2,512]{1,0:T(2,128)} %waves.1) | copy-start | bytes 12292
  22.7 15.2 %copy-start.16 = (f32[16,2048]{1,0:T(8,128)S(1)}, f32[16,2048]{1,0:T(8,128)}, u32[]{:S(2)}) copy-start(f32[16,2048]{1,0:T(8,128)} %param.16) | copy-start | bytes 393220
  23.6 16.6 %collective-permute-start.1 = (f32[256,128]{1,0:T(8,128)S(1)}, f32[256,128]{1,0:T(8,128)S(1)}, u32[]{:S(2)}, u32[]{:S(2)}) collective-permute-start(f32[256,128]{1,0:T(8,128)S(1)} %bitcast.21), channel_id=1, source_target_pairs={{0,8},{8,16},{16,24},{24,32},{32,40},{40,48},{48,56},{56,64},{64,7... | collective-permute-start | bytes 393224 | tf_op jit(solution)/shard_map/ppermute | solution.py:392
  23.7 16.5 %collective-permute-start.2 = (f32[256,128]{1,0:T(8,128)S(1)}, f32[256,128]{1,0:T(8,128)S(1)}, u32[]{:S(2)}, u32[]{:S(2)}) collective-permute-start(f32[256,128]{1,0:T(8,128)S(1)} %bitcast.22), channel_id=1, source_target_pairs={{0,248},{8,0},{16,8},{24,16},{32,24},{40,32},{48,40},{56,48},{64,5... | collective-permute-start | bytes 393224 | tf_op jit(solution)/shard_map/ppermute | solution.py:392
  27.6 13.2 %copy-start.4 = (f32[128,128]{1,0:T(8,128)S(1)}, f32[128,128]{1,0:T(8,128)}, u32[]{:S(2)}) copy-start(f32[128,128]{1,0:T(8,128)} %projection.5) | copy-start | bytes 196612
  28.4 12.3 %collective-permute-start.3 = (f32[256,128]{1,0:T(8,128)S(1)}, f32[256,128]{1,0:T(8,128)S(1)}, u32[]{:S(2)}, u32[]{:S(2)}) collective-permute-start(f32[256,128]{1,0:T(8,128)S(1)} %bitcast.23), channel_id=1, source_target_pairs={{0,1},{1,2},{2,3},{3,4},{4,5},{5,6},{6,7},{8,9},{9,10},{10,11},{11... | collective-permute-start | bytes 393224 | tf_op jit(solution)/shard_map/ppermute | solution.py:397
  31.9 8.9 %collective-permute-start.4 = (f32[256,128]{1,0:T(8,128)S(1)}, f32[256,128]{1,0:T(8,128)S(1)}, u32[]{:S(2)}, u32[]{:S(2)}) collective-permute-start(f32[256,128]{1,0:T(8,128)S(1)} %bitcast.24), channel_id=1, source_target_pairs={{1,0},{2,1},{3,2},{4,3},{5,4},{6,5},{7,6},{9,8},{10,9},{11,10},{12... | collective-permute-start | bytes 393224 | tf_op jit(solution)/shard_map/ppermute | solution.py:397
  40.2 9.5 %copy-start.10 = (f32[4]{0:T(128)S(1)}, f32[4]{0:T(128)}, u32[]{:S(2)}) copy-start(f32[4]{0:T(128)} %screening.3) | copy-start | bytes 52
  40.8 18.6 %slice-start = ((s32[16,2048]{1,0:T(8,128)}), s32[16,640]{1,0:T(8,128)S(1)}, s32[]{:S(2)}) async-start(s32[16,2048]{1,0:T(8,128)} %param.15), calls=%async_computation.3 | async-start | bytes 81920 | tf_op jit(solution)/shard_map/slice | solution.py:444
  51.0 19.4 %all-to-all-start.1 = ((f32[8,32,128]{2,1,0:T(8,128)}), f32[8,32,128]{2,1,0:T(8,128)S(1)}, u32[]{:S(2)}, u32[]{:S(2)}) async-start(f32[8,32,128]{2,1,0:T(8,128)} %get-tuple-element.38), calls=%async_computation.1 | async-start | bytes 262144 | tf_op jit(solution)/shard_map/all_to_all | solution.py:445
  70.3 9.8 %slice-start.1 = ((s32[16,2048]{1,0:T(8,128)}), s32[16,896]{1,0:T(8,128)S(1)}, s32[]{:S(2)}) async-start(s32[16,2048]{1,0:T(8,128)} %param.15), calls=%async_computation.4 | async-start | bytes 114688 | tf_op jit(solution)/shard_map/slice | solution.py:450
  71.9 24.6 %all-to-all-start.2 = ((bf16[16,24,512]{2,1,0:T(8,128)(2,1)}), bf16[16,24,512]{2,1,0:T(8,128)(2,1)S(1)}, u32[]{:S(2)}, u32[]{:S(2)}) async-start(bf16[16,24,512]{2,1,0:T(8,128)(2,1)} %local_potential.1), calls=%async_computation.2 | async-start | bytes 786432 | tf_op jit(solution)/shard_map/all_to_all | solution.py:451
  80.8 0.8 copy-start.6
  96.5 1.8 %copy-start.8 = (f32[8,2048]{1,0:T(8,128)S(1)}, f32[8,2048]{1,0:T(8,128)}, u32[]{:S(2)}) copy-start(f32[8,2048]{1,0:T(8,128)} %copy-done.7) | copy-start | bytes 196612
  96.5 1.8 %collective-permute-start.5 = (bf16[384,512]{1,0:T(8,128)(2,1)S(1)}, bf16[384,512]{1,0:T(8,128)(2,1)S(1)}, u32[]{:S(2)}, u32[]{:S(2)}) collective-permute-start(bf16[384,512]{1,0:T(8,128)(2,1)S(1)} %bitcast.18), channel_id=1, source_target_pairs={{0,8},{8,0},{1,9},{9,1},{2,10},{10,2},{3,11},{11,3},{4,12},{12,4},... | collective-permute-start | bytes 1179656 | tf_op jit(solution)/shard_map/ppermute | solution.py:401
  98.4 1.8 %copy-start.3 = (bf16[672,2048]{1,0:T(8,128)(2,1)S(1)}, bf16[672,2048]{1,0:T(8,128)(2,1)}, u32[]{:S(2)}) copy-start(bf16[672,2048]{1,0:T(8,128)(2,1)} %copy-done.2) | copy-start | bytes 8257540

commit v2 on v1

--- a/solution.py
+++ b/solution.py
@@ -34,20 +34,51 @@
 
 smem = pl.BlockSpec(memory_space=pltpu.SMEM)
 vmem = pl.BlockSpec(memory_space=pltpu.VMEM)
+anywhere = pl.BlockSpec(memory_space=pl.ANY)
+hbm = pl.BlockSpec(memory_space=pltpu.HBM)
 
 
 def cost(flops, nbytes):
     return pl.CostEstimate(flops=flops, bytes_accessed=nbytes, transcendentals=0)
 
 
-def params(mebibytes=40):
+def params(mebibytes=8):
     return pltpu.CompilerParams(vmem_limit_bytes=mebibytes << 20)
 
 
 BLOCK = 512
 
 
-def structure_kernel(meta, pos, low, frac, feat, phase, hat, own, other, weighted):
+def structure_kernel(
+    meta,
+    positions,
+    plane_low,
+    plane_height,
+    features,
+    phase_out,
+    hat,
+    own,
+    other,
+    phase,
+    weighted,
+    pos,
+    low,
+    frac,
+    feat,
+    arrived,
+    kept,
+):
+    loads = [
+        pltpu.make_async_copy(source, target, arrived.at[at])
+        for at, (source, target) in enumerate(
+            ((positions, pos), (plane_low, low), (plane_height, frac), (features, feat))
+        )
+    ]
+    for load in loads:
+        load.start()
+    for load in loads:
+        load.wait()
+    keep = pltpu.make_async_copy(phase, phase_out, kept)
     tile_row = lax.broadcasted_iota(jnp.int32, (8, BLOCK), 0)
     upper = tile_row >= 4
     role = tile_row & 3
@@ -116,6 +147,7 @@
         return 0
 
     lax.fori_loop(0, ATOMS // BLOCK, block, 0)
+    keep.start()
     core = meta[0]
     for mine in (False, True):
         start = pl.multiple_of((core if mine else 1 - core) * USED, 16)
@@ -129,6 +161,7 @@
         else:
             other[0:USED, :] = sums.astype(jnp.bfloat16)
             other[USED:HALF, :] = rest.astype(jnp.bfloat16)
+    keep.wait()
 
 
 def local_structure(meta, positions, low, frac, features):
@@ -140,11 +173,20 @@
             jax.ShapeDtypeStruct((HALF, COLS), jnp.float32),
             jax.ShapeDtypeStruct((HALF, COLS), jnp.bfloat16),
         ),
-        in_specs=[smem, vmem, vmem, vmem, vmem],
-        out_specs=(vmem, vmem, vmem, vmem),
-        scratch_shapes=[pltpu.VMEM((ATOMS, COLS), jnp.bfloat16)],
+        in_specs=[smem, hbm, hbm, hbm, hbm],
+        out_specs=(hbm, vmem, vmem, vmem),
+        scratch_shapes=[
+            pltpu.VMEM((2 * USED, ATOMS), jnp.bfloat16),
+            pltpu.VMEM((ATOMS, COLS), jnp.bfloat16),
+            pltpu.VMEM((2, ATOMS), jnp.float32),
+            pltpu.VMEM((1, ATOMS), jnp.int32),
+            pltpu.VMEM((1, ATOMS), jnp.float32),
+            pltpu.VMEM((ATOMS, CHAN), jnp.float32),
+            pltpu.SemaphoreType.DMA((4,)),
+            pltpu.SemaphoreType.DMA,
+        ],
         cost_estimate=cost(1_500_000_000, 8_000_000),
-        compiler_params=params(),
+        compiler_params=params(60),
         name="local_structure",
     )(meta, positions, low, frac, features)
 
@@ -288,80 +330,209 @@
     )(meta, screening, source, carried, alpha, beta)
 
 
-def ghost_kernel(rows, feat, out):
+def ghost_kernel(rows, features, sent, own, arrived):
+    load = pltpu.make_async_copy(features, own, arrived)
+    load.start()
+    load.wait()
+
     def eight(at, _):
         for k in range(8):
-            out[at * 8 + k] = feat[rows[at * 8 + k]]
+            sent[at * 8 + k] = own[rows[at * 8 + k]]
         return 0
 
     lax.fori_loop(0, GHOST // 8, eight, 0)
 
 
-def ghost_rows(rows, feat):
+def ghost_rows(rows, features):
     return pl.pallas_call(
         ghost_kernel,
-        out_shape=jax.ShapeDtypeStruct((GHOST, 1, CHAN), jnp.float32),
-        in_specs=[smem, vmem],
-        out_specs=vmem,
+        out_shape=(
+            jax.ShapeDtypeStruct((GHOST, 1, CHAN), jnp.float32),
+            jax.ShapeDtypeStruct((ATOMS, 1, CHAN), jnp.float32),
+        ),
+        in_specs=[smem, anywhere],
+        out_specs=(vmem, vmem),
+        scratch_shapes=[pltpu.SemaphoreType.DMA],
         cost_estimate=cost(1_000, 1_000_000),
         compiler_params=params(),
         name="ghost_rows",
-    )(rows, feat)
-
-
-def pair_messages(index, weight, table, w_short, name):
-    count = weight.shape[0]
-
-    def kernel(slots, weights, rows, projection, out, sums):
-        place = lax.broadcasted_iota(jnp.int32, (8, CHAN), 0)
-
-        def eight(at, _):
-            base = pl.multiple_of(at * 8, 8)
-            factor = weights[pl.ds(base, 8), :]
-            total = jnp.zeros((8, CHAN), jnp.float32)
-            for k in range(NBR):
-                picked = jnp.broadcast_to(rows[slots[k * count + base]], (8, CHAN))
-                for s in range(1, 8):
-                    found = jnp.broadcast_to(rows[slots[k * count + base + s]], (8, CHAN))
-                    picked = jnp.where(place == s, found, picked)
-                total = total + picked * factor[:, k : k + 1]
-            sums[pl.ds(base, 8), :] = total
+    )(rows, features)
+
+
+GROUP = 4
+STEP = 8
+
+
+def load_slots(neighbours, weight, slots, factors, arrived, first, count):
+    copies = [
+        pltpu.make_async_copy(neighbours.at[k, pl.ds(first, count)], slots[k], arrived.at[k])
+        for k in range(NBR)
+    ]
+    copies.append(
+        pltpu.make_async_copy(weight.at[:, pl.ds(first, count)], factors, arrived.at[NBR])
+    )
+    return copies
+
+
+def weighted_rows(slots, factors, columns, table, sums, count):
+    place = lax.broadcasted_iota(jnp.int32, (8, CHAN), 0)
+    masks = [place == s for s in range(8)]
+    tiles = 128 // GROUP
+
+    def tile(at, _):
+        lane = pl.multiple_of(at * 128, 128)
+        block = factors[:, pl.ds(lane, 128)]
+        for half in range(2):
+            columns[:, half * GROUP : (half + 1) * GROUP, :] = jnp.transpose(
+                block[half * 8 : half * 8 + 8]
+            ).reshape(tiles, GROUP, 8)
+
+        def step(inner, _):
+            parts = []
+            for g in range(STEP):
+                group = inner * STEP + g
+                atoms = [at * 128 + group * GROUP + j for j in range(GROUP)]
+                factor = columns[group]
+                total = None
+                for k in range(8):
+                    picked = None
+                    for half in range(2):
+                        for j in range(GROUP):
+                            found = jnp.broadcast_to(
+                                table[slots[k + 8 * half][atoms[j]]], (8, CHAN)
+                            )
+                            mask = masks[half * GROUP + j]
+                            picked = found if picked is None else jnp.where(mask, found, picked)
+                    term = picked * factor[:, k : k + 1]
+                    total = term if total is None else total + term
+                parts.append(total + pltpu.roll(total, GROUP, 0))
+            for g in range(0, STEP, 2):
+                row = pl.multiple_of(at * 128 + (inner * STEP + g) * GROUP, 8)
+                sums[pl.ds(row, 8), :] = jnp.where(place < GROUP, parts[g], parts[g + 1])
             return 0
 
-        lax.fori_loop(0, count // 8, eight, 0)
-        out[...] = jnp.dot(
-            sums[...],
-            projection[...],
-            preferred_element_type=jnp.float32,
-            precision=lax.Precision.HIGHEST,
-        )
+        return lax.fori_loop(0, tiles // STEP, step, 0)
+
+    lax.fori_loop(0, count // 128, tile, 0)
+
+
+def store_messages(sums, projection, short, out, stored, first, count):
+    short[...] = jnp.dot(
+        sums[...],
+        projection[...],
+        preferred_element_type=jnp.float32,
+        precision=lax.Precision.HIGHEST,
+    )
+    copy = pltpu.make_async_copy(short, out.at[pl.ds(first, count)], stored)
+    copy.start()
+    copy.wait()
+
+
+def pair_scratch(count):
+    return [pltpu.SMEM((count,), jnp.int32)] * NBR + [
+        pltpu.VMEM((NBR, count), jnp.float32),
+        pltpu.VMEM((128 // GROUP, 8, 8), jnp.float32),
+        pltpu.VMEM((count, CHAN), jnp.float32),
+        pltpu.VMEM((count, CHAN), jnp.float32),
+        pltpu.SemaphoreType.DMA((NBR + 1,)),
+        pltpu.SemaphoreType.DMA,
+    ]
+
+
+def first_pairs(meta, neighbours, weight, w_short, features, sides, count):
+    def kernel(meta, index, weights, projection, own, a, b, c, d, table, out, *scratch):
+        slots = scratch[:NBR]
+        factors, columns, sums, short, arrived, stored, placed = scratch[NBR:]
+        loads = load_slots(index, weights, slots, factors, arrived, 0, count)
+        core = meta[0]
+        odd = meta[2] & 1
+        loads.append(pltpu.make_async_copy(own, table.at[pl.ds(0, ATOMS)], placed.at[0]))
+        for at, (rows, slot) in enumerate(
+            ((a, 1 - core), (b, core), (c, 3 - odd), (d, 2 + odd))
+        ):
+            start = ATOMS + slot * GHOST
+            loads.append(
+                pltpu.make_async_copy(rows, table.at[pl.ds(start, GHOST)], placed.at[1 + at])
+            )
+        for load in loads:
+            load.start()
+        for load in loads:
+            load.wait()
+        weighted_rows(slots, factors, columns, table, sums, count)
+        store_messages(sums, projection, short, out, stored, 0, count)
 
     return pl.pallas_call(
         kernel,
-        out_shape=jax.ShapeDtypeStruct((count, CHAN), jnp.float32),
-        in_specs=[smem, vmem, vmem, vmem],
-        out_specs=vmem,
-        scratch_shapes=[pltpu.VMEM((count, CHAN), jnp.float32)],
+        out_shape=(
+            jax.ShapeDtypeStruct((TABLE, 1, CHAN), jnp.float32),
+            jax.ShapeDtypeStruct((ATOMS, CHAN), jnp.float32),
+        ),
+        in_specs=[smem, anywhere, anywhere, vmem] + [anywhere] * 5,
+        out_specs=(vmem, anywhere),
+        scratch_shapes=pair_scratch(count) + [pltpu.SemaphoreType.DMA((5,))],
+        cost_estimate=cost(count * 200_000, count * 57_000),
+        compiler_params=params(),
+        name="first_pairs",
+    )(meta, neighbours, weight, w_short, features, *sides)
+
+
+def more_pairs(neighbours, weight, w_short, table, messages, first, count, name):
+    def kernel(index, weights, projection, rows, before, out, *scratch):
+        slots = scratch[:NBR]
+        factors, columns, sums, short, arrived, stored = scratch[NBR:]
+        loads = load_slots(index, weights, slots, factors, arrived, first, count)
+        for load in loads:
+            load.start()
+        for load in loads:
+            load.wait()
+        weighted_rows(slots, factors, columns, rows, sums, count)
+        store_messages(sums, projection, short, out, stored, first, count)
+
+    return pl.pallas_call(
+        kernel,
+        out_shape=jax.ShapeDtypeStruct((ATOMS, CHAN), jnp.float32),
+        in_specs=[anywhere, anywhere, vmem, vmem, anywhere],
+        out_specs=anywhere,
+        input_output_aliases={4: 0},
+        scratch_shapes=pair_scratch(count),
         cost_estimate=cost(count * 200_000, count * 57_000),
         compiler_params=params(),
         name=name,
-    )(index.reshape(-1), weight, table, w_short)
-
-
-def project_kernel(meta, mine, theirs, phase, hat, short, out):
+    )(neighbours, weight, w_short, table, messages)
+
+
+def project_kernel(meta, mine, theirs, phase_in, hat, short, out, phase, arrived):
+    at = pl.program_id(0)
+    loads = [
+        pltpu.make_async_copy(phase_in.at[:, pl.ds(i * BLOCK, BLOCK)], phase.at[i], arrived.at[i])
+        for i in range(ATOMS // BLOCK)
+    ]
+
+    @pl.when(at == 0)
+    def _():
+        for load in loads:
+            load.start()
+
+    for i, load in enumerate(loads):
+
+        @pl.when(at == i)
+        def _():
+            load.wait()
+
+    atoms = pl.ds(pl.multiple_of(at * BLOCK, BLOCK), BLOCK)
     core = meta[0]
     dims = (((0,), (0,)), ((), ()))
     near = pl.multiple_of(core * USED, 16)
     far = pl.multiple_of((1 - core) * USED, 16)
     projected = lax.dot_general(
-        mine[0:USED, :], phase[pl.ds(near, USED), :], dims, preferred_element_type=jnp.float32
+        mine[0:USED, :], phase[at, pl.ds(near, USED), :], dims, preferred_element_type=jnp.float32
     ) + lax.dot_general(
-        theirs[0:USED, :], phase[pl.ds(far, USED), :], dims, preferred_element_type=jnp.float32
-    )
-    total = hat[0:1, :] * projected[0:CHAN]
+        theirs[0:USED, :], phase[at, pl.ds(far, USED), :], dims, preferred_element_type=jnp.float32
+    )
+    total = hat[0:1, atoms] * projected[0:CHAN]
     for plane in range(1, PLANES):
-        total = total + hat[plane : plane + 1, :] * projected[plane * CHAN : (plane + 1) * CHAN]
-    out[...] = jnp.transpose(total) + short[...]
+        total = total + hat[plane : plane + 1, atoms] * projected[plane * CHAN : (plane + 1) * CHAN]
+    out[...] = jnp.transpose(total) + short[atoms, :]
 
 
 def project(meta, mine, theirs, phase, hat, short):
@@ -369,17 +540,14 @@
         project_kernel,
         grid=(ATOMS // BLOCK,),
         out_shape=jax.ShapeDtypeStruct((ATOMS, CHAN), jnp.float32),
-        in_specs=[
-            smem,
-            pl.BlockSpec((HALF, COLS), lambda i: (0, 0)),
-            pl.BlockSpec((HALF, COLS), lambda i: (0, 0)),
-            pl.BlockSpec((2 * USED, BLOCK), lambda i: (0, i)),
-            pl.BlockSpec((8, BLOCK), lambda i: (0, i)),
-            pl.BlockSpec((BLOCK, CHAN), lambda i: (i, 0)),
+        in_specs=[smem, vmem, vmem, hbm, vmem, vmem],
+        out_specs=pl.BlockSpec((BLOCK, CHAN), lambda i: (i, 0)),
+        scratch_shapes=[
+            pltpu.VMEM((ATOMS // BLOCK, 2 * USED, BLOCK), jnp.bfloat16),
+            pltpu.SemaphoreType.DMA((ATOMS // BLOCK,)),
         ],
-        out_specs=pl.BlockSpec((BLOCK, CHAN), lambda i: (i, 0)),
         cost_estimate=cost(1_500_000_000, 6_000_000),
-        compiler_params=params(),
+        compiler_params=params(50),
         name="project",
     )(meta, mine, theirs, phase, hat, short)
 
@@ -387,14 +555,15 @@
 PIECES = (512, 640, 896)
 
 
-def shifted(value, axis, steps):
+def swapped(value, axis, start):
     count = lax.axis_size(axis)
-    return lax.ppermute(value, axis, [(s, (s + steps) % count) for s in range(count)])
-
-
-def stepped(value, axis, steps):
-    devices = range(lax.axis_size(axis))
-    return lax.ppermute(value, axis, [(i - steps, i) for i in devices if i - steps in devices])
+    ring = axis == LATERAL
+    route = []
+    for low in range(start, count, 2):
+        if low + 1 < count or ring:
+            high = (low + 1) % count
+            route += [(low, high), (high, low)]
+    return lax.ppermute(value, axis, route)
 
 
 def other_core(value):
@@ -423,38 +592,39 @@
     )
     joined = (own + other_core(other).astype(jnp.float32)).astype(jnp.bfloat16)
     joined = joined.reshape(CHUNKS, CHUNK, COLS)
-    joined, ghost_index, weights = tie((joined, ghost_index, pair_weight))
+    joined, ghost_index = tie((joined, ghost_index))
     parts = lax.all_to_all(joined, SWAP, 0, 0)
 
-    sent = ghost_rows(ghost_index, features.reshape(ATOMS, 1, CHAN)).reshape(GHOST, CHAN)
+    sent, own_rows = ghost_rows(ghost_index, features.reshape(ATOMS, 1, CHAN))
     sides = [
-        shifted(sent, LATERAL, 1),
-        shifted(sent, LATERAL, -1),
-        stepped(sent, VERTICAL, 1),
-        stepped(sent, VERTICAL, -1),
+        swapped(sent, LATERAL, 0),
+        swapped(sent, LATERAL, 1),
+        swapped(sent, VERTICAL, 0),
+        swapped(sent, VERTICAL, 1),
     ]
-    table = jnp.concatenate([features] + sides, axis=0).reshape(TABLE, 1, CHAN)
     alpha, beta = coefficients(meta, wave_index, channel_filter)
-    weights = weights.T
     first, second = PIECES[0], PIECES[0] + PIECES[1]
-    short_a = pair_messages(neighbours[:, :first], weights[:first], table, w_short, "pair_a")
-
-    parts, short_a, alpha, beta = tie((parts, short_a, alpha, beta))
+    table, short = first_pairs(meta, neighbours, pair_weight, w_short, own_rows, sides, first)
+
+    parts, short, alpha, beta = tie((parts, short, alpha, beta))
     source, payload = local_source(meta, screening, parts)
-    payload, slots_b = tie((payload, neighbours[:, first:second]))
+    payload, short = tie((payload, short))
     carried = lax.all_to_all(payload, VERTICAL, 0, 0)
-    short_b = pair_messages(slots_b, weights[first:second], table, w_short, "pair_b")
-
-    carried, short_b = tie((carried, short_b))
+    short = more_pairs(
+        neighbours, pair_weight, w_short, table, short, first, PIECES[1], "second_pairs"
+    )
+
+    carried, short = tie((carried, short))
     field = local_potential(meta, screening, source, carried, alpha, beta)
-    field, slots_c = tie((field, neighbours[:, second:]))
+    field, short = tie((field, short))
     mine = lax.all_to_all(field, SWAP, 0, 0)
-    short_c = pair_messages(slots_c, weights[second:], table, w_short, "pair_c")
-
-    mine, short_c = tie((mine, short_c))
+    short = more_pairs(
+        neighbours, pair_weight, w_short, table, short, second, PIECES[2], "third_pairs"
+    )
+
+    mine, short = tie((mine, short))
     mine = mine.reshape(HALF, COLS)
     theirs = other_core(mine)
-    short = jnp.concatenate([short_a, short_b, short_c], axis=0)
     return project(meta, mine, theirs, phase, hat, short)
 
 

time: 107 us -> 97.2 us (0.908)
  local copies, waits for them, and re-layouts: 12.6 us -> 0.05 us
  starting transfers between devices: 37.5 us -> 30.6 us
  waiting for transfers between devices: 3.88 us -> 10.3 us
  Pallas kernels: 49.6 us -> 51.9 us
  other arithmetic: 1.03 us -> 2.67 us
    unnamed x40 -> x20, local copies, waits for them, and re-layouts: 7.6 us -> 0.05 us
    ppermute x4, waiting for transfers between devices: 0.52 us -> 6.55 us  [swapped(): return lax.ppermute(value, axis, route)]
    ppermute x4, starting transfers between devices: 13.4 us -> 10.1 us  [swapped(): return lax.ppermute(value, axis, route)]
    slice x7 -> x0, local copies, waits for them, and re-layouts: 3.03 us -> none  [the longest x1 1.05 us: on_device(): short_c = pair_messages(slots_c, weights[second:], table, w_short, 'pair_c')]
    all_to_all x1, starting transfers between devices: 7.5 us -> 4.8 us  [on_device(): carried = lax.all_to_all(payload, VERTICAL, 0, 0)]
    pallas_call x1, Pallas kernels: 5.72 us -> 8.25 us  [local_structure(): pl.pallas_call(structure_kernel, out_shape=(jax.ShapeDtypeStruct((2 * USE...]
    optimization_barrier x1 -> x0, local copies, waits for them, and re-layouts: 1.31 us -> none  [on_device(): joined, ghost_index, weights = tie((joined, ghost_index, pair_weight))]
    pallas_call x4, Pallas kernels: 35.4 us -> 34.1 us  [the longest x2 24.3 us: more_pairs(): pl.pallas_call(kernel, out_shape=jax.ShapeDtypeStruct((ATOMS, CHAN), jnp....]
  transfers between devices with their start and end apart: 9 -> 9, of which waited for: 3 -> 5; matrix products, arithmetic and copies ran while one was open for 5% -> 0% of each run, Pallas kernels for 34% -> 37%
where the time goes in v2:
time: 97.2 us; the launch traced here: 95.7 us
  Pallas kernels  51.9 us (53%)
  starting transfers between devices  30.6 us (31%)
  waiting for transfers between devices  10.3 us (11%)
  other arithmetic  2.67 us (3%)
    pallas_call x2, Pallas kernels, more_pairs(): pl.pallas_call(kernel, out_shape=jax.ShapeDtypeStruct((ATOMS, CHAN), jnp....  24.3 us
    ppermute x4, starting transfers between devices, swapped(): return lax.ppermute(value, axis, route)  10.1 us
    all_to_all x1, starting transfers between devices, on_device(): parts = lax.all_to_all(joined, SWAP, 0, 0)  9.2 us
    pallas_call x1, Pallas kernels, first_pairs(): pl.pallas_call(kernel, out_shape=(jax.ShapeDtypeStruct((TABLE, 1, CHAN),...  8.86 us
    pallas_call x1, Pallas kernels, local_structure(): pl.pallas_call(structure_kernel, out_shape=(jax.ShapeDtypeStruct((2 * USE...  8.25 us
    ppermute x4, waiting for transfers between devices, swapped(): return lax.ppermute(value, axis, route)  6.55 us
    all_to_all x1, starting transfers between devices, on_device(): mine = lax.all_to_all(field, SWAP, 0, 0)  6.4 us
    pallas_call x1, Pallas kernels, project(): pl.pallas_call(project_kernel, grid=(ATOMS // BLOCK,), out_shape=jax.Shap...  5.85 us
  transfers between devices with their start and end apart: 9, of which 5 were waited for; matrix products, arithmetic and copies ran while one was open for 0% of the time, Pallas kernels for 37%

profile of v2, /device:TPU:4, one launch (start us, length us, event | category | flops | bytes accessed | tf_op | source)
XLA Modules:
  0.0 95.7 jit_solution(11775099508864704358)
XLA Ops:
  0.0 0.7 pad_add_fusion.meta
  0.7 0.0 copy-start.2
  0.7 0.0 copy-start.9
  0.7 8.3 %local_structure.1 = (bf16[672,2048]{1,0:T(8,128)(2,1)}, f32[8,2048]{1,0:T(8,128)}, f32[384,512]{1,0:T(8,128)}, bf16[384,512]{1,0:T(8,128)(2,1)}) custom-call(s32[3]{0:T(128)} %pad_add_fusion.meta, f32[2,2048]{1,0:T(2,128)} %positions.1, s32[1,2048]{1,0:T(1,128)} %bitcast.11, f32[1,2048]{1,0:T(1,128)} %bitcast.12, f32[2048,128]{1,0:T(8,128)} %features.1), custom_call_target="tpu_custom_call" | custom-call | flops 1500000000 | bytes 8000000 | tf_op jit(solution)/shard_map/local_structure/pallas_call | solution.py:168
  8.9 0.0 copy-start.4
  8.9 0.0 copy-start.6
  9.0 0.0 copy-start.7
  9.0 0.0 copy-start
  9.0 0.0 copy-start.1
  9.0 0.0 copy-start.3
  9.0 0.1 collective-permute-start
  9.1 1.9 %collective-permute-done = bf16[384,512]{1,0:T(8,128)(2,1)S(1)} collective-permute-done((bf16[384,512]{1,0:T(8,128)(2,1)}, bf16[384,512]{1,0:T(8,128)(2,1)S(1)}, u32[]{:S(2)}, u32[]{:S(2)}) %collective-permute-start) | collective-permute-done | bytes 393248 | tf_op jit(solution)/shard_map/ppermute | solution.py:570
  11.0 0.0 copy-start.8
  11.0 2.0 %add_convert_fusion = bf16[384,512]{1,0:T(8,128)(2,1)} fusion(f32[384,512]{1,0:T(8,128)} %get-tuple-element.31, bf16[384,512]{1,0:T(8,128)(2,1)S(1)} %collective-permute-done), kind=kLoop, calls=%fused_computation | loop fusion | flops 589824 | bytes 1572864 | tf_op jit(solution)/shard_map/convert_element_type | solution.py:593
  13.0 9.2 %all-to-all-start = ((bf16[16,24,512]{2,1,0:T(8,128)(2,1)}), bf16[16,24,512]{2,1,0:T(8,128)(2,1)S(1)}, u32[]{:S(2)}, u32[]{:S(2)}) async-start(bf16[16,24,512]{2,1,0:T(8,128)(2,1)} %bitcast.5), calls=%async_computation | async-start | bytes 786432 | tf_op jit(solution)/shard_map/all_to_all | solution.py:596
  22.2 0.0 copy-done.2
  22.2 0.0 copy-done.9
  22.3 1.0 ghost_rows.1
  23.2 0.1 collective-permute-start.1
  23.3 4.1 %collective-permute-start.2 = (f32[256,1,128]{2,1,0:T(1,128)S(1)}, f32[256,1,128]{2,1,0:T(1,128)S(1)}, u32[]{:S(2)}, u32[]{:S(2)}) collective-permute-start(f32[256,1,128]{2,1,0:T(1,128)S(1)} %get-tuple-element.36), channel_id=1, source_target_pairs={{8,16},{16,8},{24,32},{32,24},{40,48},{48,40},{56,64},{64,56},{72,... | collective-permute-start | bytes 393224 | tf_op jit(solution)/shard_map/ppermute | solution.py:566
  27.5 1.6 %collective-permute-start.3 = (f32[256,1,128]{2,1,0:T(1,128)S(1)}, f32[256,1,128]{2,1,0:T(1,128)S(1)}, u32[]{:S(2)}, u32[]{:S(2)}) collective-permute-start(f32[256,1,128]{2,1,0:T(1,128)S(1)} %get-tuple-element.36), channel_id=1, source_target_pairs={{0,1},{1,0},{2,3},{3,2},{4,5},{5,4},{6,7},{7,6},{8,9},{9,8},{10,11... | collective-permute-start | bytes 393224 | tf_op jit(solution)/shard_map/ppermute | solution.py:566
  29.0 4.3 %collective-permute-start.4 = (f32[256,1,128]{2,1,0:T(1,128)S(1)}, f32[256,1,128]{2,1,0:T(1,128)S(1)}, u32[]{:S(2)}, u32[]{:S(2)}) collective-permute-start(f32[256,1,128]{2,1,0:T(1,128)S(1)} %get-tuple-element.36), channel_id=1, source_target_pairs={{1,2},{2,1},{3,4},{4,3},{5,6},{6,5},{9,10},{10,9},{11,12},{12,11},... | collective-permute-start | bytes 393224 | tf_op jit(solution)/shard_map/ppermute | solution.py:566
  33.4 0.0 copy-done.4
  33.4 0.0 copy-done.6
  33.4 0.0 copy-done.7
  33.4 0.8 coefficients.1
  34.2 0.0 collective-permute-done.1.a
  34.2 2.2 %collective-permute-done.2.b = f32[256,1,128]{2,1,0:T(1,128)S(1)} collective-permute-done((f32[256,1,128]{2,1,0:T(1,128)S(1)}, f32[256,1,128]{2,1,0:T(1,128)S(1)}, u32[]{:S(2)}, u32[]{:S(2)}) %collective-permute-start.2) | collective-permute-done | bytes 131104 | tf_op jit(solution)/shard_map/ppermute | solution.py:566
  36.4 0.0 collective-permute-done.3.c
  36.4 4.4 %collective-permute-done.4.d = f32[256,1,128]{2,1,0:T(1,128)S(1)} collective-permute-done((f32[256,1,128]{2,1,0:T(1,128)S(1)}, f32[256,1,128]{2,1,0:T(1,128)S(1)}, u32[]{:S(2)}, u32[]{:S(2)}) %collective-permute-start.4) | collective-permute-done | bytes 131104 | tf_op jit(solution)/shard_map/ppermute | solution.py:566
  40.8 0.0 copy-done
  40.8 0.0 copy-done.1
  40.8 0.0 copy-done.3
  40.8 8.9 %first_pairs.1 = (f32[3072,1,128]{2,1,0:T(1,128)S(1)}, f32[2048,128]{1,0:T(8,128)S(1)}) custom-call(s32[3]{0:T(128)S(1)} %copy-done.6, s32[16,2048]{1,0:T(8,128)S(1)} %copy-done, f32[16,2048]{1,0:T(8,128)S(1)} %copy-done.1, f32[128,128]{1,0:T(8,128)S(1)} %copy-done.3, f32[2048,1,128]{2,1,0:T(1,128)S(1)} %get-tuple-element.35.own, ...), custom_call_target="tpu_custom_call" | custom-call | flops 102400000 | bytes 29184000 | tf_op jit(solution)/shard_map/first_pairs/pallas_call | solution.py:464
  49.6 0.0 all-to-all-done.parts
  49.7 0.0 copy-done.8
  49.7 1.3 %local_source.1 = (f32[24,512]{1,0:T(8,128)S(1)}, f32[8,32,128]{2,1,0:T(8,128)}) custom-call(s32[3]{0:T(128)S(1)} %copy-done.6, f32[4]{0:T(128)S(1)} %copy-done.8, bf16[16,24,512]{2,1,0:T(8,128)(2,1)S(1)} %all-to-all-done.parts), custom_call_target="tpu_custom_call" | custom-call | flops 1000000 | bytes 600000 | tf_op jit(solution)/shard_map/local_source/pallas_call | solution.py:270
  51.0 4.8 %all-to-all-start.1 = ((f32[8,32,128]{2,1,0:T(8,128)}), f32[8,32,128]{2,1,0:T(8,128)S(1)}, u32[]{:S(2)}, u32[]{:S(2)}) async-start(f32[8,32,128]{2,1,0:T(8,128)} %get-tuple-element.44), calls=%async_computation.1 | async-start | bytes 262144 | tf_op jit(solution)/shard_map/all_to_all | solution.py:612
  55.8 10.2 %second_pairs.1.before = f32[2048,128]{1,0:T(8,128)S(1)} custom-call(s32[16,2048]{1,0:T(8,128)S(1)} %copy-done, f32[16,2048]{1,0:T(8,128)S(1)} %copy-done.1, f32[128,128]{1,0:T(8,128)S(1)} %copy-done.3, f32[3072,1,128]{2,1,0:T(1,128)S(1)} %get-tuple-element.45.rows, f32[2048,128]{1,0:T(8,128)S(1)} %get-tuple-element.46.before), custom_call_target="tpu_custom_call", output_to_operand_aliasing={{}: (4, {})} | custom-call | flops 128000000 | bytes 36480000 | tf_op jit(solution)/shard_map/second_pairs/pallas_call | solution.py:491
  66.0 0.0 copy-start.5
  66.0 0.0 all-to-all-done.1.carried
  66.0 1.5 %local_potential.1 = bf16[16,24,512]{2,1,0:T(8,128)(2,1)} custom-call(s32[3]{0:T(128)S(1)} %copy-done.6, f32[4]{0:T(128)S(1)} %copy-done.8, f32[24,512]{1,0:T(8,128)S(1)} %get-tuple-element.41.source, f32[8,32,128]{2,1,0:T(8,128)S(1)} %all-to-all-done.1.carried, f32[24,128]{1,0:T(8,128)S(1)} %get-tuple-element.48.alpha, f32[24,128]{1,0:T(8,128)S(1)} %get-tuple-element.49.beta), custom_call_target="tpu_custom_call" | custom-call | flops 1000000 | bytes 1000000 | tf_op jit(solution)/shard_map/local_potential/pallas_call | solution.py:322
  67.5 6.4 %all-to-all-start.2 = ((bf16[16,24,512]{2,1,0:T(8,128)(2,1)}), bf16[16,24,512]{2,1,0:T(8,128)(2,1)S(1)}, u32[]{:S(2)}, u32[]{:S(2)}) async-start(bf16[16,24,512]{2,1,0:T(8,128)(2,1)} %local_potential.1), calls=%async_computation.2 | async-start | bytes 786432 | tf_op jit(solution)/shard_map/all_to_all | solution.py:620
  73.9 14.1 %third_pairs.1.short = f32[2048,128]{1,0:T(8,128)S(1)} custom-call(s32[16,2048]{1,0:T(8,128)S(1)} %copy-done, f32[16,2048]{1,0:T(8,128)S(1)} %copy-done.1, f32[128,128]{1,0:T(8,128)S(1)} %copy-done.3, f32[3072,1,128]{2,1,0:T(1,128)S(1)} %get-tuple-element.45.rows, f32[2048,128]{1,0:T(8,128)S(1)} %second_pairs.1.before), custom_call_target="tpu_custom_call", output_to_operand_aliasing={{}: (4, {})} | custom-call | flops 179200000 | bytes 51072000 | tf_op jit(solution)/shard_map/third_pairs/pallas_call | solution.py:491
  88.1 0.1 all-to-all-done.2
  88.1 0.0 collective-permute-start.5
  88.2 1.7 %collective-permute-done.5.theirs = bf16[384,512]{1,0:T(8,128)(2,1)S(1)} collective-permute-done((bf16[384,512]{1,0:T(8,128)(2,1)S(1)}, bf16[384,512]{1,0:T(8,128)(2,1)S(1)}, u32[]{:S(2)}, u32[]{:S(2)}) %collective-permute-start.5) | collective-permute-done | bytes 393248 | tf_op jit(solution)/shard_map/ppermute | solution.py:570
  89.9 0.0 copy-done.5
  89.9 5.9 %project.1 = f32[2048,128]{1,0:T(8,128)} custom-call(s32[3]{0:T(128)S(1)} %copy-done.6, bf16[384,512]{1,0:T(8,128)(2,1)S(1)} %bitcast.9, bf16[384,512]{1,0:T(8,128)(2,1)S(1)} %collective-permute-done.5.theirs, bf16[672,2048]{1,0:T(8,128)(2,1)} %get-tuple-element.54.phase_in, f32[8,2048]{1,0:T(8,128)S(1)} %copy-done.5, f32[2048,128]{1,0:T(8,128)S(1)} %third_pairs.1.short), custom_call_target="tpu_custom_call" | custom-call | flops 1500000000 | bytes 6000000 | tf_op jit(solution)/shard_map/project/pallas_call | solution.py:539
Async XLA Ops:
  0.7 21.6 %copy-start.2 = (f32[2048,128]{1,0:T(8,128)S(1)}, f32[2048,128]{1,0:T(8,128)}, u32[]{:S(2)}) copy-start(f32[2048,128]{1,0:T(8,128)} %features.1) | copy-start | bytes 3145732
  0.7 21.6 %copy-start.9 = (s32[256]{0:T(256)S(1)}, s32[256]{0:T(256)}, u32[]{:S(2)}) copy-start(s32[256]{0:T(256)} %rows) | copy-start | bytes 3076
  8.9 24.4 %copy-start.4 = (f32[512,128]{1,0:T(8,128)S(1)}, f32[512,128]{1,0:T(8,128)}, u32[]{:S(2)}) copy-start(f32[512,128]{1,0:T(8,128)} %filters.1) | copy-start | bytes 786436
  8.9 24.4 %copy-start.6 = (s32[3]{0:T(128)S(1)}, s32[3]{0:T(128)}, u32[]{:S(2)}) copy-start(s32[3]{0:T(128)} %pad_add_fusion.meta) | copy-start | bytes 40
  9.0 24.4 %copy-start.7 = (s32[2,512]{1,0:T(2,128)S(1)}, s32[2,512]{1,0:T(2,128)}, u32[]{:S(2)}) copy-start(s32[2,512]{1,0:T(2,128)} %waves.1) | copy-start | bytes 12292
  9.0 31.8 %copy-start = (s32[16,2048]{1,0:T(8,128)S(1)}, s32[16,2048]{1,0:T(8,128)}, u32[]{:S(2)}) copy-start(s32[16,2048]{1,0:T(8,128)} %index.5) | copy-start | bytes 393220
  9.0 31.8 %copy-start.1 = (f32[16,2048]{1,0:T(8,128)S(1)}, f32[16,2048]{1,0:T(8,128)}, u32[]{:S(2)}) copy-start(f32[16,2048]{1,0:T(8,128)} %weights.5) | copy-start | bytes 393220
  9.0 31.8 %copy-start.3 = (f32[128,128]{1,0:T(8,128)S(1)}, f32[128,128]{1,0:T(8,128)}, u32[]{:S(2)}) copy-start(f32[128,128]{1,0:T(8,128)} %projection.5) | copy-start | bytes 196612
  9.0 2.0 %collective-permute-start = (bf16[384,512]{1,0:T(8,128)(2,1)}, bf16[384,512]{1,0:T(8,128)(2,1)S(1)}, u32[]{:S(2)}, u32[]{:S(2)}) collective-permute-start(bf16[384,512]{1,0:T(8,128)(2,1)} %get-tuple-element.32), channel_id=1, source_target_pairs={{0,8},{8,0},{1,9},{9,1},{2,10},{10,2},{3,11},{11,3},{4,12},{12,4},... | collective-permute-start | bytes 1179656 | tf_op jit(solution)/shard_map/ppermute | solution.py:570
  11.0 38.6 %copy-start.8 = (f32[4]{0:T(128)S(1)}, f32[4]{0:T(128)}, u32[]{:S(2)}) copy-start(f32[4]{0:T(128)} %screening.3) | copy-start | bytes 52
  13.0 36.6 %all-to-all-start = ((bf16[16,24,512]{2,1,0:T(8,128)(2,1)}), bf16[16,24,512]{2,1,0:T(8,128)(2,1)S(1)}, u32[]{:S(2)}, u32[]{:S(2)}) async-start(bf16[16,24,512]{2,1,0:T(8,128)(2,1)} %bitcast.5), calls=%async_computation | async-start | bytes 786432 | tf_op jit(solution)/shard_map/all_to_all | solution.py:596
  23.2 11.0 %collective-permute-start.1 = (f32[256,1,128]{2,1,0:T(1,128)S(1)}, f32[256,1,128]{2,1,0:T(1,128)S(1)}, u32[]{:S(2)}, u32[]{:S(2)}) collective-permute-start(f32[256,1,128]{2,1,0:T(1,128)S(1)} %get-tuple-element.36), channel_id=1, source_target_pairs={{0,8},{8,0},{16,24},{24,16},{32,40},{40,32},{48,56},{56,48},{64,72... | collective-permute-start | bytes 393224 | tf_op jit(solution)/shard_map/ppermute | solution.py:566
  23.3 13.1 %collective-permute-start.2 = (f32[256,1,128]{2,1,0:T(1,128)S(1)}, f32[256,1,128]{2,1,0:T(1,128)S(1)}, u32[]{:S(2)}, u32[]{:S(2)}) collective-permute-start(f32[256,1,128]{2,1,0:T(1,128)S(1)} %get-tuple-element.36), channel_id=1, source_target_pairs={{8,16},{16,8},{24,32},{32,24},{40,48},{48,40},{56,64},{64,56},{72,... | collective-permute-start | bytes 393224 | tf_op jit(solution)/shard_map/ppermute | solution.py:566
  27.5 8.9 %collective-permute-start.3 = (f32[256,1,128]{2,1,0:T(1,128)S(1)}, f32[256,1,128]{2,1,0:T(1,128)S(1)}, u32[]{:S(2)}, u32[]{:S(2)}) collective-permute-start(f32[256,1,128]{2,1,0:T(1,128)S(1)} %get-tuple-element.36), channel_id=1, source_target_pairs={{0,1},{1,0},{2,3},{3,2},{4,5},{5,4},{6,7},{7,6},{8,9},{9,8},{10,11... | collective-permute-start | bytes 393224 | tf_op jit(solution)/shard_map/ppermute | solution.py:566
  29.0 11.7 %collective-permute-start.4 = (f32[256,1,128]{2,1,0:T(1,128)S(1)}, f32[256,1,128]{2,1,0:T(1,128)S(1)}, u32[]{:S(2)}, u32[]{:S(2)}) collective-permute-start(f32[256,1,128]{2,1,0:T(1,128)S(1)} %get-tuple-element.36), channel_id=1, source_target_pairs={{1,2},{2,1},{3,4},{4,3},{5,6},{6,5},{9,10},{10,9},{11,12},{12,11},... | collective-permute-start | bytes 393224 | tf_op jit(solution)/shard_map/ppermute | solution.py:566
  51.0 15.0 %all-to-all-start.1 = ((f32[8,32,128]{2,1,0:T(8,128)}), f32[8,32,128]{2,1,0:T(8,128)S(1)}, u32[]{:S(2)}, u32[]{:S(2)}) async-start(f32[8,32,128]{2,1,0:T(8,128)} %get-tuple-element.44), calls=%async_computation.1 | async-start | bytes 262144 | tf_op jit(solution)/shard_map/all_to_all | solution.py:612
  66.0 23.9 %copy-start.5 = (f32[8,2048]{1,0:T(8,128)S(1)}, f32[8,2048]{1,0:T(8,128)}, u32[]{:S(2)}) copy-start(f32[8,2048]{1,0:T(8,128)} %get-tuple-element.55.hat) | copy-start | bytes 196612
  67.5 20.6 %all-to-all-start.2 = ((bf16[16,24,512]{2,1,0:T(8,128)(2,1)}), bf16[16,24,512]{2,1,0:T(8,128)(2,1)S(1)}, u32[]{:S(2)}, u32[]{:S(2)}) async-start(bf16[16,24,512]{2,1,0:T(8,128)(2,1)} %local_potential.1), calls=%async_computation.2 | async-start | bytes 786432 | tf_op jit(solution)/shard_map/all_to_all | solution.py:620
  88.1 1.7 %collective-permute-start.5 = (bf16[384,512]{1,0:T(8,128)(2,1)S(1)}, bf16[384,512]{1,0:T(8,128)(2,1)S(1)}, u32[]{:S(2)}, u32[]{:S(2)}) collective-permute-start(bf16[384,512]{1,0:T(8,128)(2,1)S(1)} %bitcast.8), channel_id=1, source_target_pairs={{0,8},{8,0},{1,9},{9,1},{2,10},{10,2},{3,11},{11,3},{4,12},{12,4},... | collective-permute-start | bytes 1179656 | tf_op jit(solution)/shard_map/ppermute | solution.py:570

commit v3 on v2

--- a/solution.py
+++ b/solution.py
@@ -364,56 +364,54 @@
 
 
 def load_slots(neighbours, weight, slots, factors, arrived, first, count):
+    quarter = count // GROUP
     copies = [
-        pltpu.make_async_copy(neighbours.at[k, pl.ds(first, count)], slots[k], arrived.at[k])
+        pltpu.make_async_copy(
+            neighbours.at[k, pl.ds(first + j * quarter, quarter)],
+            slots[k * GROUP + j],
+            arrived.at[k * GROUP + j],
+        )
         for k in range(NBR)
+        for j in range(GROUP)
     ]
     copies.append(
-        pltpu.make_async_copy(weight.at[:, pl.ds(first, count)], factors, arrived.at[NBR])
+        pltpu.make_async_copy(
+            weight.at[:, pl.ds(first, count)], factors, arrived.at[NBR * GROUP]
+        )
     )
     return copies
 
 
 def weighted_rows(slots, factors, columns, table, sums, count):
+    quarter = count // GROUP
     place = lax.broadcasted_iota(jnp.int32, (8, CHAN), 0)
     masks = [place == s for s in range(8)]
-    tiles = 128 // GROUP
-
-    def tile(at, _):
-        lane = pl.multiple_of(at * 128, 128)
-        block = factors[:, pl.ds(lane, 128)]
+    for j in range(GROUP):
         for half in range(2):
-            columns[:, half * GROUP : (half + 1) * GROUP, :] = jnp.transpose(
-                block[half * 8 : half * 8 + 8]
-            ).reshape(tiles, GROUP, 8)
-
-        def step(inner, _):
-            parts = []
-            for g in range(STEP):
-                group = inner * STEP + g
-                atoms = [at * 128 + group * GROUP + j for j in range(GROUP)]
-                factor = columns[group]
-                total = None
-                for k in range(8):
-                    picked = None
-                    for half in range(2):
-                        for j in range(GROUP):
-                            found = jnp.broadcast_to(
-                                table[slots[k + 8 * half][atoms[j]]], (8, CHAN)
-                            )
-                            mask = masks[half * GROUP + j]
-                            picked = found if picked is None else jnp.where(mask, found, picked)
-                    term = picked * factor[:, k : k + 1]
-                    total = term if total is None else total + term
-                parts.append(total + pltpu.roll(total, GROUP, 0))
-            for g in range(0, STEP, 2):
-                row = pl.multiple_of(at * 128 + (inner * STEP + g) * GROUP, 8)
-                sums[pl.ds(row, 8), :] = jnp.where(place < GROUP, parts[g], parts[g + 1])
-            return 0
-
-        return lax.fori_loop(0, tiles // STEP, step, 0)
-
-    lax.fori_loop(0, count // 128, tile, 0)
+            columns[:, half * GROUP + j, :] = jnp.transpose(
+                factors[half * 8 : half * 8 + 8, j * quarter : (j + 1) * quarter]
+            )
+
+    def step(at, _):
+        for g in range(STEP):
+            group = at * STEP + g
+            factor = columns[group]
+            total = None
+            for k in range(8):
+                picked = None
+                for half in range(2):
+                    for j in range(GROUP):
+                        row = slots[(k + 8 * half) * GROUP + j][group]
+                        found = jnp.broadcast_to(table[row], (8, CHAN))
+                        mask = masks[half * GROUP + j]
+                        picked = found if picked is None else jnp.where(mask, found, picked)
+                term = picked * factor[:, k : k + 1]
+                total = term if total is None else total + term
+            total = total + pltpu.roll(total, GROUP, 0)
+            sums[pl.ds(group, GROUP, stride=quarter), :] = total[0:GROUP]
+        return 0
+
+    lax.fori_loop(0, quarter // STEP, step, 0)
 
 
 def store_messages(sums, projection, short, out, stored, first, count):
@@ -429,20 +427,20 @@
 
 
 def pair_scratch(count):
-    return [pltpu.SMEM((count,), jnp.int32)] * NBR + [
+    return [pltpu.SMEM((count // GROUP,), jnp.int32)] * (NBR * GROUP) + [
         pltpu.VMEM((NBR, count), jnp.float32),
-        pltpu.VMEM((128 // GROUP, 8, 8), jnp.float32),
+        pltpu.VMEM((count // GROUP, 8, 8), jnp.float32),
         pltpu.VMEM((count, CHAN), jnp.float32),
         pltpu.VMEM((count, CHAN), jnp.float32),
-        pltpu.SemaphoreType.DMA((NBR + 1,)),
+        pltpu.SemaphoreType.DMA((NBR * GROUP + 1,)),
         pltpu.SemaphoreType.DMA,
     ]
 
 
 def first_pairs(meta, neighbours, weight, w_short, features, sides, count):
     def kernel(meta, index, weights, projection, own, a, b, c, d, table, out, *scratch):
-        slots = scratch[:NBR]
-        factors, columns, sums, short, arrived, stored, placed = scratch[NBR:]
+        slots = scratch[: NBR * GROUP]
+        factors, columns, sums, short, arrived, stored, placed = scratch[NBR * GROUP :]
         loads = load_slots(index, weights, slots, factors, arrived, 0, count)
         core = meta[0]
         odd = meta[2] & 1
@@ -478,8 +476,8 @@
 
 def more_pairs(neighbours, weight, w_short, table, messages, first, count, name):
     def kernel(index, weights, projection, rows, before, out, *scratch):
-        slots = scratch[:NBR]
-        factors, columns, sums, short, arrived, stored = scratch[NBR:]
+        slots = scratch[: NBR * GROUP]
+        factors, columns, sums, short, arrived, stored = scratch[NBR * GROUP :]
         loads = load_slots(index, weights, slots, factors, arrived, first, count)
         for load in loads:
             load.start()
@@ -552,7 +550,7 @@
     )(meta, mine, theirs, phase, hat, short)
 
 
-PIECES = (512, 640, 896)
+PIECES = (512, 512, 1024)
 
 
 def swapped(value, axis, start):

time: 97.2 us -> 94.6 us (0.973)
  Pallas kernels: 51.9 us -> 49.2 us
    pallas_call x2, Pallas kernels: 24.3 us -> 21.9 us  [more_pairs(): pl.pallas_call(kernel, out_shape=jax.ShapeDtypeStruct((ATOMS, CHAN), jnp....]
  transfers between devices with their start and end apart: 9 -> 9, of which waited for: 5 -> 5; matrix products, arithmetic and copies ran while one was open for 0% -> 0% of each run, Pallas kernels for 37% -> 35%
where the time goes in v3:
time: 94.6 us; the launch traced here: 93.1 us
  Pallas kernels  49.2 us (52%)
  starting transfers between devices  30.7 us (32%)
  waiting for transfers between devices  10.2 us (11%)
  other arithmetic  2.67 us (3%)
    pallas_call x2, Pallas kernels, more_pairs(): pl.pallas_call(kernel, out_shape=jax.ShapeDtypeStruct((ATOMS, CHAN), jnp....  21.9 us
    ppermute x4, starting transfers between devices, swapped(): return lax.ppermute(value, axis, route)  10.1 us
    all_to_all x1, starting transfers between devices, on_device(): parts = lax.all_to_all(joined, SWAP, 0, 0)  9.2 us
    pallas_call x1, Pallas kernels, first_pairs(): pl.pallas_call(kernel, out_shape=(jax.ShapeDtypeStruct((TABLE, 1, CHAN),...  8.66 us
    pallas_call x1, Pallas kernels, local_structure(): pl.pallas_call(structure_kernel, out_shape=(jax.ShapeDtypeStruct((2 * USE...  8.25 us
    ppermute x4, waiting for transfers between devices, swapped(): return lax.ppermute(value, axis, route)  6.55 us
    all_to_all x1, starting transfers between devices, on_device(): mine = lax.all_to_all(field, SWAP, 0, 0)  6.41 us
    pallas_call x1, Pallas kernels, project(): pl.pallas_call(project_kernel, grid=(ATOMS // BLOCK,), out_shape=jax.Shap...  5.85 us
  transfers between devices with their start and end apart: 9, of which 5 were waited for; matrix products, arithmetic and copies ran while one was open for 0% of the time, Pallas kernels for 35%

profile of v3, /device:TPU:4, one launch (start us, length us, event | category | flops | bytes accessed | tf_op | source)
XLA Modules:
  0.0 93.1 jit_solution(12091307894571471097)
XLA Ops:
  0.0 0.7 pad_add_fusion.meta
  0.7 0.0 copy-start.2
  0.7 0.0 copy-start.9
  0.7 8.3 %local_structure.1 = (bf16[672,2048]{1,0:T(8,128)(2,1)}, f32[8,2048]{1,0:T(8,128)}, f32[384,512]{1,0:T(8,128)}, bf16[384,512]{1,0:T(8,128)(2,1)}) custom-call(s32[3]{0:T(128)} %pad_add_fusion.meta, f32[2,2048]{1,0:T(2,128)} %positions.1, s32[1,2048]{1,0:T(1,128)} %bitcast.11, f32[1,2048]{1,0:T(1,128)} %bitcast.12, f32[2048,128]{1,0:T(8,128)} %features.1), custom_call_target="tpu_custom_call" | custom-call | flops 1500000000 | bytes 8000000 | tf_op jit(solution)/shard_map/local_structure/pallas_call | solution.py:168
  8.9 0.0 copy-start.4
  8.9 0.0 copy-start.6
  9.0 0.0 copy-start.7
  9.0 0.0 copy-start
  9.0 0.0 copy-start.1
  9.0 0.0 copy-start.3
  9.0 0.1 collective-permute-start
  9.1 1.9 %collective-permute-done = bf16[384,512]{1,0:T(8,128)(2,1)S(1)} collective-permute-done((bf16[384,512]{1,0:T(8,128)(2,1)}, bf16[384,512]{1,0:T(8,128)(2,1)S(1)}, u32[]{:S(2)}, u32[]{:S(2)}) %collective-permute-start) | collective-permute-done | bytes 393248 | tf_op jit(solution)/shard_map/ppermute | solution.py:568
  11.0 0.0 copy-start.8
  11.0 2.0 %add_convert_fusion = bf16[384,512]{1,0:T(8,128)(2,1)} fusion(f32[384,512]{1,0:T(8,128)} %get-tuple-element.31, bf16[384,512]{1,0:T(8,128)(2,1)S(1)} %collective-permute-done), kind=kLoop, calls=%fused_computation | loop fusion | flops 589824 | bytes 1572864 | tf_op jit(solution)/shard_map/convert_element_type | solution.py:591
  13.0 9.2 %all-to-all-start = ((bf16[16,24,512]{2,1,0:T(8,128)(2,1)}), bf16[16,24,512]{2,1,0:T(8,128)(2,1)S(1)}, u32[]{:S(2)}, u32[]{:S(2)}) async-start(bf16[16,24,512]{2,1,0:T(8,128)(2,1)} %bitcast.5), calls=%async_computation | async-start | bytes 786432 | tf_op jit(solution)/shard_map/all_to_all | solution.py:594
  22.2 0.0 copy-done.2
  22.2 0.0 copy-done.9
  22.3 1.0 %ghost_rows.1 = (f32[256,1,128]{2,1,0:T(1,128)S(1)}, f32[2048,1,128]{2,1,0:T(1,128)S(1)}) custom-call(s32[256]{0:T(256)S(1)} %copy-done.9, f32[2048,1,128]{2,1,0:T(1,128)S(1)} %bitcast.10), custom_call_target="tpu_custom_call" | custom-call | flops 1000 | bytes 1000000 | tf_op jit(solution)/shard_map/ghost_rows/pallas_call | solution.py:347
  23.2 0.1 collective-permute-start.1
  23.3 4.1 %collective-permute-start.2 = (f32[256,1,128]{2,1,0:T(1,128)S(1)}, f32[256,1,128]{2,1,0:T(1,128)S(1)}, u32[]{:S(2)}, u32[]{:S(2)}) collective-permute-start(f32[256,1,128]{2,1,0:T(1,128)S(1)} %get-tuple-element.36), channel_id=1, source_target_pairs={{8,16},{16,8},{24,32},{32,24},{40,48},{48,40},{56,64},{64,56},{72,... | collective-permute-start | bytes 393224 | tf_op jit(solution)/shard_map/ppermute | solution.py:564
  27.5 1.6 %collective-permute-start.3 = (f32[256,1,128]{2,1,0:T(1,128)S(1)}, f32[256,1,128]{2,1,0:T(1,128)S(1)}, u32[]{:S(2)}, u32[]{:S(2)}) collective-permute-start(f32[256,1,128]{2,1,0:T(1,128)S(1)} %get-tuple-element.36), channel_id=1, source_target_pairs={{0,1},{1,0},{2,3},{3,2},{4,5},{5,4},{6,7},{7,6},{8,9},{9,8},{10,11... | collective-permute-start | bytes 393224 | tf_op jit(solution)/shard_map/ppermute | solution.py:564
  29.0 4.3 %collective-permute-start.4 = (f32[256,1,128]{2,1,0:T(1,128)S(1)}, f32[256,1,128]{2,1,0:T(1,128)S(1)}, u32[]{:S(2)}, u32[]{:S(2)}) collective-permute-start(f32[256,1,128]{2,1,0:T(1,128)S(1)} %get-tuple-element.36), channel_id=1, source_target_pairs={{1,2},{2,1},{3,4},{4,3},{5,6},{6,5},{9,10},{10,9},{11,12},{12,11},... | collective-permute-start | bytes 393224 | tf_op jit(solution)/shard_map/ppermute | solution.py:564
  33.4 0.0 copy-done.4
  33.4 0.0 copy-done.6
  33.4 0.0 copy-done.7
  33.4 0.8 coefficients.1
  34.2 0.0 collective-permute-done.1.a
  34.2 2.2 %collective-permute-done.2.b = f32[256,1,128]{2,1,0:T(1,128)S(1)} collective-permute-done((f32[256,1,128]{2,1,0:T(1,128)S(1)}, f32[256,1,128]{2,1,0:T(1,128)S(1)}, u32[]{:S(2)}, u32[]{:S(2)}) %collective-permute-start.2) | collective-permute-done | bytes 131104 | tf_op jit(solution)/shard_map/ppermute | solution.py:564
  36.4 0.0 collective-permute-done.3.c
  36.4 4.4 %collective-permute-done.4.d = f32[256,1,128]{2,1,0:T(1,128)S(1)} collective-permute-done((f32[256,1,128]{2,1,0:T(1,128)S(1)}, f32[256,1,128]{2,1,0:T(1,128)S(1)}, u32[]{:S(2)}, u32[]{:S(2)}) %collective-permute-start.4) | collective-permute-done | bytes 131104 | tf_op jit(solution)/shard_map/ppermute | solution.py:564
  40.8 0.0 copy-done
  40.8 0.0 copy-done.1
  40.8 0.0 copy-done.3
  40.8 8.7 %first_pairs.1 = (f32[3072,1,128]{2,1,0:T(1,128)S(1)}, f32[2048,128]{1,0:T(8,128)S(1)}) custom-call(s32[3]{0:T(128)S(1)} %copy-done.6, s32[16,2048]{1,0:T(8,128)S(1)} %copy-done, f32[16,2048]{1,0:T(8,128)S(1)} %copy-done.1, f32[128,128]{1,0:T(8,128)S(1)} %copy-done.3, f32[2048,1,128]{2,1,0:T(1,128)S(1)} %get-tuple-element.35.own, ...), custom_call_target="tpu_custom_call" | custom-call | flops 102400000 | bytes 29184000 | tf_op jit(solution)/shard_map/first_pairs/pallas_call | solution.py:462
  49.4 0.0 all-to-all-done.parts
  49.5 0.0 copy-done.8
  49.5 1.3 %local_source.1 = (f32[24,512]{1,0:T(8,128)S(1)}, f32[8,32,128]{2,1,0:T(8,128)}) custom-call(s32[3]{0:T(128)S(1)} %copy-done.6, f32[4]{0:T(128)S(1)} %copy-done.8, bf16[16,24,512]{2,1,0:T(8,128)(2,1)S(1)} %all-to-all-done.parts), custom_call_target="tpu_custom_call" | custom-call | flops 1000000 | bytes 600000 | tf_op jit(solution)/shard_map/local_source/pallas_call | solution.py:270
  50.8 4.8 %all-to-all-start.1 = ((f32[8,32,128]{2,1,0:T(8,128)}), f32[8,32,128]{2,1,0:T(8,128)S(1)}, u32[]{:S(2)}, u32[]{:S(2)}) async-start(f32[8,32,128]{2,1,0:T(8,128)} %get-tuple-element.44), calls=%async_computation.1 | async-start | bytes 262144 | tf_op jit(solution)/shard_map/all_to_all | solution.py:610
  55.6 7.7 %second_pairs.1.before = f32[2048,128]{1,0:T(8,128)S(1)} custom-call(s32[16,2048]{1,0:T(8,128)S(1)} %copy-done, f32[16,2048]{1,0:T(8,128)S(1)} %copy-done.1, f32[128,128]{1,0:T(8,128)S(1)} %copy-done.3, f32[3072,1,128]{2,1,0:T(1,128)S(1)} %get-tuple-element.45.rows, f32[2048,128]{1,0:T(8,128)S(1)} %get-tuple-element.46.before), custom_call_target="tpu_custom_call", output_to_operand_aliasing={{}: (4, {})} | custom-call | flops 102400000 | bytes 29184000 | tf_op jit(solution)/shard_map/second_pairs/pallas_call | solution.py:489
  63.3 0.0 copy-start.5
  63.3 0.0 all-to-all-done.1.carried
  63.3 1.5 %local_potential.1 = bf16[16,24,512]{2,1,0:T(8,128)(2,1)} custom-call(s32[3]{0:T(128)S(1)} %copy-done.6, f32[4]{0:T(128)S(1)} %copy-done.8, f32[24,512]{1,0:T(8,128)S(1)} %get-tuple-element.41.source, f32[8,32,128]{2,1,0:T(8,128)S(1)} %all-to-all-done.1.carried, f32[24,128]{1,0:T(8,128)S(1)} %get-tuple-element.48.alpha, f32[24,128]{1,0:T(8,128)S(1)} %get-tuple-element.49.beta), custom_call_target="tpu_custom_call" | custom-call | flops 1000000 | bytes 1000000 | tf_op jit(solution)/shard_map/local_potential/pallas_call | solution.py:322
  64.9 6.4 %all-to-all-start.2 = ((bf16[16,24,512]{2,1,0:T(8,128)(2,1)}), bf16[16,24,512]{2,1,0:T(8,128)(2,1)S(1)}, u32[]{:S(2)}, u32[]{:S(2)}) async-start(bf16[16,24,512]{2,1,0:T(8,128)(2,1)} %local_potential.1), calls=%async_computation.2 | async-start | bytes 786432 | tf_op jit(solution)/shard_map/all_to_all | solution.py:618
  71.3 14.1 %third_pairs.1.short = f32[2048,128]{1,0:T(8,128)S(1)} custom-call(s32[16,2048]{1,0:T(8,128)S(1)} %copy-done, f32[16,2048]{1,0:T(8,128)S(1)} %copy-done.1, f32[128,128]{1,0:T(8,128)S(1)} %copy-done.3, f32[3072,1,128]{2,1,0:T(1,128)S(1)} %get-tuple-element.45.rows, f32[2048,128]{1,0:T(8,128)S(1)} %second_pairs.1.before), custom_call_target="tpu_custom_call", output_to_operand_aliasing={{}: (4, {})} | custom-call | flops 204800000 | bytes 58368000 | tf_op jit(solution)/shard_map/third_pairs/pallas_call | solution.py:489
  85.4 0.1 all-to-all-done.2
  85.5 0.0 collective-permute-start.5
  85.5 1.7 %collective-permute-done.5.theirs = bf16[384,512]{1,0:T(8,128)(2,1)S(1)} collective-permute-done((bf16[384,512]{1,0:T(8,128)(2,1)S(1)}, bf16[384,512]{1,0:T(8,128)(2,1)S(1)}, u32[]{:S(2)}, u32[]{:S(2)}) %collective-permute-start.5) | collective-permute-done | bytes 393248 | tf_op jit(solution)/shard_map/ppermute | solution.py:568
  87.2 0.0 copy-done.5
  87.2 5.8 %project.1 = f32[2048,128]{1,0:T(8,128)} custom-call(s32[3]{0:T(128)S(1)} %copy-done.6, bf16[384,512]{1,0:T(8,128)(2,1)S(1)} %bitcast.9, bf16[384,512]{1,0:T(8,128)(2,1)S(1)} %collective-permute-done.5.theirs, bf16[672,2048]{1,0:T(8,128)(2,1)} %get-tuple-element.54.phase_in, f32[8,2048]{1,0:T(8,128)S(1)} %copy-done.5, f32[2048,128]{1,0:T(8,128)S(1)} %third_pairs.1.short), custom_call_target="tpu_custom_call" | custom-call | flops 1500000000 | bytes 6000000 | tf_op jit(solution)/shard_map/project/pallas_call | solution.py:537
Async XLA Ops:
  0.7 21.6 %copy-start.2 = (f32[2048,128]{1,0:T(8,128)S(1)}, f32[2048,128]{1,0:T(8,128)}, u32[]{:S(2)}) copy-start(f32[2048,128]{1,0:T(8,128)} %features.1) | copy-start | bytes 3145732
  0.7 21.6 %copy-start.9 = (s32[256]{0:T(256)S(1)}, s32[256]{0:T(256)}, u32[]{:S(2)}) copy-start(s32[256]{0:T(256)} %rows) | copy-start | bytes 3076
  8.9 24.4 %copy-start.4 = (f32[512,128]{1,0:T(8,128)S(1)}, f32[512,128]{1,0:T(8,128)}, u32[]{:S(2)}) copy-start(f32[512,128]{1,0:T(8,128)} %filters.1) | copy-start | bytes 786436
  8.9 24.4 %copy-start.6 = (s32[3]{0:T(128)S(1)}, s32[3]{0:T(128)}, u32[]{:S(2)}) copy-start(s32[3]{0:T(128)} %pad_add_fusion.meta) | copy-start | bytes 40
  9.0 24.4 %copy-start.7 = (s32[2,512]{1,0:T(2,128)S(1)}, s32[2,512]{1,0:T(2,128)}, u32[]{:S(2)}) copy-start(s32[2,512]{1,0:T(2,128)} %waves.1) | copy-start | bytes 12292
  9.0 31.8 %copy-start = (s32[16,2048]{1,0:T(8,128)S(1)}, s32[16,2048]{1,0:T(8,128)}, u32[]{:S(2)}) copy-start(s32[16,2048]{1,0:T(8,128)} %index.5) | copy-start | bytes 393220
  9.0 31.8 %copy-start.1 = (f32[16,2048]{1,0:T(8,128)S(1)}, f32[16,2048]{1,0:T(8,128)}, u32[]{:S(2)}) copy-start(f32[16,2048]{1,0:T(8,128)} %weights.5) | copy-start | bytes 393220
  9.0 31.8 %copy-start.3 = (f32[128,128]{1,0:T(8,128)S(1)}, f32[128,128]{1,0:T(8,128)}, u32[]{:S(2)}) copy-start(f32[128,128]{1,0:T(8,128)} %projection.5) | copy-start | bytes 196612
  9.0 2.0 %collective-permute-start = (bf16[384,512]{1,0:T(8,128)(2,1)}, bf16[384,512]{1,0:T(8,128)(2,1)S(1)}, u32[]{:S(2)}, u32[]{:S(2)}) collective-permute-start(bf16[384,512]{1,0:T(8,128)(2,1)} %get-tuple-element.32), channel_id=1, source_target_pairs={{0,8},{8,0},{1,9},{9,1},{2,10},{10,2},{3,11},{11,3},{4,12},{12,4},... | collective-permute-start | bytes 1179656 | tf_op jit(solution)/shard_map/ppermute | solution.py:568
  11.0 38.4 %copy-start.8 = (f32[4]{0:T(128)S(1)}, f32[4]{0:T(128)}, u32[]{:S(2)}) copy-start(f32[4]{0:T(128)} %screening.3) | copy-start | bytes 52
  13.0 36.4 %all-to-all-start = ((bf16[16,24,512]{2,1,0:T(8,128)(2,1)}), bf16[16,24,512]{2,1,0:T(8,128)(2,1)S(1)}, u32[]{:S(2)}, u32[]{:S(2)}) async-start(bf16[16,24,512]{2,1,0:T(8,128)(2,1)} %bitcast.5), calls=%async_computation | async-start | bytes 786432 | tf_op jit(solution)/shard_map/all_to_all | solution.py:594
  23.2 11.0 %collective-permute-start.1 = (f32[256,1,128]{2,1,0:T(1,128)S(1)}, f32[256,1,128]{2,1,0:T(1,128)S(1)}, u32[]{:S(2)}, u32[]{:S(2)}) collective-permute-start(f32[256,1,128]{2,1,0:T(1,128)S(1)} %get-tuple-element.36), channel_id=1, source_target_pairs={{0,8},{8,0},{16,24},{24,16},{32,40},{40,32},{48,56},{56,48},{64,72... | collective-permute-start | bytes 393224 | tf_op jit(solution)/shard_map/ppermute | solution.py:564
  23.3 13.1 %collective-permute-start.2 = (f32[256,1,128]{2,1,0:T(1,128)S(1)}, f32[256,1,128]{2,1,0:T(1,128)S(1)}, u32[]{:S(2)}, u32[]{:S(2)}) collective-permute-start(f32[256,1,128]{2,1,0:T(1,128)S(1)} %get-tuple-element.36), channel_id=1, source_target_pairs={{8,16},{16,8},{24,32},{32,24},{40,48},{48,40},{56,64},{64,56},{72,... | collective-permute-start | bytes 393224 | tf_op jit(solution)/shard_map/ppermute | solution.py:564
  27.5 8.9 %collective-permute-start.3 = (f32[256,1,128]{2,1,0:T(1,128)S(1)}, f32[256,1,128]{2,1,0:T(1,128)S(1)}, u32[]{:S(2)}, u32[]{:S(2)}) collective-permute-start(f32[256,1,128]{2,1,0:T(1,128)S(1)} %get-tuple-element.36), channel_id=1, source_target_pairs={{0,1},{1,0},{2,3},{3,2},{4,5},{5,4},{6,7},{7,6},{8,9},{9,8},{10,11... | collective-permute-start | bytes 393224 | tf_op jit(solution)/shard_map/ppermute | solution.py:564
  29.0 11.7 %collective-permute-start.4 = (f32[256,1,128]{2,1,0:T(1,128)S(1)}, f32[256,1,128]{2,1,0:T(1,128)S(1)}, u32[]{:S(2)}, u32[]{:S(2)}) collective-permute-start(f32[256,1,128]{2,1,0:T(1,128)S(1)} %get-tuple-element.36), channel_id=1, source_target_pairs={{1,2},{2,1},{3,4},{4,3},{5,6},{6,5},{9,10},{10,9},{11,12},{12,11},... | collective-permute-start | bytes 393224 | tf_op jit(solution)/shard_map/ppermute | solution.py:564
  50.8 12.6 %all-to-all-start.1 = ((f32[8,32,128]{2,1,0:T(8,128)}), f32[8,32,128]{2,1,0:T(8,128)S(1)}, u32[]{:S(2)}, u32[]{:S(2)}) async-start(f32[8,32,128]{2,1,0:T(8,128)} %get-tuple-element.44), calls=%async_computation.1 | async-start | bytes 262144 | tf_op jit(solution)/shard_map/all_to_all | solution.py:610
  63.3 23.9 %copy-start.5 = (f32[8,2048]{1,0:T(8,128)S(1)}, f32[8,2048]{1,0:T(8,128)}, u32[]{:S(2)}) copy-start(f32[8,2048]{1,0:T(8,128)} %get-tuple-element.55.hat) | copy-start | bytes 196612
  64.9 20.6 %all-to-all-start.2 = ((bf16[16,24,512]{2,1,0:T(8,128)(2,1)}), bf16[16,24,512]{2,1,0:T(8,128)(2,1)S(1)}, u32[]{:S(2)}, u32[]{:S(2)}) async-start(bf16[16,24,512]{2,1,0:T(8,128)(2,1)} %local_potential.1), calls=%async_computation.2 | async-start | bytes 786432 | tf_op jit(solution)/shard_map/all_to_all | solution.py:618
  85.5 1.8 %collective-permute-start.5 = (bf16[384,512]{1,0:T(8,128)(2,1)S(1)}, bf16[384,512]{1,0:T(8,128)(2,1)S(1)}, u32[]{:S(2)}, u32[]{:S(2)}) collective-permute-start(bf16[384,512]{1,0:T(8,128)(2,1)S(1)} %bitcast.8), channel_id=1, source_target_pairs={{0,8},{8,0},{1,9},{9,1},{2,10},{10,2},{3,11},{11,3},{4,12},{12,4},... | collective-permute-start | bytes 1179656 | tf_op jit(solution)/shard_map/ppermute | solution.py:568

commit v4 on v3

--- a/solution.py
+++ b/solution.py
@@ -50,7 +50,6 @@
 
 
 def structure_kernel(
-    meta,
     positions,
     plane_low,
     plane_height,
@@ -148,7 +147,7 @@
 
     lax.fori_loop(0, ATOMS // BLOCK, block, 0)
     keep.start()
-    core = meta[0]
+    core = lax.axis_index("core")
     for mine in (False, True):
         start = pl.multiple_of((core if mine else 1 - core) * USED, 16)
         sums = jnp.dot(
@@ -164,7 +163,7 @@
     keep.wait()
 
 
-def local_structure(meta, positions, low, frac, features):
+def local_structure(positions, low, frac, features):
     return pl.pallas_call(
         structure_kernel,
         out_shape=(
@@ -173,7 +172,7 @@
             jax.ShapeDtypeStruct((HALF, COLS), jnp.float32),
             jax.ShapeDtypeStruct((HALF, COLS), jnp.bfloat16),
         ),
-        in_specs=[smem, hbm, hbm, hbm, hbm],
+        in_specs=[hbm, hbm, hbm, hbm],
         out_specs=(hbm, vmem, vmem, vmem),
         scratch_shapes=[
             pltpu.VMEM((2 * USED, ATOMS), jnp.bfloat16),
@@ -188,7 +187,7 @@
         cost_estimate=cost(1_500_000_000, 8_000_000),
         compiler_params=params(60),
         name="local_structure",
-    )(meta, positions, low, frac, features)
+    )(positions, low, frac, features)
 
 
 def wave_square(half, chunk):
@@ -199,8 +198,8 @@
     return (n_square + a_square).astype(jnp.float32)
 
 
-def coefficient_kernel(meta, waves, filters, alpha, beta):
-    half, chunk = meta[0], meta[1]
+def coefficient_kernel(waves, filters, alpha, beta):
+    half, chunk = lax.axis_index("core"), lax.axis_index(SWAP)
     place = lax.broadcasted_iota(jnp.int32, (CHUNK, 512), 0)
     role = place & 3
     n = 6 * half + 1 + (place >> 2)
@@ -223,29 +222,29 @@
     beta[...] = both[CHUNK : 2 * CHUNK]
 
 
-def coefficients(meta, waves, filters):
+def coefficients(waves, filters):
     return pl.pallas_call(
         coefficient_kernel,
         out_shape=(jax.ShapeDtypeStruct((CHUNK, CHAN), jnp.float32),) * 2,
-        in_specs=[smem, vmem, vmem],
+        in_specs=[vmem, vmem],
         out_specs=(vmem, vmem),
         cost_estimate=cost(40_000_000, 300_000),
         compiler_params=params(),
         name="coefficients",
-    )(meta, waves, filters)
+    )(waves, filters)
 
 
 def spatial_wave(square, screen):
     return jnp.sqrt((two_pi * two_pi) * square + screen * screen)
 
 
-def source_kernel(meta, screening, parts, source, payload):
+def source_kernel(screening, parts, source, payload):
     total = parts[0].astype(jnp.float32)
     for at in range(1, CHUNKS):
         total = total + parts[at].astype(jnp.float32)
     total = total * float(ATOMS * XY_DEVICES) ** -0.5
     source[...] = total
-    square = wave_square(meta[0], meta[1])
+    square = wave_square(lax.axis_index("core"), lax.axis_index(SWAP))
     decay = [
         jnp.exp(-plane_gap * spatial_wave(square, screening[plane])) for plane in range(PLANES)
     ]
@@ -256,7 +255,7 @@
     downward = planes[PLANES - 1]
     for plane in reversed(range(PLANES - 1)):
         downward = decay[plane] * downward + planes[plane]
-    layer = meta[2]
+    layer = lax.axis_index(VERTICAL)
     which = lax.broadcasted_iota(jnp.int32, (8, CHAN), 0)
     screens = jnp.zeros((8, CHAN), jnp.float32)
     for plane in range(PLANES):
@@ -266,24 +265,24 @@
         payload[target, CHUNK:PAYLOAD, :] = screens
 
 
-def local_source(meta, screening, parts):
+def local_source(screening, parts):
     return pl.pallas_call(
         source_kernel,
         out_shape=(
             jax.ShapeDtypeStruct((CHUNK, COLS), jnp.float32),
             jax.ShapeDtypeStruct((LAYERS, PAYLOAD, CHAN), jnp.float32),
         ),
-        in_specs=[smem, smem, vmem],
+        in_specs=[smem, vmem],
         out_specs=(vmem, vmem),
         cost_estimate=cost(1_000_000, 600_000),
         compiler_params=params(),
         name="local_source",
-    )(meta, screening, parts)
-
-
-def potential_kernel(meta, screening, source, carried, alpha, beta, out):
-    square = wave_square(meta[0], meta[1])
-    layer = meta[2]
+    )(screening, parts)
+
+
+def potential_kernel(screening, source, carried, alpha, beta, out):
+    square = wave_square(lax.axis_index("core"), lax.axis_index(SWAP))
+    layer = lax.axis_index(VERTICAL)
     upward = jnp.zeros((CHUNK, CHAN), jnp.float32)
     downward = jnp.zeros((CHUNK, CHAN), jnp.float32)
     scales = []
@@ -318,16 +317,16 @@
         out[at] = full
 
 
-def local_potential(meta, screening, source, carried, alpha, beta):
+def local_potential(screening, source, carried, alpha, beta):
     return pl.pallas_call(
         potential_kernel,
         out_shape=jax.ShapeDtypeStruct((CHUNKS, CHUNK, COLS), jnp.bfloat16),
-        in_specs=[smem, smem, vmem, vmem, vmem, vmem],
+        in_specs=[smem, vmem, vmem, vmem, vmem],
         out_specs=vmem,
         cost_estimate=cost(1_000_000, 1_000_000),
         compiler_params=params(),
         name="local_potential",
-    )(meta, screening, source, carried, alpha, beta)
+    )(screening, source, carried, alpha, beta)
 
 
 def ghost_kernel(rows, features, sent, own, arrived):
@@ -346,15 +345,12 @@
 def ghost_rows(rows, features):
     return pl.pallas_call(
         ghost_kernel,
-        out_shape=(
-            jax.ShapeDtypeStruct((GHOST, 1, CHAN), jnp.float32),
-            jax.ShapeDtypeStruct((ATOMS, 1, CHAN), jnp.float32),
-        ),
+        out_shape=jax.ShapeDtypeStruct((GHOST, 1, CHAN), jnp.float32),
         in_specs=[smem, anywhere],
-        out_specs=(vmem, vmem),
-        scratch_shapes=[pltpu.SemaphoreType.DMA],
+        out_specs=vmem,
+        scratch_shapes=[pltpu.VMEM((ATOMS, 1, CHAN), jnp.float32), pltpu.SemaphoreType.DMA],
         cost_estimate=cost(1_000, 1_000_000),
-        compiler_params=params(),
+        compiler_params=params(56),
         name="ghost_rows",
     )(rows, features)
 
@@ -437,13 +433,13 @@
     ]
 
 
-def first_pairs(meta, neighbours, weight, w_short, features, sides, count):
-    def kernel(meta, index, weights, projection, own, a, b, c, d, table, out, *scratch):
+def first_pairs(neighbours, weight, w_short, features, sides, count):
+    def kernel(index, weights, projection, own, a, b, c, d, table, out, *scratch):
         slots = scratch[: NBR * GROUP]
         factors, columns, sums, short, arrived, stored, placed = scratch[NBR * GROUP :]
         loads = load_slots(index, weights, slots, factors, arrived, 0, count)
-        core = meta[0]
-        odd = meta[2] & 1
+        core = lax.axis_index("core")
+        odd = lax.axis_index(VERTICAL) & 1
         loads.append(pltpu.make_async_copy(own, table.at[pl.ds(0, ATOMS)], placed.at[0]))
         for at, (rows, slot) in enumerate(
             ((a, 1 - core), (b, core), (c, 3 - odd), (d, 2 + odd))
@@ -465,13 +461,13 @@
             jax.ShapeDtypeStruct((TABLE, 1, CHAN), jnp.float32),
             jax.ShapeDtypeStruct((ATOMS, CHAN), jnp.float32),
         ),
-        in_specs=[smem, anywhere, anywhere, vmem] + [anywhere] * 5,
+        in_specs=[anywhere, anywhere, vmem] + [anywhere] * 5,
         out_specs=(vmem, anywhere),
         scratch_shapes=pair_scratch(count) + [pltpu.SemaphoreType.DMA((5,))],
         cost_estimate=cost(count * 200_000, count * 57_000),
         compiler_params=params(),
         name="first_pairs",
-    )(meta, neighbours, weight, w_short, features, *sides)
+    )(neighbours, weight, w_short, features, *sides)
 
 
 def more_pairs(neighbours, weight, w_short, table, messages, first, count, name):
@@ -499,7 +495,7 @@
     )(neighbours, weight, w_short, table, messages)
 
 
-def project_kernel(meta, mine, theirs, phase_in, hat, short, out, phase, arrived):
+def project_kernel(mine, theirs, phase_in, hat, short, out, phase, arrived):
     at = pl.program_id(0)
     loads = [
         pltpu.make_async_copy(phase_in.at[:, pl.ds(i * BLOCK, BLOCK)], phase.at[i], arrived.at[i])
@@ -518,7 +514,7 @@
             load.wait()
 
     atoms = pl.ds(pl.multiple_of(at * BLOCK, BLOCK), BLOCK)
-    core = meta[0]
+    core = lax.axis_index("core")
     dims = (((0,), (0,)), ((), ()))
     near = pl.multiple_of(core * USED, 16)
     far = pl.multiple_of((1 - core) * USED, 16)
@@ -533,12 +529,12 @@
     out[...] = jnp.transpose(total) + short[atoms, :]
 
 
-def project(meta, mine, theirs, phase, hat, short):
+def project(mine, theirs, phase, hat, short):
     return pl.pallas_call(
         project_kernel,
         grid=(ATOMS // BLOCK,),
         out_shape=jax.ShapeDtypeStruct((ATOMS, CHAN), jnp.float32),
-        in_specs=[smem, vmem, vmem, hbm, vmem, vmem],
+        in_specs=[vmem, vmem, hbm, vmem, vmem],
         out_specs=pl.BlockSpec((BLOCK, CHAN), lambda i: (i, 0)),
         scratch_shapes=[
             pltpu.VMEM((ATOMS // BLOCK, 2 * USED, BLOCK), jnp.bfloat16),
@@ -547,7 +543,7 @@
         cost_estimate=cost(1_500_000_000, 6_000_000),
         compiler_params=params(50),
         name="project",
-    )(meta, mine, theirs, phase, hat, short)
+    )(mine, theirs, phase, hat, short)
 
 
 PIECES = (512, 512, 1024)
@@ -582,48 +578,47 @@
     w_short,
 ):
     tie = lax.optimization_barrier
-    meta = jnp.stack(
-        [lax.axis_index("core"), lax.axis_index(SWAP), lax.axis_index(VERTICAL)]
-    ).astype(jnp.int32)
-    phase, hat, own, other = local_structure(
-        meta, positions, plane_index.reshape(1, -1), plane_frac.reshape(1, -1), features
-    )
-    joined = (own + other_core(other).astype(jnp.float32)).astype(jnp.bfloat16)
-    joined = joined.reshape(CHUNKS, CHUNK, COLS)
-    joined, ghost_index = tie((joined, ghost_index))
-    parts = lax.all_to_all(joined, SWAP, 0, 0)
-
-    sent, own_rows = ghost_rows(ghost_index, features.reshape(ATOMS, 1, CHAN))
+    own_rows = features.reshape(ATOMS, 1, CHAN)
+    sent = ghost_rows(ghost_index, own_rows)
+    sent, positions = tie((sent, positions))
     sides = [
         swapped(sent, LATERAL, 0),
         swapped(sent, LATERAL, 1),
         swapped(sent, VERTICAL, 0),
         swapped(sent, VERTICAL, 1),
     ]
-    alpha, beta = coefficients(meta, wave_index, channel_filter)
+    phase, hat, own, other = local_structure(
+        positions, plane_index.reshape(1, -1), plane_frac.reshape(1, -1), features
+    )
+    own, other, *_ = tie((own, other, *sides))
+    joined = (own + other_core(other).astype(jnp.float32)).astype(jnp.bfloat16)
+    joined = joined.reshape(CHUNKS, CHUNK, COLS)
+    joined, waves, slots, weights = tie((joined, wave_index, neighbours, pair_weight))
+    parts = lax.all_to_all(joined, SWAP, 0, 0)
+    alpha, beta = coefficients(waves, channel_filter)
     first, second = PIECES[0], PIECES[0] + PIECES[1]
-    table, short = first_pairs(meta, neighbours, pair_weight, w_short, own_rows, sides, first)
+    table, short = first_pairs(slots, weights, w_short, own_rows, sides, first)
 
     parts, short, alpha, beta = tie((parts, short, alpha, beta))
-    source, payload = local_source(meta, screening, parts)
+    source, payload = local_source(screening, parts)
     payload, short = tie((payload, short))
     carried = lax.all_to_all(payload, VERTICAL, 0, 0)
     short = more_pairs(
-        neighbours, pair_weight, w_short, table, short, first, PIECES[1], "second_pairs"
+        slots, weights, w_short, table, short, first, PIECES[1], "second_pairs"
     )
 
     carried, short = tie((carried, short))
-    field = local_potential(meta, screening, source, carried, alpha, beta)
+    field = local_potential(screening, source, carried, alpha, beta)
     field, short = tie((field, short))
     mine = lax.all_to_all(field, SWAP, 0, 0)
     short = more_pairs(
-        neighbours, pair_weight, w_short, table, short, second, PIECES[2], "third_pairs"
+        slots, weights, w_short, table, short, second, PIECES[2], "third_pairs"
     )
 
     mine, short = tie((mine, short))
     mine = mine.reshape(HALF, COLS)
     theirs = other_core(mine)
-    return project(meta, mine, theirs, phase, hat, short)
+    return project(mine, theirs, phase, hat, short)
 
 
 def solution(mesh):

time: 94.6 us -> 92.5 us (0.978)
  local copies, waits for them, and re-layouts: 0.05 us -> 5.89 us
  waiting for transfers between devices: 10.2 us -> 5.84 us
  starting transfers between devices: 30.7 us -> 28.2 us
    ppermute x4, waiting for transfers between devices: 6.55 us -> 0.01 us  [swapped(): return lax.ppermute(value, axis, route)]
    unnamed x20 -> x28, local copies, waits for them, and re-layouts: 0.05 us -> 5.89 us
    all_to_all x1, starting transfers between devices: 9.2 us -> 4.1 us  [on_device(): parts = lax.all_to_all(joined, SWAP, 0, 0)]
    all_to_all x1, waiting for transfers between devices: 0.01 us -> 2.55 us  [on_device(): parts = lax.all_to_all(joined, SWAP, 0, 0)]
    pallas_call x1, Pallas kernels: 0.95 us -> 2.9 us  [ghost_rows(): pl.pallas_call(ghost_kernel, out_shape=jax.ShapeDtypeStruct((GHOST, 1, CH...]
    ppermute x4, starting transfers between devices: 10.1 us -> 11.6 us  [swapped(): return lax.ppermute(value, axis, route)]
    all_to_all x1, starting transfers between devices: 4.8 us -> 6.17 us  [on_device(): carried = lax.all_to_all(payload, VERTICAL, 0, 0)]
  transfers between devices with their start and end apart: 9 -> 9, of which waited for: 5 -> 3; matrix products, arithmetic and copies ran while one was open for 0% -> 0% of each run, Pallas kernels for 35% -> 42%
where the time goes in v4:
time: 92.5 us; the launch traced here: 90.9 us
  Pallas kernels  48.8 us (53%)
  starting transfers between devices  28.2 us (30%)
  local copies, waits for them, and re-layouts  5.89 us (6%)
  waiting for transfers between devices  5.84 us (6%)
  other arithmetic  2 us (2%)
    pallas_call x2, Pallas kernels, more_pairs(): pl.pallas_call(kernel, out_shape=jax.ShapeDtypeStruct((ATOMS, CHAN), jnp....  21.9 us
    ppermute x4, starting transfers between devices, swapped(): return lax.ppermute(value, axis, route)  11.6 us
    pallas_call x1, Pallas kernels, first_pairs(): pl.pallas_call(kernel, out_shape=(jax.ShapeDtypeStruct((TABLE, 1, CHAN),...  8.1 us
    pallas_call x1, Pallas kernels, local_structure(): pl.pallas_call(structure_kernel, out_shape=(jax.ShapeDtypeStruct((2 * USE...  7.52 us
    all_to_all x1, starting transfers between devices, on_device(): carried = lax.all_to_all(payload, VERTICAL, 0, 0)  6.17 us
    unnamed x28, local copies, waits for them, and re-layouts  5.89 us
    all_to_all x1, starting transfers between devices, on_device(): mine = lax.all_to_all(field, SWAP, 0, 0)  5.72 us
    pallas_call x1, Pallas kernels, project(): pl.pallas_call(project_kernel, grid=(ATOMS // BLOCK,), out_shape=jax.Shap...  5.28 us
  transfers between devices with their start and end apart: 9, of which 3 were waited for; matrix products, arithmetic and copies ran while one was open for 0% of the time, Pallas kernels for 42%

profile of v4, /device:TPU:4, one launch (start us, length us, event | category | flops | bytes accessed | tf_op | source)
XLA Modules:
  0.0 90.9 jit_solution(17679037206449874015)
XLA Ops:
  0.0 2.9 %ghost_rows.1 = f32[256,1,128]{2,1,0:T(1,128)} custom-call(s32[256]{0:T(256)} %rows.1, f32[2048,1,128]{2,1,0:T(1,128)} %bitcast.5), custom_call_target="tpu_custom_call" | custom-call | flops 1000 | bytes 1000000 | tf_op jit(solution)/shard_map/ghost_rows/pallas_call | solution.py:346
  2.9 4.9 %collective-permute-start.3 = (f32[256,1,128]{2,1,0:T(1,128)}, f32[256,1,128]{2,1,0:T(1,128)S(1)}, u32[]{:S(2)}, u32[]{:S(2)}) collective-permute-start(f32[256,1,128]{2,1,0:T(1,128)} %ghost_rows.1), channel_id=1, source_target_pairs={{1,2},{2,1},{3,4},{4,3},{5,6},{6,5},{9,10},{10,9},{11,12},{12,11},... | collective-permute-start | bytes 393224 | tf_op jit(solution)/shard_map/ppermute | solution.py:560
  7.8 0.3 collective-permute-start.2
  8.1 6.5 %collective-permute-start.1 = (f32[256,1,128]{2,1,0:T(1,128)}, f32[256,1,128]{2,1,0:T(1,128)S(1)}, u32[]{:S(2)}, u32[]{:S(2)}) collective-permute-start(f32[256,1,128]{2,1,0:T(1,128)} %ghost_rows.1), channel_id=1, source_target_pairs={{8,16},{16,8},{24,32},{32,24},{40,48},{48,40},{56,64},{64,56},{72,... | collective-permute-start | bytes 393224 | tf_op jit(solution)/shard_map/ppermute | solution.py:560
  14.5 0.0 collective-permute-start
  14.5 0.0 copy-start.4
  14.5 0.0 copy-start.12
  14.5 0.0 copy-start.1
  14.5 0.0 copy-start.2
  14.5 0.0 copy-start.3
  14.6 7.5 %local_structure.1 = (bf16[672,2048]{1,0:T(8,128)(2,1)}, f32[8,2048]{1,0:T(8,128)}, f32[384,512]{1,0:T(8,128)}, bf16[384,512]{1,0:T(8,128)(2,1)}) custom-call(f32[2,2048]{1,0:T(2,128)} %positions, s32[1,2048]{1,0:T(1,128)} %bitcast.9, f32[1,2048]{1,0:T(1,128)} %bitcast.10, f32[2048,128]{1,0:T(8,128)} %features.1), custom_call_target="tpu_custom_call" | custom-call | flops 1500000000 | bytes 8000000 | tf_op jit(solution)/shard_map/local_structure/pallas_call | solution.py:167
  22.1 0.0 copy-start.13
  22.1 0.0 collective-permute-done.3.d
  22.1 0.0 collective-permute-done.2.c
  22.1 0.0 copy-start.5
  22.1 0.6 copy-done.5
  22.8 0.0 collective-permute-done.1.b
  22.8 0.0 copy-start.7
  22.8 0.6 copy-done.7
  23.4 0.0 collective-permute-done.a
  23.4 0.0 copy-start.9
  23.4 0.6 copy-done.9
  24.1 0.5 collective-permute-start.4
  24.6 1.6 %collective-permute-done.4 = bf16[384,512]{1,0:T(8,128)(2,1)S(1)} collective-permute-done((bf16[384,512]{1,0:T(8,128)(2,1)}, bf16[384,512]{1,0:T(8,128)(2,1)S(1)}, u32[]{:S(2)}, u32[]{:S(2)}) %collective-permute-start.4) | collective-permute-done | bytes 393248 | tf_op jit(solution)/shard_map/ppermute | solution.py:564
  26.1 2.0 %add_convert_fusion = bf16[384,512]{1,0:T(8,128)(2,1)} fusion(f32[384,512]{1,0:T(8,128)} %get-tuple-element.39, bf16[384,512]{1,0:T(8,128)(2,1)S(1)} %collective-permute-done.4), kind=kLoop, calls=%fused_computation | loop fusion | flops 589824 | bytes 1572864 | tf_op jit(solution)/shard_map/convert_element_type | solution.py:594
  28.1 4.1 %all-to-all-start = ((bf16[16,24,512]{2,1,0:T(8,128)(2,1)}), bf16[16,24,512]{2,1,0:T(8,128)(2,1)S(1)}, u32[]{:S(2)}, u32[]{:S(2)}) async-start(bf16[16,24,512]{2,1,0:T(8,128)(2,1)} %bitcast.3), calls=%async_computation | async-start | bytes 786432 | tf_op jit(solution)/shard_map/all_to_all | solution.py:597
  32.2 0.0 copy-done.4
  32.2 0.0 copy-done.12
  32.3 0.3 coefficients.1
  32.5 0.0 copy-done.1
  32.5 0.0 copy-done.2
  32.5 0.0 copy-done.3
  32.6 0.0 copy-start
  32.6 1.2 %copy-done = f32[2048,128]{1,0:T(8,128)S(1)} copy-done((f32[2048,128]{1,0:T(8,128)S(1)}, f32[2048,128]{1,0:T(8,128)}, u32[]{:S(2)}) %copy-start) | copy-done | bytes 1048600
  33.8 0.0 copy-start.6
  33.8 0.9 copy-done.6
  34.7 0.0 copy-start.8
  34.7 0.9 copy-done.8
  35.6 0.0 copy-start.10
  35.6 0.9 copy-done.10
  36.5 8.1 %first_pairs.1 = (f32[3072,1,128]{2,1,0:T(1,128)S(1)}, f32[2048,128]{1,0:T(8,128)S(1)}) custom-call(s32[16,2048]{1,0:T(8,128)S(1)} %copy-done.1, f32[16,2048]{1,0:T(8,128)S(1)} %copy-done.2, f32[128,128]{1,0:T(8,128)S(1)} %copy-done.3, f32[2048,1,128]{2,1,0:T(1,128)S(1)} %bitcast.6, f32[256,1,128]{2,1,0:T(1,128)S(1)} %copy-done.10, ...), custom_call_target="tpu_custom_call" | custom-call | flops 102400000 | bytes 29184000 | tf_op jit(solution)/shard_map/first_pairs/pallas_call | solution.py:458
  44.6 2.6 %all-to-all-done.parts = bf16[16,24,512]{2,1,0:T(8,128)(2,1)S(1)} async-done(((bf16[16,24,512]{2,1,0:T(8,128)(2,1)}), bf16[16,24,512]{2,1,0:T(8,128)(2,1)S(1)}, u32[]{:S(2)}, u32[]{:S(2)}) %all-to-all-start) | async-done | bytes 393248 | tf_op jit(solution)/shard_map/all_to_all | solution.py:597
  47.2 0.0 copy-done.13
  47.2 1.3 %local_source.1 = (f32[24,512]{1,0:T(8,128)S(1)}, f32[8,32,128]{2,1,0:T(8,128)}) custom-call(f32[4]{0:T(128)S(1)} %copy-done.13, bf16[16,24,512]{2,1,0:T(8,128)(2,1)S(1)} %all-to-all-done.parts), custom_call_target="tpu_custom_call" | custom-call | flops 1000000 | bytes 600000 | tf_op jit(solution)/shard_map/local_source/pallas_call | solution.py:269
  48.5 6.2 %all-to-all-start.1 = ((f32[8,32,128]{2,1,0:T(8,128)}), f32[8,32,128]{2,1,0:T(8,128)S(1)}, u32[]{:S(2)}, u32[]{:S(2)}) async-start(f32[8,32,128]{2,1,0:T(8,128)} %get-tuple-element.52), calls=%async_computation.1 | async-start | bytes 262144 | tf_op jit(solution)/shard_map/all_to_all | solution.py:605
  54.6 7.7 %second_pairs.1.before = f32[2048,128]{1,0:T(8,128)S(1)} custom-call(s32[16,2048]{1,0:T(8,128)S(1)} %copy-done.1, f32[16,2048]{1,0:T(8,128)S(1)} %copy-done.2, f32[128,128]{1,0:T(8,128)S(1)} %copy-done.3, f32[3072,1,128]{2,1,0:T(1,128)S(1)} %get-tuple-element.53.rows, f32[2048,128]{1,0:T(8,128)S(1)} %get-tuple-element.54.before), custom_call_target="tpu_custom_call", output_to_operand_aliasing={{}: (4, {})} | custom-call | flops 102400000 | bytes 29184000 | tf_op jit(solution)/shard_map/second_pairs/pallas_call | solution.py:485
  62.4 0.0 copy-start.11
  62.4 0.0 all-to-all-done.1.carried
  62.4 1.5 %local_potential.1 = bf16[16,24,512]{2,1,0:T(8,128)(2,1)} custom-call(f32[4]{0:T(128)S(1)} %copy-done.13, f32[24,512]{1,0:T(8,128)S(1)} %get-tuple-element.49.source, f32[8,32,128]{2,1,0:T(8,128)S(1)} %all-to-all-done.1.carried, f32[24,128]{1,0:T(8,128)S(1)} %get-tuple-element.56.alpha, f32[24,128]{1,0:T(8,128)S(1)} %get-tuple-element.57.beta), custom_call_target="tpu_custom_call" | custom-call | flops 1000000 | bytes 1000000 | tf_op jit(solution)/shard_map/local_potential/pallas_call | solution.py:321
  63.9 5.7 %all-to-all-start.2 = ((bf16[16,24,512]{2,1,0:T(8,128)(2,1)}), bf16[16,24,512]{2,1,0:T(8,128)(2,1)S(1)}, u32[]{:S(2)}, u32[]{:S(2)}) async-start(bf16[16,24,512]{2,1,0:T(8,128)(2,1)} %local_potential.1), calls=%async_computation.2 | async-start | bytes 786432 | tf_op jit(solution)/shard_map/all_to_all | solution.py:613
  69.6 14.1 %third_pairs.1.short = f32[2048,128]{1,0:T(8,128)S(1)} custom-call(s32[16,2048]{1,0:T(8,128)S(1)} %copy-done.1, f32[16,2048]{1,0:T(8,128)S(1)} %copy-done.2, f32[128,128]{1,0:T(8,128)S(1)} %copy-done.3, f32[3072,1,128]{2,1,0:T(1,128)S(1)} %get-tuple-element.53.rows, f32[2048,128]{1,0:T(8,128)S(1)} %second_pairs.1.before), custom_call_target="tpu_custom_call", output_to_operand_aliasing={{}: (4, {})} | custom-call | flops 204800000 | bytes 58368000 | tf_op jit(solution)/shard_map/third_pairs/pallas_call | solution.py:485
  83.8 0.0 all-to-all-done.2
  83.8 0.1 collective-permute-start.5
  83.9 1.7 %collective-permute-done.5.theirs = bf16[384,512]{1,0:T(8,128)(2,1)S(1)} collective-permute-done((bf16[384,512]{1,0:T(8,128)(2,1)S(1)}, bf16[384,512]{1,0:T(8,128)(2,1)S(1)}, u32[]{:S(2)}, u32[]{:S(2)}) %collective-permute-start.5) | collective-permute-done | bytes 393248 | tf_op jit(solution)/shard_map/ppermute | solution.py:564
  85.6 0.0 copy-done.11
  85.6 5.3 %project.1 = f32[2048,128]{1,0:T(8,128)} custom-call(bf16[384,512]{1,0:T(8,128)(2,1)S(1)} %bitcast.8, bf16[384,512]{1,0:T(8,128)(2,1)S(1)} %collective-permute-done.5.theirs, bf16[672,2048]{1,0:T(8,128)(2,1)} %get-tuple-element.62.phase_in, f32[8,2048]{1,0:T(8,128)S(1)} %copy-done.11, f32[2048,128]{1,0:T(8,128)S(1)} %third_pairs.1.short), custom_call_target="tpu_custom_call" | custom-call | flops 1500000000 | bytes 6000000 | tf_op jit(solution)/shard_map/project/pallas_call | solution.py:533
Async XLA Ops:
  2.9 19.2 %collective-permute-start.3 = (f32[256,1,128]{2,1,0:T(1,128)}, f32[256,1,128]{2,1,0:T(1,128)S(1)}, u32[]{:S(2)}, u32[]{:S(2)}) collective-permute-start(f32[256,1,128]{2,1,0:T(1,128)} %ghost_rows.1), channel_id=1, source_target_pairs={{1,2},{2,1},{3,4},{4,3},{5,6},{6,5},{9,10},{10,9},{11,12},{12,11},... | collective-permute-start | bytes 393224 | tf_op jit(solution)/shard_map/ppermute | solution.py:560
  7.8 14.3 %collective-permute-start.2 = (f32[256,1,128]{2,1,0:T(1,128)}, f32[256,1,128]{2,1,0:T(1,128)S(1)}, u32[]{:S(2)}, u32[]{:S(2)}) collective-permute-start(f32[256,1,128]{2,1,0:T(1,128)} %ghost_rows.1), channel_id=1, source_target_pairs={{0,1},{1,0},{2,3},{3,2},{4,5},{5,4},{6,7},{7,6},{8,9},{9,8},{10,11... | collective-permute-start | bytes 393224 | tf_op jit(solution)/shard_map/ppermute | solution.py:560
  8.1 14.7 %collective-permute-start.1 = (f32[256,1,128]{2,1,0:T(1,128)}, f32[256,1,128]{2,1,0:T(1,128)S(1)}, u32[]{:S(2)}, u32[]{:S(2)}) collective-permute-start(f32[256,1,128]{2,1,0:T(1,128)} %ghost_rows.1), channel_id=1, source_target_pairs={{8,16},{16,8},{24,32},{32,24},{40,48},{48,40},{56,64},{64,56},{72,... | collective-permute-start | bytes 393224 | tf_op jit(solution)/shard_map/ppermute | solution.py:560
  14.5 8.9 %collective-permute-start = (f32[256,1,128]{2,1,0:T(1,128)}, f32[256,1,128]{2,1,0:T(1,128)S(1)}, u32[]{:S(2)}, u32[]{:S(2)}) collective-permute-start(f32[256,1,128]{2,1,0:T(1,128)} %ghost_rows.1), channel_id=1, source_target_pairs={{0,8},{8,0},{16,24},{24,16},{32,40},{40,32},{48,56},{56,48},{64,72... | collective-permute-start | bytes 393224 | tf_op jit(solution)/shard_map/ppermute | solution.py:560
  14.5 17.7 %copy-start.4 = (f32[512,128]{1,0:T(8,128)S(1)}, f32[512,128]{1,0:T(8,128)}, u32[]{:S(2)}) copy-start(f32[512,128]{1,0:T(8,128)} %filters.1) | copy-start | bytes 786436
  14.5 17.7 %copy-start.12 = (s32[2,512]{1,0:T(2,128)S(1)}, s32[2,512]{1,0:T(2,128)}, u32[]{:S(2)}) copy-start(s32[2,512]{1,0:T(2,128)} %waves) | copy-start | bytes 12292
  14.5 18.0 %copy-start.1 = (s32[16,2048]{1,0:T(8,128)S(1)}, s32[16,2048]{1,0:T(8,128)}, u32[]{:S(2)}) copy-start(s32[16,2048]{1,0:T(8,128)} %index.2) | copy-start | bytes 393220
  14.5 18.0 %copy-start.2 = (f32[16,2048]{1,0:T(8,128)S(1)}, f32[16,2048]{1,0:T(8,128)}, u32[]{:S(2)}) copy-start(f32[16,2048]{1,0:T(8,128)} %weights.2) | copy-start | bytes 393220
  14.5 18.0 %copy-start.3 = (f32[128,128]{1,0:T(8,128)S(1)}, f32[128,128]{1,0:T(8,128)}, u32[]{:S(2)}) copy-start(f32[128,128]{1,0:T(8,128)} %projection.5) | copy-start | bytes 196612
  22.1 25.1 %copy-start.13 = (f32[4]{0:T(128)S(1)}, f32[4]{0:T(128)}, u32[]{:S(2)}) copy-start(f32[4]{0:T(128)} %screening.3) | copy-start | bytes 52
  22.1 0.6 copy-start.5
  22.8 0.7 copy-start.7
  23.4 0.6 copy-start.9
  24.1 2.1 %collective-permute-start.4 = (bf16[384,512]{1,0:T(8,128)(2,1)}, bf16[384,512]{1,0:T(8,128)(2,1)S(1)}, u32[]{:S(2)}, u32[]{:S(2)}) collective-permute-start(bf16[384,512]{1,0:T(8,128)(2,1)} %get-tuple-element.40), channel_id=1, source_target_pairs={{0,8},{8,0},{1,9},{9,1},{2,10},{10,2},{3,11},{11,3},{4,12},{12,4},... | collective-permute-start | bytes 1179656 | tf_op jit(solution)/shard_map/ppermute | solution.py:564
  28.1 19.0 %all-to-all-start = ((bf16[16,24,512]{2,1,0:T(8,128)(2,1)}), bf16[16,24,512]{2,1,0:T(8,128)(2,1)S(1)}, u32[]{:S(2)}, u32[]{:S(2)}) async-start(bf16[16,24,512]{2,1,0:T(8,128)(2,1)} %bitcast.3), calls=%async_computation | async-start | bytes 786432 | tf_op jit(solution)/shard_map/all_to_all | solution.py:597
  32.6 1.2 %copy-start = (f32[2048,128]{1,0:T(8,128)S(1)}, f32[2048,128]{1,0:T(8,128)}, u32[]{:S(2)}) copy-start(f32[2048,128]{1,0:T(8,128)} %features.1) | copy-start | bytes 3145732
  33.8 0.9 copy-start.6
  34.7 0.9 copy-start.8
  35.6 0.9 copy-start.10
  48.5 13.9 %all-to-all-start.1 = ((f32[8,32,128]{2,1,0:T(8,128)}), f32[8,32,128]{2,1,0:T(8,128)S(1)}, u32[]{:S(2)}, u32[]{:S(2)}) async-start(f32[8,32,128]{2,1,0:T(8,128)} %get-tuple-element.52), calls=%async_computation.1 | async-start | bytes 262144 | tf_op jit(solution)/shard_map/all_to_all | solution.py:605
  62.4 23.2 %copy-start.11 = (f32[8,2048]{1,0:T(8,128)S(1)}, f32[8,2048]{1,0:T(8,128)}, u32[]{:S(2)}) copy-start(f32[8,2048]{1,0:T(8,128)} %get-tuple-element.63.hat) | copy-start | bytes 196612
  63.9 19.9 %all-to-all-start.2 = ((bf16[16,24,512]{2,1,0:T(8,128)(2,1)}), bf16[16,24,512]{2,1,0:T(8,128)(2,1)S(1)}, u32[]{:S(2)}, u32[]{:S(2)}) async-start(bf16[16,24,512]{2,1,0:T(8,128)(2,1)} %local_potential.1), calls=%async_computation.2 | async-start | bytes 786432 | tf_op jit(solution)/shard_map/all_to_all | solution.py:613
  83.8 1.8 %collective-permute-start.5 = (bf16[384,512]{1,0:T(8,128)(2,1)S(1)}, bf16[384,512]{1,0:T(8,128)(2,1)S(1)}, u32[]{:S(2)}, u32[]{:S(2)}) collective-permute-start(bf16[384,512]{1,0:T(8,128)(2,1)S(1)} %bitcast.7), channel_id=1, source_target_pairs={{0,8},{8,0},{1,9},{9,1},{2,10},{10,2},{3,11},{11,3},{4,12},{12,4},... | collective-permute-start | bytes 1179656 | tf_op jit(solution)/shard_map/ppermute | solution.py:564

commit v5 on v4

--- a/solution.py
+++ b/solution.py
@@ -433,45 +433,35 @@
     ]
 
 
-def first_pairs(neighbours, weight, w_short, features, sides, count):
-    def kernel(index, weights, projection, own, a, b, c, d, table, out, *scratch):
-        slots = scratch[: NBR * GROUP]
-        factors, columns, sums, short, arrived, stored, placed = scratch[NBR * GROUP :]
-        loads = load_slots(index, weights, slots, factors, arrived, 0, count)
-        core = lax.axis_index("core")
-        odd = lax.axis_index(VERTICAL) & 1
-        loads.append(pltpu.make_async_copy(own, table.at[pl.ds(0, ATOMS)], placed.at[0]))
-        for at, (rows, slot) in enumerate(
-            ((a, 1 - core), (b, core), (c, 3 - odd), (d, 2 + odd))
-        ):
-            start = ATOMS + slot * GHOST
-            loads.append(
-                pltpu.make_async_copy(rows, table.at[pl.ds(start, GHOST)], placed.at[1 + at])
-            )
-        for load in loads:
-            load.start()
-        for load in loads:
-            load.wait()
-        weighted_rows(slots, factors, columns, table, sums, count)
-        store_messages(sums, projection, short, out, stored, 0, count)
-
-    return pl.pallas_call(
-        kernel,
-        out_shape=(
-            jax.ShapeDtypeStruct((TABLE, 1, CHAN), jnp.float32),
-            jax.ShapeDtypeStruct((ATOMS, CHAN), jnp.float32),
-        ),
-        in_specs=[anywhere, anywhere, vmem] + [anywhere] * 5,
-        out_specs=(vmem, anywhere),
-        scratch_shapes=pair_scratch(count) + [pltpu.SemaphoreType.DMA((5,))],
-        cost_estimate=cost(count * 200_000, count * 57_000),
+def table_kernel(own, a, b, c, d, table, placed):
+    core = lax.axis_index("core")
+    odd = lax.axis_index(VERTICAL) & 1
+    copies = [pltpu.make_async_copy(own, table.at[pl.ds(0, ATOMS)], placed.at[0])]
+    for at, (rows, slot) in enumerate(((a, 1 - core), (b, core), (c, 3 - odd), (d, 2 + odd))):
+        start = ATOMS + slot * GHOST
+        copies.append(pltpu.make_async_copy(rows, table.at[pl.ds(start, GHOST)], placed.at[1 + at]))
+    for copy in copies:
+        copy.start()
+    for copy in copies:
+        copy.wait()
+
+
+def lookup_table(features, sides):
+    return pl.pallas_call(
+        table_kernel,
+        out_shape=jax.ShapeDtypeStruct((TABLE, 1, CHAN), jnp.float32),
+        in_specs=[anywhere] * 5,
+        out_specs=vmem,
+        scratch_shapes=[pltpu.SemaphoreType.DMA((5,))],
+        cost_estimate=cost(1_000, 3_000_000),
         compiler_params=params(),
-        name="first_pairs",
-    )(neighbours, weight, w_short, features, *sides)
-
-
-def more_pairs(neighbours, weight, w_short, table, messages, first, count, name):
-    def kernel(index, weights, projection, rows, before, out, *scratch):
+        name="lookup_table",
+    )(features, *sides)
+
+
+def pair_messages(neighbours, weight, w_short, table, messages, first, count, name):
+    def kernel(index, weights, projection, rows, *rest):
+        out, *scratch = rest if messages is None else rest[1:]
         slots = scratch[: NBR * GROUP]
         factors, columns, sums, short, arrived, stored = scratch[NBR * GROUP :]
         loads = load_slots(index, weights, slots, factors, arrived, first, count)
@@ -482,17 +472,18 @@
         weighted_rows(slots, factors, columns, rows, sums, count)
         store_messages(sums, projection, short, out, stored, first, count)
 
+    earlier = [] if messages is None else [messages]
     return pl.pallas_call(
         kernel,
         out_shape=jax.ShapeDtypeStruct((ATOMS, CHAN), jnp.float32),
-        in_specs=[anywhere, anywhere, vmem, vmem, anywhere],
+        in_specs=[anywhere, anywhere, vmem, vmem] + [anywhere] * len(earlier),
         out_specs=anywhere,
-        input_output_aliases={4: 0},
+        input_output_aliases={4: 0} if earlier else {},
         scratch_shapes=pair_scratch(count),
         cost_estimate=cost(count * 200_000, count * 57_000),
         compiler_params=params(),
         name=name,
-    )(neighbours, weight, w_short, table, messages)
+    )(neighbours, weight, w_short, table, *earlier)
 
 
 def project_kernel(mine, theirs, phase_in, hat, short, out, phase, arrived):
@@ -590,20 +581,22 @@
     phase, hat, own, other = local_structure(
         positions, plane_index.reshape(1, -1), plane_frac.reshape(1, -1), features
     )
-    own, other, *_ = tie((own, other, *sides))
+    own, other, *sides = tie((own, other, *sides))
+    table = lookup_table(own_rows, sides)
+    own, other, table = tie((own, other, table))
     joined = (own + other_core(other).astype(jnp.float32)).astype(jnp.bfloat16)
     joined = joined.reshape(CHUNKS, CHUNK, COLS)
     joined, waves, slots, weights = tie((joined, wave_index, neighbours, pair_weight))
     parts = lax.all_to_all(joined, SWAP, 0, 0)
     alpha, beta = coefficients(waves, channel_filter)
     first, second = PIECES[0], PIECES[0] + PIECES[1]
-    table, short = first_pairs(slots, weights, w_short, own_rows, sides, first)
+    short = pair_messages(slots, weights, w_short, table, None, 0, first, "first_pairs")
 
     parts, short, alpha, beta = tie((parts, short, alpha, beta))
     source, payload = local_source(screening, parts)
     payload, short = tie((payload, short))
     carried = lax.all_to_all(payload, VERTICAL, 0, 0)
-    short = more_pairs(
+    short = pair_messages(
         slots, weights, w_short, table, short, first, PIECES[1], "second_pairs"
     )
 
@@ -611,7 +604,7 @@
     field = local_potential(screening, source, carried, alpha, beta)
     field, short = tie((field, short))
     mine = lax.all_to_all(field, SWAP, 0, 0)
-    short = more_pairs(
+    short = pair_messages(
         slots, weights, w_short, table, short, second, PIECES[2], "third_pairs"
     )
 

time: 92.5 us -> 87.9 us (0.950)
  local copies, waits for them, and re-layouts: 5.89 us -> 1.04 us
  waiting for transfers between devices: 5.84 us -> 8.99 us
  starting transfers between devices: 28.2 us -> 26.1 us
  other arithmetic: 2 us -> 0.87 us
    unnamed x28 -> x20, local copies, waits for them, and re-layouts: 5.89 us -> 1.04 us
    all_to_all x1, waiting for transfers between devices: 2.55 us -> 5.91 us  [on_device(): parts = lax.all_to_all(joined, SWAP, 0, 0)]
    all_to_all x1, starting transfers between devices: 5.72 us -> 3.55 us  [on_device(): mine = lax.all_to_all(field, SWAP, 0, 0)]
    convert_element_type x1, other arithmetic: 2 us -> 0.87 us  [on_device(): joined = (own + other_core(other).astype(jnp.float32)).astype(jnp.bfloat16)]
    pallas_call x3 -> x4, Pallas kernels: 30 us -> 30.4 us  [the longest x3 29.6 us: pair_messages(): pl.pallas_call(kernel, out_shape=jax.ShapeDtypeStruct((ATOMS, CHAN), jnp....]
  transfers between devices with their start and end apart: 9 -> 9, of which waited for: 3 -> 3; matrix products, arithmetic and copies ran while one was open for 0% -> 0% of each run, Pallas kernels for 42% -> 43%
where the time goes in v5:
time: 87.9 us; the launch traced here: 86.5 us
  Pallas kernels  49.3 us (56%)
  starting transfers between devices  26.1 us (30%)
  waiting for transfers between devices  8.99 us (10%)
  local copies, waits for them, and re-layouts  1.04 us (1%)
    pallas_call x3, Pallas kernels, pair_messages(): pl.pallas_call(kernel, out_shape=jax.ShapeDtypeStruct((ATOMS, CHAN), jnp....  29.6 us
    ppermute x4, starting transfers between devices, swapped(): return lax.ppermute(value, axis, route)  11.6 us
    pallas_call x1, Pallas kernels, local_structure(): pl.pallas_call(structure_kernel, out_shape=(jax.ShapeDtypeStruct((2 * USE...  7.56 us
    all_to_all x1, starting transfers between devices, on_device(): carried = lax.all_to_all(payload, VERTICAL, 0, 0)  6.17 us
    all_to_all x1, waiting for transfers between devices, on_device(): parts = lax.all_to_all(joined, SWAP, 0, 0)  5.91 us
    pallas_call x1, Pallas kernels, project(): pl.pallas_call(project_kernel, grid=(ATOMS // BLOCK,), out_shape=jax.Shap...  5.25 us
    all_to_all x1, starting transfers between devices, on_device(): parts = lax.all_to_all(joined, SWAP, 0, 0)  4.1 us
    all_to_all x1, starting transfers between devices, on_device(): mine = lax.all_to_all(field, SWAP, 0, 0)  3.55 us
  transfers between devices with their start and end apart: 9, of which 3 were waited for; matrix products, arithmetic and copies ran while one was open for 0% of the time, Pallas kernels for 43%

profile of v5, /device:TPU:4, one launch (start us, length us, event | category | flops | bytes accessed | tf_op | source)
XLA Modules:
  0.0 86.5 jit_solution(825894203959721649)
XLA Ops:
  0.0 2.9 %ghost_rows.1 = f32[256,1,128]{2,1,0:T(1,128)} custom-call(s32[256]{0:T(256)} %rows.1, f32[2048,1,128]{2,1,0:T(1,128)} %bitcast.5), custom_call_target="tpu_custom_call" | custom-call | flops 1000 | bytes 1000000 | tf_op jit(solution)/shard_map/ghost_rows/pallas_call | solution.py:346
  2.9 4.9 %collective-permute-start.3 = (f32[256,1,128]{2,1,0:T(1,128)}, f32[256,1,128]{2,1,0:T(1,128)S(1)}, u32[]{:S(2)}, u32[]{:S(2)}) collective-permute-start(f32[256,1,128]{2,1,0:T(1,128)} %ghost_rows.1), channel_id=1, source_target_pairs={{1,2},{2,1},{3,4},{4,3},{5,6},{6,5},{9,10},{10,9},{11,12},{12,11},... | collective-permute-start | bytes 393224 | tf_op jit(solution)/shard_map/ppermute | solution.py:551
  7.8 0.3 collective-permute-start.2
  8.1 6.5 %collective-permute-start.1 = (f32[256,1,128]{2,1,0:T(1,128)}, f32[256,1,128]{2,1,0:T(1,128)S(1)}, u32[]{:S(2)}, u32[]{:S(2)}) collective-permute-start(f32[256,1,128]{2,1,0:T(1,128)} %ghost_rows.1), channel_id=1, source_target_pairs={{8,16},{16,8},{24,32},{32,24},{40,48},{48,40},{56,64},{64,56},{72,... | collective-permute-start | bytes 393224 | tf_op jit(solution)/shard_map/ppermute | solution.py:551
  14.5 0.0 collective-permute-start
  14.5 0.0 copy-start
  14.5 7.6 %local_structure.1 = (bf16[672,2048]{1,0:T(8,128)(2,1)}, f32[8,2048]{1,0:T(8,128)}, f32[384,512]{1,0:T(8,128)}, bf16[384,512]{1,0:T(8,128)(2,1)}) custom-call(f32[2,2048]{1,0:T(2,128)} %positions, s32[1,2048]{1,0:T(1,128)} %bitcast.9, f32[1,2048]{1,0:T(1,128)} %bitcast.10, f32[2048,128]{1,0:T(8,128)} %features.1), custom_call_target="tpu_custom_call" | custom-call | flops 1500000000 | bytes 8000000 | tf_op jit(solution)/shard_map/local_structure/pallas_call | solution.py:167
  22.1 0.0 copy-start.9
  22.1 0.0 copy-start.8
  22.1 0.0 collective-permute-done.3.d
  22.1 0.0 collective-permute-done.2.c
  22.1 0.0 collective-permute-done.1.b
  22.2 0.0 collective-permute-done.a
  22.2 0.0 copy-done
  22.2 0.0 copy-start.6
  22.2 0.0 copy-start.1
  22.2 0.0 copy-start.2
  22.2 0.0 copy-start.3
  22.2 0.8 lookup_table.1.rows
  23.1 0.0 copy-done.9
  23.1 0.0 copy-start.7
  23.1 0.6 collective-permute-start.4
  23.7 1.3 %collective-permute-done.4 = bf16[384,512]{1,0:T(8,128)(2,1)S(1)} collective-permute-done((bf16[384,512]{1,0:T(8,128)(2,1)S(1)}, bf16[384,512]{1,0:T(8,128)(2,1)S(1)}, u32[]{:S(2)}, u32[]{:S(2)}) %collective-permute-start.4) | collective-permute-done | bytes 393248 | tf_op jit(solution)/shard_map/ppermute | solution.py:555
  25.0 0.0 copy-done.8
  25.0 0.9 %add_convert_fusion = bf16[384,512]{1,0:T(8,128)(2,1)} fusion(f32[384,512]{1,0:T(8,128)S(1)} %copy-done.8, bf16[384,512]{1,0:T(8,128)(2,1)S(1)} %collective-permute-done.4), kind=kLoop, calls=%fused_computation | loop fusion | flops 589824 | bytes 1572864 | tf_op jit(solution)/shard_map/convert_element_type | solution.py:587
  25.9 4.1 %all-to-all-start = ((bf16[16,24,512]{2,1,0:T(8,128)(2,1)}), bf16[16,24,512]{2,1,0:T(8,128)(2,1)S(1)}, u32[]{:S(2)}, u32[]{:S(2)}) async-start(bf16[16,24,512]{2,1,0:T(8,128)(2,1)} %bitcast.3), calls=%async_computation | async-start | bytes 786432 | tf_op jit(solution)/shard_map/all_to_all | solution.py:590
  30.0 0.0 copy-done.6
  30.0 0.0 copy-start.4
  30.0 0.9 %copy-done.4 = f32[512,128]{1,0:T(8,128)S(1)} copy-done((f32[512,128]{1,0:T(8,128)S(1)}, f32[512,128]{1,0:T(8,128)}, u32[]{:S(2)}) %copy-start.4) | copy-done | bytes 262168
  31.0 0.3 coefficients.1
  31.2 0.0 copy-done.1
  31.2 0.0 copy-done.2
  31.2 0.0 copy-done.3
  31.3 7.7 %first_pairs.1.rest_0_ = f32[2048,128]{1,0:T(8,128)S(1)} custom-call(s32[16,2048]{1,0:T(8,128)S(1)} %copy-done.1, f32[16,2048]{1,0:T(8,128)S(1)} %copy-done.2, f32[128,128]{1,0:T(8,128)S(1)} %copy-done.3, f32[3072,1,128]{2,1,0:T(1,128)S(1)} %lookup_table.1.rows), custom_call_target="tpu_custom_call" | custom-call | flops 102400000 | bytes 29184000 | tf_op jit(solution)/shard_map/first_pairs/pallas_call | solution.py:476
  39.0 5.9 %all-to-all-done.parts = bf16[16,24,512]{2,1,0:T(8,128)(2,1)S(1)} async-done(((bf16[16,24,512]{2,1,0:T(8,128)(2,1)}), bf16[16,24,512]{2,1,0:T(8,128)(2,1)S(1)}, u32[]{:S(2)}, u32[]{:S(2)}) %all-to-all-start) | async-done | bytes 393248 | tf_op jit(solution)/shard_map/all_to_all | solution.py:590
  44.9 0.0 copy-done.7
  44.9 1.3 %local_source.1 = (f32[24,512]{1,0:T(8,128)S(1)}, f32[8,32,128]{2,1,0:T(8,128)}) custom-call(f32[4]{0:T(128)S(1)} %copy-done.7, bf16[16,24,512]{2,1,0:T(8,128)(2,1)S(1)} %all-to-all-done.parts), custom_call_target="tpu_custom_call" | custom-call | flops 1000000 | bytes 600000 | tf_op jit(solution)/shard_map/local_source/pallas_call | solution.py:269
  46.2 6.2 %all-to-all-start.1 = ((f32[8,32,128]{2,1,0:T(8,128)}), f32[8,32,128]{2,1,0:T(8,128)S(1)}, u32[]{:S(2)}, u32[]{:S(2)}) async-start(f32[8,32,128]{2,1,0:T(8,128)} %get-tuple-element.63), calls=%async_computation.1 | async-start | bytes 262144 | tf_op jit(solution)/shard_map/all_to_all | solution.py:598
  52.4 7.7 %second_pairs.1.rest_0_ = f32[2048,128]{1,0:T(8,128)S(1)} custom-call(s32[16,2048]{1,0:T(8,128)S(1)} %copy-done.1, f32[16,2048]{1,0:T(8,128)S(1)} %copy-done.2, f32[128,128]{1,0:T(8,128)S(1)} %copy-done.3, f32[3072,1,128]{2,1,0:T(1,128)S(1)} %lookup_table.1.rows, f32[2048,128]{1,0:T(8,128)S(1)} %first_pairs.1.rest_0_), custom_call_target="tpu_custom_call", output_to_operand_aliasing={{}: (4, {})} | custom-call | flops 102400000 | bytes 29184000 | tf_op jit(solution)/shard_map/second_pairs/pallas_call | solution.py:476
  60.1 0.0 copy-start.5
  60.1 0.0 all-to-all-done.1.carried
  60.2 1.5 %local_potential.1 = bf16[16,24,512]{2,1,0:T(8,128)(2,1)} custom-call(f32[4]{0:T(128)S(1)} %copy-done.7, f32[24,512]{1,0:T(8,128)S(1)} %get-tuple-element.60.source, f32[8,32,128]{2,1,0:T(8,128)S(1)} %all-to-all-done.1.carried, f32[24,128]{1,0:T(8,128)S(1)} %get-tuple-element.66.alpha, f32[24,128]{1,0:T(8,128)S(1)} %get-tuple-element.67.beta), custom_call_target="tpu_custom_call" | custom-call | flops 1000000 | bytes 1000000 | tf_op jit(solution)/shard_map/local_potential/pallas_call | solution.py:321
  61.7 3.6 %all-to-all-start.2 = ((bf16[16,24,512]{2,1,0:T(8,128)(2,1)}), bf16[16,24,512]{2,1,0:T(8,128)(2,1)S(1)}, u32[]{:S(2)}, u32[]{:S(2)}) async-start(bf16[16,24,512]{2,1,0:T(8,128)(2,1)} %local_potential.1), calls=%async_computation.2 | async-start | bytes 786432 | tf_op jit(solution)/shard_map/all_to_all | solution.py:606
  65.2 14.1 %third_pairs.1.short = f32[2048,128]{1,0:T(8,128)S(1)} custom-call(s32[16,2048]{1,0:T(8,128)S(1)} %copy-done.1, f32[16,2048]{1,0:T(8,128)S(1)} %copy-done.2, f32[128,128]{1,0:T(8,128)S(1)} %copy-done.3, f32[3072,1,128]{2,1,0:T(1,128)S(1)} %lookup_table.1.rows, f32[2048,128]{1,0:T(8,128)S(1)} %second_pairs.1.rest_0_), custom_call_target="tpu_custom_call", output_to_operand_aliasing={{}: (4, {})} | custom-call | flops 204800000 | bytes 58368000 | tf_op jit(solution)/shard_map/third_pairs/pallas_call | solution.py:476
  79.4 0.0 all-to-all-done.2
  79.4 0.1 collective-permute-start.5
  79.5 1.7 %collective-permute-done.5.theirs = bf16[384,512]{1,0:T(8,128)(2,1)S(1)} collective-permute-done((bf16[384,512]{1,0:T(8,128)(2,1)S(1)}, bf16[384,512]{1,0:T(8,128)(2,1)S(1)}, u32[]{:S(2)}, u32[]{:S(2)}) %collective-permute-start.5) | collective-permute-done | bytes 393248 | tf_op jit(solution)/shard_map/ppermute | solution.py:555
  81.2 0.0 copy-done.5
  81.2 5.3 %project.1 = f32[2048,128]{1,0:T(8,128)} custom-call(bf16[384,512]{1,0:T(8,128)(2,1)S(1)} %bitcast.8, bf16[384,512]{1,0:T(8,128)(2,1)S(1)} %collective-permute-done.5.theirs, bf16[672,2048]{1,0:T(8,128)(2,1)} %get-tuple-element.72.phase_in, f32[8,2048]{1,0:T(8,128)S(1)} %copy-done.5, f32[2048,128]{1,0:T(8,128)S(1)} %third_pairs.1.short), custom_call_target="tpu_custom_call" | custom-call | flops 1500000000 | bytes 6000000 | tf_op jit(solution)/shard_map/project/pallas_call | solution.py:524
Async XLA Ops:
  2.9 19.2 %collective-permute-start.3 = (f32[256,1,128]{2,1,0:T(1,128)}, f32[256,1,128]{2,1,0:T(1,128)S(1)}, u32[]{:S(2)}, u32[]{:S(2)}) collective-permute-start(f32[256,1,128]{2,1,0:T(1,128)} %ghost_rows.1), channel_id=1, source_target_pairs={{1,2},{2,1},{3,4},{4,3},{5,6},{6,5},{9,10},{10,9},{11,12},{12,11},... | collective-permute-start | bytes 393224 | tf_op jit(solution)/shard_map/ppermute | solution.py:551
  7.8 14.3 %collective-permute-start.2 = (f32[256,1,128]{2,1,0:T(1,128)}, f32[256,1,128]{2,1,0:T(1,128)S(1)}, u32[]{:S(2)}, u32[]{:S(2)}) collective-permute-start(f32[256,1,128]{2,1,0:T(1,128)} %ghost_rows.1), channel_id=1, source_target_pairs={{0,1},{1,0},{2,3},{3,2},{4,5},{5,4},{6,7},{7,6},{8,9},{9,8},{10,11... | collective-permute-start | bytes 393224 | tf_op jit(solution)/shard_map/ppermute | solution.py:551
  8.1 14.1 %collective-permute-start.1 = (f32[256,1,128]{2,1,0:T(1,128)}, f32[256,1,128]{2,1,0:T(1,128)S(1)}, u32[]{:S(2)}, u32[]{:S(2)}) collective-permute-start(f32[256,1,128]{2,1,0:T(1,128)} %ghost_rows.1), channel_id=1, source_target_pairs={{8,16},{16,8},{24,32},{32,24},{40,48},{48,40},{56,64},{64,56},{72,... | collective-permute-start | bytes 393224 | tf_op jit(solution)/shard_map/ppermute | solution.py:551
  14.5 7.6 %collective-permute-start = (f32[256,1,128]{2,1,0:T(1,128)}, f32[256,1,128]{2,1,0:T(1,128)S(1)}, u32[]{:S(2)}, u32[]{:S(2)}) collective-permute-start(f32[256,1,128]{2,1,0:T(1,128)} %ghost_rows.1), channel_id=1, source_target_pairs={{0,8},{8,0},{16,24},{24,16},{32,40},{40,32},{48,56},{56,48},{64,72... | collective-permute-start | bytes 393224 | tf_op jit(solution)/shard_map/ppermute | solution.py:551
  14.5 7.6 %copy-start = (f32[2048,128]{1,0:T(8,128)S(1)}, f32[2048,128]{1,0:T(8,128)}, u32[]{:S(2)}) copy-start(f32[2048,128]{1,0:T(8,128)} %features.1) | copy-start | bytes 3145732
  22.1 1.0 %copy-start.9 = (bf16[384,512]{1,0:T(8,128)(2,1)S(1)}, bf16[384,512]{1,0:T(8,128)(2,1)}, u32[]{:S(2)}) copy-start(bf16[384,512]{1,0:T(8,128)(2,1)} %get-tuple-element.51) | copy-start | bytes 1179652
  22.1 2.9 %copy-start.8 = (f32[384,512]{1,0:T(8,128)S(1)}, f32[384,512]{1,0:T(8,128)}, u32[]{:S(2)}) copy-start(f32[384,512]{1,0:T(8,128)} %get-tuple-element.50) | copy-start | bytes 2359300
  22.2 7.8 %copy-start.6 = (s32[2,512]{1,0:T(2,128)S(1)}, s32[2,512]{1,0:T(2,128)}, u32[]{:S(2)}) copy-start(s32[2,512]{1,0:T(2,128)} %waves) | copy-start | bytes 12292
  22.2 9.0 %copy-start.1 = (s32[16,2048]{1,0:T(8,128)S(1)}, s32[16,2048]{1,0:T(8,128)}, u32[]{:S(2)}) copy-start(s32[16,2048]{1,0:T(8,128)} %index.2) | copy-start | bytes 393220
  22.2 9.0 %copy-start.2 = (f32[16,2048]{1,0:T(8,128)S(1)}, f32[16,2048]{1,0:T(8,128)}, u32[]{:S(2)}) copy-start(f32[16,2048]{1,0:T(8,128)} %weights.2) | copy-start | bytes 393220
  22.2 9.0 %copy-start.3 = (f32[128,128]{1,0:T(8,128)S(1)}, f32[128,128]{1,0:T(8,128)}, u32[]{:S(2)}) copy-start(f32[128,128]{1,0:T(8,128)} %projection.5) | copy-start | bytes 196612
  23.1 21.8 %copy-start.7 = (f32[4]{0:T(128)S(1)}, f32[4]{0:T(128)}, u32[]{:S(2)}) copy-start(f32[4]{0:T(128)} %screening.3) | copy-start | bytes 52
  23.1 1.9 %collective-permute-start.4 = (bf16[384,512]{1,0:T(8,128)(2,1)S(1)}, bf16[384,512]{1,0:T(8,128)(2,1)S(1)}, u32[]{:S(2)}, u32[]{:S(2)}) collective-permute-start(bf16[384,512]{1,0:T(8,128)(2,1)S(1)} %copy-done.9), channel_id=1, source_target_pairs={{0,8},{8,0},{1,9},{9,1},{2,10},{10,2},{3,11},{11,3},{4,12},{12,4},... | collective-permute-start | bytes 1179656 | tf_op jit(solution)/shard_map/ppermute | solution.py:555
  25.9 19.0 %all-to-all-start = ((bf16[16,24,512]{2,1,0:T(8,128)(2,1)}), bf16[16,24,512]{2,1,0:T(8,128)(2,1)S(1)}, u32[]{:S(2)}, u32[]{:S(2)}) async-start(bf16[16,24,512]{2,1,0:T(8,128)(2,1)} %bitcast.3), calls=%async_computation | async-start | bytes 786432 | tf_op jit(solution)/shard_map/all_to_all | solution.py:590
  30.0 1.0 %copy-start.4 = (f32[512,128]{1,0:T(8,128)S(1)}, f32[512,128]{1,0:T(8,128)}, u32[]{:S(2)}) copy-start(f32[512,128]{1,0:T(8,128)} %filters.1) | copy-start | bytes 786436
  46.2 13.9 %all-to-all-start.1 = ((f32[8,32,128]{2,1,0:T(8,128)}), f32[8,32,128]{2,1,0:T(8,128)S(1)}, u32[]{:S(2)}, u32[]{:S(2)}) async-start(f32[8,32,128]{2,1,0:T(8,128)} %get-tuple-element.63), calls=%async_computation.1 | async-start | bytes 262144 | tf_op jit(solution)/shard_map/all_to_all | solution.py:598
  60.1 21.1 %copy-start.5 = (f32[8,2048]{1,0:T(8,128)S(1)}, f32[8,2048]{1,0:T(8,128)}, u32[]{:S(2)}) copy-start(f32[8,2048]{1,0:T(8,128)} %get-tuple-element.73.hat) | copy-start | bytes 196612
  61.7 17.7 %all-to-all-start.2 = ((bf16[16,24,512]{2,1,0:T(8,128)(2,1)}), bf16[16,24,512]{2,1,0:T(8,128)(2,1)S(1)}, u32[]{:S(2)}, u32[]{:S(2)}) async-start(bf16[16,24,512]{2,1,0:T(8,128)(2,1)} %local_potential.1), calls=%async_computation.2 | async-start | bytes 786432 | tf_op jit(solution)/shard_map/all_to_all | solution.py:606
  79.4 1.8 %collective-permute-start.5 = (bf16[384,512]{1,0:T(8,128)(2,1)S(1)}, bf16[384,512]{1,0:T(8,128)(2,1)S(1)}, u32[]{:S(2)}, u32[]{:S(2)}) collective-permute-start(bf16[384,512]{1,0:T(8,128)(2,1)S(1)} %bitcast.7), channel_id=1, source_target_pairs={{0,8},{8,0},{1,9},{9,1},{2,10},{10,2},{3,11},{11,3},{4,12},{12,4},... | collective-permute-start | bytes 1179656 | tf_op jit(solution)/shard_map/ppermute | solution.py:555
